TPU v7x, 32 devices: a whole 2x2x4 slice. The times are simulated.
32 devices in a mesh: head: 2 (over x), blk: 16 (over z, y, core).
Axes of the slice: x: 2, y: 2, z: 4, core: 2. Of those that a mesh axis runs over, the one named last changes fastest.
Arguments:
- query_act: bfloat16 [4096, 5120], P(('blk', 'head')), may hold values from -6 to 6
- key_act: bfloat16 [4096, 1024], P(('blk', 'head')), may hold values from -6 to 6
- value_act: bfloat16 [4096, 1024], P(('blk', 'head')), may hold values from -6 to 6
- attn_out: bfloat16 [4096, 5120], P(('blk', 'head')), may hold values from -4 to 4
- grad_out: bfloat16 [4096, 5120], P(('blk', 'head')), may hold values from -6 to 6
- log_sum: float32 [4096, 40], P(('blk', 'head')), may hold values from 5 to 6.5
- kv_lists: int32 [32, 32], P('blk'), may hold values from -1 to 31, as said below
Outputs:
- grad_query: bfloat16 [4096, 5120], P(('blk', 'head'))
- grad_key: bfloat16 [4096, 1024], P(('blk', 'head'))
- grad_value: bfloat16 [4096, 1024], P(('blk', 'head'))
Inputs may be any that keep to these rules, and one draw needn't show every extreme that they name: `kv_lists`: the pack is made of prompt trees: the first holds 16 blocks, the last 16, and those between 32 blocks each, in order. A tree is a prompt, then branches. Row r names in rising order the blocks whose keys block r sees (the tree's prompt blocks up to r, and the earlier blocks of r's branch), then -1 to the end. Every entry lies in the same tree as r and is at most r; r itself is always named.
All inputs are finite; a program needn't handle non-finite values.
Results may differ from a plain program's by a relative error of at most 0.0049.
Values may be sent and summed in bfloat16 or wider, within the bound.
No kernel may reach another device: no remote copies, remote signals or barrier semaphores. Data moves between devices by JAX's collectives and lax.ppermute only.
A program may use at most 64 MiB of HBM per device.

v0:
```python
import jax
import jax.numpy as jnp
from jax import lax
from jax.sharding import PartitionSpec as P

QH = 40
KVH = 8
HD = 128
BLOCK = 128


def passed_along(array, axis, by):
    size = lax.axis_size(axis)
    pairs = [(i, i + by) for i in range(size) if 0 <= i + by < size]
    return lax.ppermute(array, axis, pairs)


def shifted(array, axis, by):
    size = lax.axis_size(axis)
    return lax.ppermute(array, axis, [(i, (i + by) % size) for i in range(size)])


def head_delta(grad_rows, out_rows, heads):
    count = grad_rows.shape[0]
    return jnp.einsum(
        "thd,thd->th",
        grad_rows.reshape(count, heads, HD),
        out_rows.reshape(count, heads, HD),
        preferred_element_type=jnp.float32,
    )


def local(query_act, key_act, value_act, attn_out, grad_out, log_sum, kv_lists):
    head_count = lax.axis_size("head")
    blk_count = lax.axis_size("blk")
    sent_delta = head_delta(grad_out, attn_out, QH)
    query_rows, key_rows, value_rows, grad_rows, total_rows, delta_rows = (
        lax.all_to_all(
            query_act.astype(jnp.float32), "head", split_axis=1, concat_axis=0, tiled=True
        ).astype(query_act.dtype),
        lax.all_to_all(
            key_act.astype(jnp.float32), "head", split_axis=1, concat_axis=0, tiled=True
        ).astype(key_act.dtype),
        lax.all_to_all(
            value_act.astype(jnp.float32), "head", split_axis=1, concat_axis=0, tiled=True
        ).astype(value_act.dtype),
        lax.all_to_all(
            grad_out.astype(jnp.float32), "head", split_axis=1, concat_axis=0, tiled=True
        ).astype(grad_out.dtype),
        lax.all_to_all(log_sum, "head", split_axis=1, concat_axis=0, tiled=True),
        lax.all_to_all(sent_delta, "head", split_axis=1, concat_axis=0, tiled=True),
    )
    tokens = query_rows.shape[0]
    local_heads = KVH // head_count
    group_size = QH // KVH
    blocks_dev = tokens // BLOCK
    scaling = HD ** (-0.5)
    queries = query_rows.reshape(tokens, local_heads, group_size, HD)
    out_grads = grad_rows.reshape(tokens, local_heads, group_size, HD)
    row_totals = total_rows.reshape(tokens, local_heads, group_size).transpose(1, 2, 0)[
        :, :, :, None
    ]
    row_deltas = delta_rows.reshape(tokens, local_heads, group_size).transpose(1, 2, 0)[
        :, :, :, None
    ]
    position = lax.axis_index("blk")
    query_pos = position * tokens + jnp.arange(tokens, dtype=jnp.int32)

    def block_mask(rotation):
        source = (position - rotation) % blk_count
        key_ids = source * blocks_dev + jnp.arange(blocks_dev, dtype=jnp.int32)
        listed = jnp.any(kv_lists[:, :, None] == key_ids[None, None, :], axis=1)
        key_pos = source * tokens + jnp.arange(tokens, dtype=jnp.int32)
        return (listed, key_pos)

    def attend(kv_pair, key_sums, query_grad, listed, key_pos):
        visible = jnp.repeat(jnp.repeat(listed, BLOCK, axis=0), BLOCK, axis=1) & (
            key_pos[None, :] <= query_pos[:, None]
        )
        key_block = kv_pair[0].reshape(tokens, local_heads, HD)
        value_block = kv_pair[1].reshape(tokens, local_heads, HD)
        scores = (
            jnp.einsum("tkgd,skd->kgts", queries, key_block, preferred_element_type=jnp.float32)
            * scaling
        )
        weights = jnp.where(visible, jnp.exp(scores - row_totals), 0.0)
        grad_probs = jnp.einsum(
            "tkgd,skd->kgts", out_grads, value_block, preferred_element_type=jnp.float32
        )
        grad_scores = (weights * (grad_probs - row_deltas)).astype(jnp.bfloat16)
        probs_low = weights.astype(jnp.bfloat16)
        value_part = jnp.einsum(
            "kgts,tkgd->skd", probs_low, out_grads, preferred_element_type=jnp.float32
        )
        key_part = (
            jnp.einsum("kgts,tkgd->skd", grad_scores, queries, preferred_element_type=jnp.float32)
            * scaling
        )
        query_part = (
            jnp.einsum("kgts,skd->tkgd", grad_scores, key_block, preferred_element_type=jnp.float32)
            * scaling
        )
        added = jnp.stack(
            [
                key_part.reshape(tokens, local_heads * HD),
                value_part.reshape(tokens, local_heads * HD),
            ]
        )
        return (key_sums + added, query_grad + query_part)

    def visit(rotation, kv_pair, key_sums, query_grad):
        listed, key_pos = block_mask(rotation)
        return attend(kv_pair, key_sums, query_grad, listed, key_pos)

    kv_pair = jnp.stack([key_rows, value_rows])
    empty_sums = jnp.zeros((2, tokens, local_heads * HD), jnp.float32)
    empty_grad = jnp.zeros((tokens, local_heads, group_size, HD), jnp.float32)

    def advance(rotation, carried):
        kv_here, key_sums, query_grad = carried
        arrived = passed_along(kv_here, "blk", 1)
        key_sums, query_grad = visit(rotation, kv_here, key_sums, query_grad)
        key_sums = shifted(key_sums, "blk", 1)
        return (arrived, key_sums, query_grad)

    kv_here, key_sums, query_grad = lax.fori_loop(
        0, blk_count - 1, advance, (kv_pair, empty_sums, empty_grad)
    )
    key_sums, query_grad = visit(blk_count - 1, kv_here, key_sums, query_grad)
    key_sums = shifted(key_sums.astype(jnp.bfloat16), "blk", 1 - blk_count).astype(key_sums.dtype)
    query_low = query_grad.reshape(tokens, local_heads * group_size * HD).astype(jnp.bfloat16)
    key_low = key_sums[0].astype(jnp.bfloat16)
    value_low = key_sums[1].astype(jnp.bfloat16)
    grad_query, grad_key, grad_value = (
        lax.all_to_all(query_low, "head", split_axis=0, concat_axis=1, tiled=True),
        lax.all_to_all(key_low, "head", split_axis=0, concat_axis=1, tiled=True),
        lax.all_to_all(value_low, "head", split_axis=0, concat_axis=1, tiled=True),
    )
    return (grad_query, grad_key, grad_value)


def solution(mesh):
    return jax.shard_map(
        local,
        mesh=mesh,
        in_specs=(
            P(("blk", "head"), None),
            P(("blk", "head"), None),
            P(("blk", "head"), None),
            P(("blk", "head"), None),
            P(("blk", "head"), None),
            P(("blk", "head"), None),
            P("blk", None),
        ),
        out_specs=(P(("blk", "head"), None), P(("blk", "head"), None), P(("blk", "head"), None)),
        check_vma=False,
    )
```

profile of v0, /device:TPU:8, one launch (start us, length us, event | category | flops | bytes accessed | tf_op | source)
XLA Modules:
  0.0 588.1 jit_solution(13870720464254667845)
XLA Ops:
  9.2 3.2 all-to-all-start.5
  16.4 3.4 all-to-all-start.1
  20.7 4.3 all-to-all-done.1
  25.0 3.4 all-to-all-start
  29.9 3.7 all-to-all-done
  33.6 3.6 all-to-all-start.2
  38.7 11.2 %all-to-all-done.2 = bf16[128,2,2560]{0,2,1:T(8,128)(2,1)S(1)} async-done(((bf16[128,2,2560]{0,2,1:T(8,128)(2,1)}), bf16[128,2,2560]{0,2,1:T(8,128)(2,1)S(1)}, u32[]{:S(2)}, u32[]{:S(2)}) %all-to-all-start.2) | async-done | bytes 1310752 | tf_op jit(solution)/shard_map/all_to_all | solution.py:38
  49.9 4.7 all-to-all-start.4
  56.6 11.6 %copy.132 = bf16[2,128,2560]{1,0,2:T(2,128)(2,1)} copy(bf16[2,128,2560]{1,2,0:T(8,128)(2,1)S(1)} %bitcast.237) | data formatting | bytes 2621440 | tf_op jit(solution)/shard_map/convert_element_type | solution.py:40
  68.2 3.4 convert_element_type.111
  71.6 9.9 %copy.135 = bf16[2,128,2560]{1,0,2:T(2,128)(2,1)S(1)} copy(bf16[2,128,2560]{1,2,0:T(8,128)(2,1)} %bitcast.163) | data formatting | bytes 2621440 | tf_op jit(solution)/shard_map/convert_element_type | solution.py:49
  83.3 451.7 %while.20 = (s32[]{:T(128)}, bf16[2,256,512]{1,2,0:T(8,128)(2,1)}, f32[2,256,512]{1,2,0:T(8,128)S(1)}, f32[256,4,5,128]{3,0,2,1:T(8,128)}, s32[2,32]{1,0:T(2,128...) while((s32[]{:T(128)}, bf16[2,256,512]{1,2,0:T(8,128)(2,1)}, ...), condition=%wide.region_2.3_spmd.clone, body=%wide.region_0.2_spmd.clone.sunk | while | flops 1693582080 | bytes 63441640 | solution.py:126
  92.5 3.5 collective-permute-start
  96.1 4.4 bitcast_add_fusion.3
  100.5 13.1 %collective-permute-done = bf16[2,256,512]{1,2,0:T(8,128)(2,1)} collective-permute-done((bf16[2,256,512]{1,2,0:T(8,128)(2,1)S(1)}, bf16[2,256,512]{1,2,0:T(8,128)(2,1)}, u32[]{:S(2)}, u32[]{:S(2)}) %collective-permute-start) | collective-permute-done | bytes 524320 | tf_op jit(solution)/shard_map/while/body/eval_jaxpr/ppermute | solution.py:15
  125.3 5.2 bitcast_add_fusion.3
  130.4 13.2 %collective-permute-done = bf16[2,256,512]{1,2,0:T(8,128)(2,1)} collective-permute-done((bf16[2,256,512]{1,2,0:T(8,128)(2,1)S(1)}, bf16[2,256,512]{1,2,0:T(8,128)(2,1)}, u32[]{:S(2)}, u32[]{:S(2)}) %collective-permute-start) | collective-permute-done | bytes 524320 | tf_op jit(solution)/shard_map/while/body/eval_jaxpr/ppermute | solution.py:15
  154.7 5.2 bitcast_add_fusion.3
  159.8 14.0 %collective-permute-done = bf16[2,256,512]{1,2,0:T(8,128)(2,1)} collective-permute-done((bf16[2,256,512]{1,2,0:T(8,128)(2,1)S(1)}, bf16[2,256,512]{1,2,0:T(8,128)(2,1)}, u32[]{:S(2)}, u32[]{:S(2)}) %collective-permute-start) | collective-permute-done | bytes 524320 | tf_op jit(solution)/shard_map/while/body/eval_jaxpr/ppermute | solution.py:15
  184.8 5.2 bitcast_add_fusion.3
  189.9 14.0 %collective-permute-done = bf16[2,256,512]{1,2,0:T(8,128)(2,1)} collective-permute-done((bf16[2,256,512]{1,2,0:T(8,128)(2,1)S(1)}, bf16[2,256,512]{1,2,0:T(8,128)(2,1)}, u32[]{:S(2)}, u32[]{:S(2)}) %collective-permute-start) | collective-permute-done | bytes 524320 | tf_op jit(solution)/shard_map/while/body/eval_jaxpr/ppermute | solution.py:15
  214.9 5.2 bitcast_add_fusion.3
  220.0 14.0 %collective-permute-done = bf16[2,256,512]{1,2,0:T(8,128)(2,1)} collective-permute-done((bf16[2,256,512]{1,2,0:T(8,128)(2,1)S(1)}, bf16[2,256,512]{1,2,0:T(8,128)(2,1)}, u32[]{:S(2)}, u32[]{:S(2)}) %collective-permute-start) | collective-permute-done | bytes 524320 | tf_op jit(solution)/shard_map/while/body/eval_jaxpr/ppermute | solution.py:15
  245.0 5.2 bitcast_add_fusion.3
  250.1 14.0 %collective-permute-done = bf16[2,256,512]{1,2,0:T(8,128)(2,1)} collective-permute-done((bf16[2,256,512]{1,2,0:T(8,128)(2,1)S(1)}, bf16[2,256,512]{1,2,0:T(8,128)(2,1)}, u32[]{:S(2)}, u32[]{:S(2)}) %collective-permute-start) | collective-permute-done | bytes 524320 | tf_op jit(solution)/shard_map/while/body/eval_jaxpr/ppermute | solution.py:15
  275.0 5.2 bitcast_add_fusion.3
  280.2 14.0 %collective-permute-done = bf16[2,256,512]{1,2,0:T(8,128)(2,1)} collective-permute-done((bf16[2,256,512]{1,2,0:T(8,128)(2,1)S(1)}, bf16[2,256,512]{1,2,0:T(8,128)(2,1)}, u32[]{:S(2)}, u32[]{:S(2)}) %collective-permute-start) | collective-permute-done | bytes 524320 | tf_op jit(solution)/shard_map/while/body/eval_jaxpr/ppermute | solution.py:15
  305.1 5.2 bitcast_add_fusion.3
  310.3 14.0 %collective-permute-done = bf16[2,256,512]{1,2,0:T(8,128)(2,1)} collective-permute-done((bf16[2,256,512]{1,2,0:T(8,128)(2,1)S(1)}, bf16[2,256,512]{1,2,0:T(8,128)(2,1)}, u32[]{:S(2)}, u32[]{:S(2)}) %collective-permute-start) | collective-permute-done | bytes 524320 | tf_op jit(solution)/shard_map/while/body/eval_jaxpr/ppermute | solution.py:15
  335.2 5.2 bitcast_add_fusion.3
  340.4 14.0 %collective-permute-done = bf16[2,256,512]{1,2,0:T(8,128)(2,1)} collective-permute-done((bf16[2,256,512]{1,2,0:T(8,128)(2,1)S(1)}, bf16[2,256,512]{1,2,0:T(8,128)(2,1)}, u32[]{:S(2)}, u32[]{:S(2)}) %collective-permute-start) | collective-permute-done | bytes 524320 | tf_op jit(solution)/shard_map/while/body/eval_jaxpr/ppermute | solution.py:15
  365.3 5.2 bitcast_add_fusion.3
  370.5 14.0 %collective-permute-done = bf16[2,256,512]{1,2,0:T(8,128)(2,1)} collective-permute-done((bf16[2,256,512]{1,2,0:T(8,128)(2,1)S(1)}, bf16[2,256,512]{1,2,0:T(8,128)(2,1)}, u32[]{:S(2)}, u32[]{:S(2)}) %collective-permute-start) | collective-permute-done | bytes 524320 | tf_op jit(solution)/shard_map/while/body/eval_jaxpr/ppermute | solution.py:15
  395.4 5.2 bitcast_add_fusion.3
  400.6 14.0 %collective-permute-done = bf16[2,256,512]{1,2,0:T(8,128)(2,1)} collective-permute-done((bf16[2,256,512]{1,2,0:T(8,128)(2,1)S(1)}, bf16[2,256,512]{1,2,0:T(8,128)(2,1)}, u32[]{:S(2)}, u32[]{:S(2)}) %collective-permute-start) | collective-permute-done | bytes 524320 | tf_op jit(solution)/shard_map/while/body/eval_jaxpr/ppermute | solution.py:15
  425.5 5.2 bitcast_add_fusion.3
  430.7 14.0 %collective-permute-done = bf16[2,256,512]{1,2,0:T(8,128)(2,1)} collective-permute-done((bf16[2,256,512]{1,2,0:T(8,128)(2,1)S(1)}, bf16[2,256,512]{1,2,0:T(8,128)(2,1)}, u32[]{:S(2)}, u32[]{:S(2)}) %collective-permute-start) | collective-permute-done | bytes 524320 | tf_op jit(solution)/shard_map/while/body/eval_jaxpr/ppermute | solution.py:15
  455.6 5.2 bitcast_add_fusion.3
  460.8 14.0 %collective-permute-done = bf16[2,256,512]{1,2,0:T(8,128)(2,1)} collective-permute-done((bf16[2,256,512]{1,2,0:T(8,128)(2,1)S(1)}, bf16[2,256,512]{1,2,0:T(8,128)(2,1)}, u32[]{:S(2)}, u32[]{:S(2)}) %collective-permute-start) | collective-permute-done | bytes 524320 | tf_op jit(solution)/shard_map/while/body/eval_jaxpr/ppermute | solution.py:15
  485.7 5.2 bitcast_add_fusion.3
  490.9 14.0 %collective-permute-done = bf16[2,256,512]{1,2,0:T(8,128)(2,1)} collective-permute-done((bf16[2,256,512]{1,2,0:T(8,128)(2,1)S(1)}, bf16[2,256,512]{1,2,0:T(8,128)(2,1)}, u32[]{:S(2)}, u32[]{:S(2)}) %collective-permute-start) | collective-permute-done | bytes 524320 | tf_op jit(solution)/shard_map/while/body/eval_jaxpr/ppermute | solution.py:15
  515.8 5.2 bitcast_add_fusion.3
  521.0 14.0 %collective-permute-done = bf16[2,256,512]{1,2,0:T(8,128)(2,1)} collective-permute-done((bf16[2,256,512]{1,2,0:T(8,128)(2,1)S(1)}, bf16[2,256,512]{1,2,0:T(8,128)(2,1)}, u32[]{:S(2)}, u32[]{:S(2)}) %collective-permute-start) | collective-permute-done | bytes 524320 | tf_op jit(solution)/shard_map/while/body/eval_jaxpr/ppermute | solution.py:15
  542.8 9.5 %collective-permute-done.2 = bf16[2,256,512]{1,2,0:T(8,128)(2,1)S(1)} collective-permute-done((bf16[2,256,512]{1,2,0:T(8,128)(2,1)S(1)}, bf16[2,256,512]{1,2,0:T(8,128)(2,1)S(1)}, u32[]{:S(2)}, u32[]{:S(2)}) %collective-permute-start.2) | collective-permute-done | bytes 524320 | tf_op jit(solution)/shard_map/ppermute | solution.py:20
  553.2 3.4 all-to-all-start.7
  562.2 3.4 all-to-all-start.8
  572.3 3.6 all-to-all-start.6
  578.0 8.7 %all-to-all-done.6 = bf16[2,128,2560]{1,2,0:T(8,128)(2,1)S(1)} async-done(((bf16[2,128,2560]{1,2,0:T(8,128)(2,1)}), bf16[2,128,2560]{1,2,0:T(8,128)(2,1)S(1)}, u32[]{:S(2)}, u32[]{:S(2)}) %all-to-all-start.6) | async-done | bytes 1310752 | tf_op jit(solution)/shard_map/all_to_all | solution.py:135
  (404 shorter events, 205.9 us)
Async XLA Ops:
  0.6 6.3 %copy-start.6 = (bf16[128,5120]{1,0:T(8,128)(2,1)S(1)}, bf16[128,5120]{1,0:T(8,128)(2,1)}, u32[]{:S(2)}) copy-start(bf16[128,5120]{1,0:T(8,128)(2,1)} %param.12) | copy-start | bytes 3932164
  2.1 7.1 %all-to-all-start.3 = ((f32[128,2,20]{0,2,1:T(8,128)}), f32[128,2,20]{0,2,1:T(8,128)S(1)}, u32[]{:S(2)}, u32[]{:S(2)}) async-start(f32[128,2,20]{0,2,1:T(8,128)} %all_to_all.117), calls=%async_computation.3 | async-start | bytes 49152 | tf_op jit(solution)/shard_map/all_to_all | solution.py:50
  6.9 5.6 copy-start.10
  6.9 12.9 %copy-start.11 = (bf16[128,1024]{1,0:T(8,128)(2,1)S(1)}, bf16[128,1024]{1,0:T(8,128)(2,1)}, u32[]{:S(2)}) copy-start(bf16[128,1024]{1,0:T(8,128)(2,1)} %param.10) | copy-start | bytes 786436
  7.2 21.2 %copy-start.7 = (bf16[128,5120]{1,0:T(8,128)(2,1)S(1)}, bf16[128,5120]{1,0:T(8,128)(2,1)}, u32[]{:S(2)}) copy-start(bf16[128,5120]{1,0:T(8,128)(2,1)} %param.9) | copy-start | bytes 3932164
  9.2 7.1 %all-to-all-start.5 = ((f32[128,2,20]{0,2,1:T(8,128)}), f32[128,2,20]{0,2,1:T(8,128)S(1)}, u32[]{:S(2)}, u32[]{:S(2)}) async-start(f32[128,2,20]{0,2,1:T(8,128)} %all_to_all.123), calls=%async_computation.5 | async-start | bytes 49152 | tf_op jit(solution)/shard_map/all_to_all | solution.py:51
  16.4 8.6 %all-to-all-start.1 = ((bf16[128,2,512]{0,2,1:T(8,128)(2,1)}), bf16[128,2,512]{0,2,1:T(8,128)(2,1)S(1)}, u32[]{:S(2)}, u32[]{:S(2)}) async-start(bf16[128,2,512]{0,2,1:T(8,128)(2,1)} %bitcast.3), calls=%async_computation.1 | async-start | bytes 524288 | tf_op jit(solution)/shard_map/all_to_all | solution.py:44
  25.0 8.6 %all-to-all-start = ((bf16[128,2,512]{0,2,1:T(8,128)(2,1)}), bf16[128,2,512]{0,2,1:T(8,128)(2,1)S(1)}, u32[]{:S(2)}, u32[]{:S(2)}) async-start(bf16[128,2,512]{0,2,1:T(8,128)(2,1)} %bitcast), calls=%async_computation | async-start | bytes 524288 | tf_op jit(solution)/shard_map/all_to_all | solution.py:41
  28.4 8.8 %copy-start.5 = (bf16[128,5120]{1,0:T(8,128)(2,1)S(1)}, bf16[128,5120]{1,0:T(8,128)(2,1)}, u32[]{:S(2)}) copy-start(bf16[128,5120]{1,0:T(8,128)(2,1)} %param.13) | copy-start | bytes 3932164
  33.6 16.3 %all-to-all-start.2 = ((bf16[128,2,2560]{0,2,1:T(8,128)(2,1)}), bf16[128,2,2560]{0,2,1:T(8,128)(2,1)S(1)}, u32[]{:S(2)}, u32[]{:S(2)}) async-start(bf16[128,2,2560]{0,2,1:T(8,128)(2,1)} %bitcast.239), calls=%async_computation.2 | async-start | bytes 2621440 | tf_op jit(solution)/shard_map/all_to_all | solution.py:38
  37.2 17.4 %copy-start.12 = (s32[2,32]{1,0:T(2,128)S(1)}, s32[2,32]{1,0:T(2,128)}, u32[]{:S(2)}) copy-start(s32[2,32]{1,0:T(2,128)} %param.15) | copy-start | bytes 772
  49.9 21.7 %all-to-all-start.4 = ((bf16[128,2,2560]{0,2,1:T(8,128)(2,1)}), bf16[128,2,2560]{0,2,1:T(8,128)(2,1)}, u32[]{:S(2)}, u32[]{:S(2)}) async-start(bf16[128,2,2560]{0,2,1:T(8,128)(2,1)} %bitcast.238), calls=%async_computation.4 | async-start | bytes 2621440 | tf_op jit(solution)/shard_map/all_to_all | solution.py:47
  92.5 21.1 %collective-permute-start.1 = (f32[2,256,512]{1,2,0:T(8,128)}, f32[2,256,512]{1,2,0:T(8,128)S(1)}, u32[]{:S(2)}, u32[]{:S(2)}) collective-permute-start(f32[2,256,512]{1,2,0:T(8,128)} %maximum_add_fusion.3), channel_id=1, source_target_pairs={{0,1},{1,2},{2,3},{3,4},{4,5},{5,6},{6,7},{7,8},{8,9},{9,10},{10,1... | collective-permute-start | bytes 3145736 | tf_op jit(solution)/shard_map/while/body/eval_jaxpr/ppermute | solution.py:20
  92.5 21.1 %collective-permute-start = (bf16[2,256,512]{1,2,0:T(8,128)(2,1)S(1)}, bf16[2,256,512]{1,2,0:T(8,128)(2,1)}, u32[]{:S(2)}, u32[]{:S(2)}) collective-permute-start(bf16[2,256,512]{1,2,0:T(8,128)(2,1)S(1)} %copy.208), channel_id=1, source_target_pairs={{0,1},{1,2},{2,3},{3,4},{4,5},{5,6},{6,7},{7,8},{8,9},{9,10},{10,1... | collective-permute-start | bytes 1572872 | tf_op jit(solution)/shard_map/while/body/eval_jaxpr/ppermute | solution.py:15
  122.6 21.1 %collective-permute-start.1 = (f32[2,256,512]{1,2,0:T(8,128)}, f32[2,256,512]{1,2,0:T(8,128)S(1)}, u32[]{:S(2)}, u32[]{:S(2)}) collective-permute-start(f32[2,256,512]{1,2,0:T(8,128)} %maximum_add_fusion.3), channel_id=1, source_target_pairs={{0,1},{1,2},{2,3},{3,4},{4,5},{5,6},{6,7},{7,8},{8,9},{9,10},{10,1... | collective-permute-start | bytes 3145736 | tf_op jit(solution)/shard_map/while/body/eval_jaxpr/ppermute | solution.py:20
  122.6 21.1 %collective-permute-start = (bf16[2,256,512]{1,2,0:T(8,128)(2,1)S(1)}, bf16[2,256,512]{1,2,0:T(8,128)(2,1)}, u32[]{:S(2)}, u32[]{:S(2)}) collective-permute-start(bf16[2,256,512]{1,2,0:T(8,128)(2,1)S(1)} %copy.208), channel_id=1, source_target_pairs={{0,1},{1,2},{2,3},{3,4},{4,5},{5,6},{6,7},{7,8},{8,9},{9,10},{10,1... | collective-permute-start | bytes 1572872 | tf_op jit(solution)/shard_map/while/body/eval_jaxpr/ppermute | solution.py:15
  152.7 21.1 %collective-permute-start.1 = (f32[2,256,512]{1,2,0:T(8,128)}, f32[2,256,512]{1,2,0:T(8,128)S(1)}, u32[]{:S(2)}, u32[]{:S(2)}) collective-permute-start(f32[2,256,512]{1,2,0:T(8,128)} %maximum_add_fusion.3), channel_id=1, source_target_pairs={{0,1},{1,2},{2,3},{3,4},{4,5},{5,6},{6,7},{7,8},{8,9},{9,10},{10,1... | collective-permute-start | bytes 3145736 | tf_op jit(solution)/shard_map/while/body/eval_jaxpr/ppermute | solution.py:20
  152.7 21.1 %collective-permute-start = (bf16[2,256,512]{1,2,0:T(8,128)(2,1)S(1)}, bf16[2,256,512]{1,2,0:T(8,128)(2,1)}, u32[]{:S(2)}, u32[]{:S(2)}) collective-permute-start(bf16[2,256,512]{1,2,0:T(8,128)(2,1)S(1)} %copy.208), channel_id=1, source_target_pairs={{0,1},{1,2},{2,3},{3,4},{4,5},{5,6},{6,7},{7,8},{8,9},{9,10},{10,1... | collective-permute-start | bytes 1572872 | tf_op jit(solution)/shard_map/while/body/eval_jaxpr/ppermute | solution.py:15
  182.8 21.1 %collective-permute-start.1 = (f32[2,256,512]{1,2,0:T(8,128)}, f32[2,256,512]{1,2,0:T(8,128)S(1)}, u32[]{:S(2)}, u32[]{:S(2)}) collective-permute-start(f32[2,256,512]{1,2,0:T(8,128)} %maximum_add_fusion.3), channel_id=1, source_target_pairs={{0,1},{1,2},{2,3},{3,4},{4,5},{5,6},{6,7},{7,8},{8,9},{9,10},{10,1... | collective-permute-start | bytes 3145736 | tf_op jit(solution)/shard_map/while/body/eval_jaxpr/ppermute | solution.py:20
  182.8 21.1 %collective-permute-start = (bf16[2,256,512]{1,2,0:T(8,128)(2,1)S(1)}, bf16[2,256,512]{1,2,0:T(8,128)(2,1)}, u32[]{:S(2)}, u32[]{:S(2)}) collective-permute-start(bf16[2,256,512]{1,2,0:T(8,128)(2,1)S(1)} %copy.208), channel_id=1, source_target_pairs={{0,1},{1,2},{2,3},{3,4},{4,5},{5,6},{6,7},{7,8},{8,9},{9,10},{10,1... | collective-permute-start | bytes 1572872 | tf_op jit(solution)/shard_map/while/body/eval_jaxpr/ppermute | solution.py:15
  212.9 21.1 %collective-permute-start.1 = (f32[2,256,512]{1,2,0:T(8,128)}, f32[2,256,512]{1,2,0:T(8,128)S(1)}, u32[]{:S(2)}, u32[]{:S(2)}) collective-permute-start(f32[2,256,512]{1,2,0:T(8,128)} %maximum_add_fusion.3), channel_id=1, source_target_pairs={{0,1},{1,2},{2,3},{3,4},{4,5},{5,6},{6,7},{7,8},{8,9},{9,10},{10,1... | collective-permute-start | bytes 3145736 | tf_op jit(solution)/shard_map/while/body/eval_jaxpr/ppermute | solution.py:20
  212.9 21.1 %collective-permute-start = (bf16[2,256,512]{1,2,0:T(8,128)(2,1)S(1)}, bf16[2,256,512]{1,2,0:T(8,128)(2,1)}, u32[]{:S(2)}, u32[]{:S(2)}) collective-permute-start(bf16[2,256,512]{1,2,0:T(8,128)(2,1)S(1)} %copy.208), channel_id=1, source_target_pairs={{0,1},{1,2},{2,3},{3,4},{4,5},{5,6},{6,7},{7,8},{8,9},{9,10},{10,1... | collective-permute-start | bytes 1572872 | tf_op jit(solution)/shard_map/while/body/eval_jaxpr/ppermute | solution.py:15
  243.0 21.1 %collective-permute-start.1 = (f32[2,256,512]{1,2,0:T(8,128)}, f32[2,256,512]{1,2,0:T(8,128)S(1)}, u32[]{:S(2)}, u32[]{:S(2)}) collective-permute-start(f32[2,256,512]{1,2,0:T(8,128)} %maximum_add_fusion.3), channel_id=1, source_target_pairs={{0,1},{1,2},{2,3},{3,4},{4,5},{5,6},{6,7},{7,8},{8,9},{9,10},{10,1... | collective-permute-start | bytes 3145736 | tf_op jit(solution)/shard_map/while/body/eval_jaxpr/ppermute | solution.py:20
  243.0 21.1 %collective-permute-start = (bf16[2,256,512]{1,2,0:T(8,128)(2,1)S(1)}, bf16[2,256,512]{1,2,0:T(8,128)(2,1)}, u32[]{:S(2)}, u32[]{:S(2)}) collective-permute-start(bf16[2,256,512]{1,2,0:T(8,128)(2,1)S(1)} %copy.208), channel_id=1, source_target_pairs={{0,1},{1,2},{2,3},{3,4},{4,5},{5,6},{6,7},{7,8},{8,9},{9,10},{10,1... | collective-permute-start | bytes 1572872 | tf_op jit(solution)/shard_map/while/body/eval_jaxpr/ppermute | solution.py:15
  273.1 21.1 %collective-permute-start.1 = (f32[2,256,512]{1,2,0:T(8,128)}, f32[2,256,512]{1,2,0:T(8,128)S(1)}, u32[]{:S(2)}, u32[]{:S(2)}) collective-permute-start(f32[2,256,512]{1,2,0:T(8,128)} %maximum_add_fusion.3), channel_id=1, source_target_pairs={{0,1},{1,2},{2,3},{3,4},{4,5},{5,6},{6,7},{7,8},{8,9},{9,10},{10,1... | collective-permute-start | bytes 3145736 | tf_op jit(solution)/shard_map/while/body/eval_jaxpr/ppermute | solution.py:20
  273.1 21.1 %collective-permute-start = (bf16[2,256,512]{1,2,0:T(8,128)(2,1)S(1)}, bf16[2,256,512]{1,2,0:T(8,128)(2,1)}, u32[]{:S(2)}, u32[]{:S(2)}) collective-permute-start(bf16[2,256,512]{1,2,0:T(8,128)(2,1)S(1)} %copy.208), channel_id=1, source_target_pairs={{0,1},{1,2},{2,3},{3,4},{4,5},{5,6},{6,7},{7,8},{8,9},{9,10},{10,1... | collective-permute-start | bytes 1572872 | tf_op jit(solution)/shard_map/while/body/eval_jaxpr/ppermute | solution.py:15
  303.2 21.1 %collective-permute-start.1 = (f32[2,256,512]{1,2,0:T(8,128)}, f32[2,256,512]{1,2,0:T(8,128)S(1)}, u32[]{:S(2)}, u32[]{:S(2)}) collective-permute-start(f32[2,256,512]{1,2,0:T(8,128)} %maximum_add_fusion.3), channel_id=1, source_target_pairs={{0,1},{1,2},{2,3},{3,4},{4,5},{5,6},{6,7},{7,8},{8,9},{9,10},{10,1... | collective-permute-start | bytes 3145736 | tf_op jit(solution)/shard_map/while/body/eval_jaxpr/ppermute | solution.py:20
  303.2 21.1 %collective-permute-start = (bf16[2,256,512]{1,2,0:T(8,128)(2,1)S(1)}, bf16[2,256,512]{1,2,0:T(8,128)(2,1)}, u32[]{:S(2)}, u32[]{:S(2)}) collective-permute-start(bf16[2,256,512]{1,2,0:T(8,128)(2,1)S(1)} %copy.208), channel_id=1, source_target_pairs={{0,1},{1,2},{2,3},{3,4},{4,5},{5,6},{6,7},{7,8},{8,9},{9,10},{10,1... | collective-permute-start | bytes 1572872 | tf_op jit(solution)/shard_map/while/body/eval_jaxpr/ppermute | solution.py:15
  333.3 21.1 %collective-permute-start.1 = (f32[2,256,512]{1,2,0:T(8,128)}, f32[2,256,512]{1,2,0:T(8,128)S(1)}, u32[]{:S(2)}, u32[]{:S(2)}) collective-permute-start(f32[2,256,512]{1,2,0:T(8,128)} %maximum_add_fusion.3), channel_id=1, source_target_pairs={{0,1},{1,2},{2,3},{3,4},{4,5},{5,6},{6,7},{7,8},{8,9},{9,10},{10,1... | collective-permute-start | bytes 3145736 | tf_op jit(solution)/shard_map/while/body/eval_jaxpr/ppermute | solution.py:20
  333.3 21.1 %collective-permute-start = (bf16[2,256,512]{1,2,0:T(8,128)(2,1)S(1)}, bf16[2,256,512]{1,2,0:T(8,128)(2,1)}, u32[]{:S(2)}, u32[]{:S(2)}) collective-permute-start(bf16[2,256,512]{1,2,0:T(8,128)(2,1)S(1)} %copy.208), channel_id=1, source_target_pairs={{0,1},{1,2},{2,3},{3,4},{4,5},{5,6},{6,7},{7,8},{8,9},{9,10},{10,1... | collective-permute-start | bytes 1572872 | tf_op jit(solution)/shard_map/while/body/eval_jaxpr/ppermute | solution.py:15
  363.4 21.1 %collective-permute-start.1 = (f32[2,256,512]{1,2,0:T(8,128)}, f32[2,256,512]{1,2,0:T(8,128)S(1)}, u32[]{:S(2)}, u32[]{:S(2)}) collective-permute-start(f32[2,256,512]{1,2,0:T(8,128)} %maximum_add_fusion.3), channel_id=1, source_target_pairs={{0,1},{1,2},{2,3},{3,4},{4,5},{5,6},{6,7},{7,8},{8,9},{9,10},{10,1... | collective-permute-start | bytes 3145736 | tf_op jit(solution)/shard_map/while/body/eval_jaxpr/ppermute | solution.py:20
  363.4 21.1 %collective-permute-start = (bf16[2,256,512]{1,2,0:T(8,128)(2,1)S(1)}, bf16[2,256,512]{1,2,0:T(8,128)(2,1)}, u32[]{:S(2)}, u32[]{:S(2)}) collective-permute-start(bf16[2,256,512]{1,2,0:T(8,128)(2,1)S(1)} %copy.208), channel_id=1, source_target_pairs={{0,1},{1,2},{2,3},{3,4},{4,5},{5,6},{6,7},{7,8},{8,9},{9,10},{10,1... | collective-permute-start | bytes 1572872 | tf_op jit(solution)/shard_map/while/body/eval_jaxpr/ppermute | solution.py:15
  393.5 21.1 %collective-permute-start.1 = (f32[2,256,512]{1,2,0:T(8,128)}, f32[2,256,512]{1,2,0:T(8,128)S(1)}, u32[]{:S(2)}, u32[]{:S(2)}) collective-permute-start(f32[2,256,512]{1,2,0:T(8,128)} %maximum_add_fusion.3), channel_id=1, source_target_pairs={{0,1},{1,2},{2,3},{3,4},{4,5},{5,6},{6,7},{7,8},{8,9},{9,10},{10,1... | collective-permute-start | bytes 3145736 | tf_op jit(solution)/shard_map/while/body/eval_jaxpr/ppermute | solution.py:20
  393.5 21.1 %collective-permute-start = (bf16[2,256,512]{1,2,0:T(8,128)(2,1)S(1)}, bf16[2,256,512]{1,2,0:T(8,128)(2,1)}, u32[]{:S(2)}, u32[]{:S(2)}) collective-permute-start(bf16[2,256,512]{1,2,0:T(8,128)(2,1)S(1)} %copy.208), channel_id=1, source_target_pairs={{0,1},{1,2},{2,3},{3,4},{4,5},{5,6},{6,7},{7,8},{8,9},{9,10},{10,1... | collective-permute-start | bytes 1572872 | tf_op jit(solution)/shard_map/while/body/eval_jaxpr/ppermute | solution.py:15
  423.6 21.1 %collective-permute-start.1 = (f32[2,256,512]{1,2,0:T(8,128)}, f32[2,256,512]{1,2,0:T(8,128)S(1)}, u32[]{:S(2)}, u32[]{:S(2)}) collective-permute-start(f32[2,256,512]{1,2,0:T(8,128)} %maximum_add_fusion.3), channel_id=1, source_target_pairs={{0,1},{1,2},{2,3},{3,4},{4,5},{5,6},{6,7},{7,8},{8,9},{9,10},{10,1... | collective-permute-start | bytes 3145736 | tf_op jit(solution)/shard_map/while/body/eval_jaxpr/ppermute | solution.py:20
  423.6 21.1 %collective-permute-start = (bf16[2,256,512]{1,2,0:T(8,128)(2,1)S(1)}, bf16[2,256,512]{1,2,0:T(8,128)(2,1)}, u32[]{:S(2)}, u32[]{:S(2)}) collective-permute-start(bf16[2,256,512]{1,2,0:T(8,128)(2,1)S(1)} %copy.208), channel_id=1, source_target_pairs={{0,1},{1,2},{2,3},{3,4},{4,5},{5,6},{6,7},{7,8},{8,9},{9,10},{10,1... | collective-permute-start | bytes 1572872 | tf_op jit(solution)/shard_map/while/body/eval_jaxpr/ppermute | solution.py:15
  453.7 21.1 %collective-permute-start.1 = (f32[2,256,512]{1,2,0:T(8,128)}, f32[2,256,512]{1,2,0:T(8,128)S(1)}, u32[]{:S(2)}, u32[]{:S(2)}) collective-permute-start(f32[2,256,512]{1,2,0:T(8,128)} %maximum_add_fusion.3), channel_id=1, source_target_pairs={{0,1},{1,2},{2,3},{3,4},{4,5},{5,6},{6,7},{7,8},{8,9},{9,10},{10,1... | collective-permute-start | bytes 3145736 | tf_op jit(solution)/shard_map/while/body/eval_jaxpr/ppermute | solution.py:20
  453.7 21.1 %collective-permute-start = (bf16[2,256,512]{1,2,0:T(8,128)(2,1)S(1)}, bf16[2,256,512]{1,2,0:T(8,128)(2,1)}, u32[]{:S(2)}, u32[]{:S(2)}) collective-permute-start(bf16[2,256,512]{1,2,0:T(8,128)(2,1)S(1)} %copy.208), channel_id=1, source_target_pairs={{0,1},{1,2},{2,3},{3,4},{4,5},{5,6},{6,7},{7,8},{8,9},{9,10},{10,1... | collective-permute-start | bytes 1572872 | tf_op jit(solution)/shard_map/while/body/eval_jaxpr/ppermute | solution.py:15
  483.8 21.1 %collective-permute-start.1 = (f32[2,256,512]{1,2,0:T(8,128)}, f32[2,256,512]{1,2,0:T(8,128)S(1)}, u32[]{:S(2)}, u32[]{:S(2)}) collective-permute-start(f32[2,256,512]{1,2,0:T(8,128)} %maximum_add_fusion.3), channel_id=1, source_target_pairs={{0,1},{1,2},{2,3},{3,4},{4,5},{5,6},{6,7},{7,8},{8,9},{9,10},{10,1... | collective-permute-start | bytes 3145736 | tf_op jit(solution)/shard_map/while/body/eval_jaxpr/ppermute | solution.py:20
  483.8 21.1 %collective-permute-start = (bf16[2,256,512]{1,2,0:T(8,128)(2,1)S(1)}, bf16[2,256,512]{1,2,0:T(8,128)(2,1)}, u32[]{:S(2)}, u32[]{:S(2)}) collective-permute-start(bf16[2,256,512]{1,2,0:T(8,128)(2,1)S(1)} %copy.208), channel_id=1, source_target_pairs={{0,1},{1,2},{2,3},{3,4},{4,5},{5,6},{6,7},{7,8},{8,9},{9,10},{10,1... | collective-permute-start | bytes 1572872 | tf_op jit(solution)/shard_map/while/body/eval_jaxpr/ppermute | solution.py:15
  513.9 21.1 %collective-permute-start.1 = (f32[2,256,512]{1,2,0:T(8,128)}, f32[2,256,512]{1,2,0:T(8,128)S(1)}, u32[]{:S(2)}, u32[]{:S(2)}) collective-permute-start(f32[2,256,512]{1,2,0:T(8,128)} %maximum_add_fusion.3), channel_id=1, source_target_pairs={{0,1},{1,2},{2,3},{3,4},{4,5},{5,6},{6,7},{7,8},{8,9},{9,10},{10,1... | collective-permute-start | bytes 3145736 | tf_op jit(solution)/shard_map/while/body/eval_jaxpr/ppermute | solution.py:20
  513.9 21.1 %collective-permute-start = (bf16[2,256,512]{1,2,0:T(8,128)(2,1)S(1)}, bf16[2,256,512]{1,2,0:T(8,128)(2,1)}, u32[]{:S(2)}, u32[]{:S(2)}) collective-permute-start(bf16[2,256,512]{1,2,0:T(8,128)(2,1)S(1)} %copy.208), channel_id=1, source_target_pairs={{0,1},{1,2},{2,3},{3,4},{4,5},{5,6},{6,7},{7,8},{8,9},{9,10},{10,1... | collective-permute-start | bytes 1572872 | tf_op jit(solution)/shard_map/while/body/eval_jaxpr/ppermute | solution.py:15
  535.0 2.3 copy-start.2
  541.5 15.1 %copy-start.1 = (f32[256,4,5,128]{3,0,2,1:T(8,128)S(1)}, f32[256,4,5,128]{3,0,2,1:T(8,128)}, u32[]{:S(2)}) copy-start(f32[256,4,5,128]{3,0,2,1:T(8,128)} %get-tuple-element.270) | copy-start | bytes 7864324
  542.7 9.6 %collective-permute-start.2 = (bf16[2,256,512]{1,2,0:T(8,128)(2,1)S(1)}, bf16[2,256,512]{1,2,0:T(8,128)(2,1)S(1)}, u32[]{:S(2)}, u32[]{:S(2)}) collective-permute-start(bf16[2,256,512]{1,2,0:T(8,128)(2,1)S(1)} %fusion.24), channel_id=1, source_target_pairs={{0,1},{1,2},{2,3},{3,4},{4,5},{5,6},{6,7},{7,8},{8,9},{9,10},{10,1... | collective-permute-start | bytes 1572872 | tf_op jit(solution)/shard_map/ppermute | solution.py:20
  553.2 9.0 %all-to-all-start.7 = ((bf16[2,128,512]{2,1,0:T(8,128)(2,1)}), bf16[2,128,512]{2,1,0:T(8,128)(2,1)S(1)}, u32[]{:S(2)}, u32[]{:S(2)}) async-start(bf16[2,128,512]{2,1,0:T(8,128)(2,1)} %bitcast.36), calls=%async_computation.7 | async-start | bytes 524288 | tf_op jit(solution)/shard_map/all_to_all | solution.py:136
  562.2 10.1 %all-to-all-start.8 = ((bf16[2,128,512]{2,1,0:T(8,128)(2,1)}), bf16[2,128,512]{2,1,0:T(8,128)(2,1)S(1)}, u32[]{:S(2)}, u32[]{:S(2)}) async-start(bf16[2,128,512]{2,1,0:T(8,128)(2,1)} %bitcast.39), calls=%async_computation.8 | async-start | bytes 524288 | tf_op jit(solution)/shard_map/all_to_all | solution.py:137
  572.3 14.4 %all-to-all-start.6 = ((bf16[2,128,2560]{1,2,0:T(8,128)(2,1)}), bf16[2,128,2560]{1,2,0:T(8,128)(2,1)S(1)}, u32[]{:S(2)}, u32[]{:S(2)}) async-start(bf16[2,128,2560]{1,2,0:T(8,128)(2,1)} %copy.145), calls=%async_computation.6 | async-start | bytes 2621440 | tf_op jit(solution)/shard_map/all_to_all | solution.py:135
  (33 other events, 57.0 us)
where the time goes:
time: 591 us; the launch traced here: 588 us
  waiting for transfers between devices  253 us (43%)
  matrix products  155 us (26%)
  local copies, waits for them, and re-layouts  91.1 us (15%)
  starting transfers between devices  63.3 us (11%)
  other arithmetic  22.7 us (4%)
    ppermute x15, waiting for transfers between devices, passed_along(): return lax.ppermute(array, axis, pairs)  208 us
    dot_general x16, matrix products, attend(): jnp.einsum('kgts,skd->tkgd', grad_scores, key_block, preferred_element_ty...  79.8 us
    while x105, local copies, waits for them, and re-layouts  31.7 us
    ppermute x15, starting transfers between devices, passed_along(): return lax.ppermute(array, axis, pairs)  31 us
    dot_general x16, matrix products, attend(): jnp.einsum('tkgd,skd->kgts', out_grads, value_block, preferred_element_ty...  26.7 us
    convert_element_type x4, local copies, waits for them, and re-layouts, local(): query_rows, key_rows, value_rows, grad_rows, total_rows, delta_rows = (la...  26.5 us
    dot_general x16, matrix products, attend(): jnp.einsum('kgts,tkgd->skd', probs_low, out_grads, preferred_element_type...  18.4 us
    add x15, other arithmetic, attend(): return (key_sums + added, query_grad + query_part)  16.8 us
  transfers between devices with their start and end apart: 40, of which 24 were waited for; matrix products, arithmetic and copies ran while one was open for 19% of the time, Pallas kernels for 0%

commit v1 on v0

--- a/solution.py
+++ b/solution.py
@@ -1,12 +1,375 @@
+import functools
+import math
+
 import jax
 import jax.numpy as jnp
 from jax import lax
+from jax.experimental import pallas as pl
+from jax.experimental.pallas import tpu as pltpu
 from jax.sharding import PartitionSpec as P
 
 QH = 40
 KVH = 8
 HD = 128
 BLOCK = 128
+TREE_B = 32
+GROUP = QH // KVH
+SCALING = HD ** (-0.5)
+F32 = jnp.float32
+BF16 = jnp.bfloat16
+
+Q_ROWS = GROUP * BLOCK
+LIST_AT = 2 * BLOCK
+KV_ROWS = LIST_AT + 16
+X_AT = 2 * Q_ROWS
+QG_ROWS = X_AT + 48
+COUNT_COL = TREE_B
+OWN_COL = TREE_B + 1
+VMEM_LIMIT = 20 << 20
+
+
+def dot_nt(a, b):
+    return lax.dot_general(a, b, (((1,), (1,)), ((), ())), preferred_element_type=F32)
+
+
+def dot_nn(a, b):
+    return lax.dot_general(a, b, (((1,), (0,)), ((), ())), preferred_element_type=F32)
+
+
+def three_parts(array):
+    high = array.astype(BF16)
+    rest = array - high.astype(F32)
+    middle = rest.astype(BF16)
+    return high, middle, (rest - middle.astype(F32)).astype(BF16)
+
+
+def in_vmem(count):
+    return [pl.BlockSpec(memory_space=pltpu.VMEM)] * count
+
+
+def call(kernel, name, in_specs, outs, scratch, micros, args, after=(), limit=VMEM_LIMIT):
+    given = len(args)
+
+    def body(*refs):
+        kernel(*refs[:given], *refs[given + len(after) :])
+
+    return pl.pallas_call(
+        body,
+        name=name,
+        in_specs=[*in_specs, *[pl.BlockSpec(memory_space=pl.ANY)] * len(after)],
+        out_specs=in_vmem(len(outs)),
+        out_shape=[jax.ShapeDtypeStruct(*out) for out in outs],
+        scratch_shapes=scratch,
+        cost_estimate=pl.CostEstimate(flops=int(micros * 1e9), bytes_accessed=int(micros * 3e6), transcendentals=0),
+        compiler_params=pltpu.CompilerParams(vmem_limit_bytes=limit),
+    )(*args, *after)
+
+
+def kv_pack_kernel(key_in, value_in, lists_in, kept, given, rows, key, value, lists, arrived):
+    copies = [
+        pltpu.make_async_copy(source, target, arrived.at[i])
+        for i, (source, target) in enumerate(((lists_in, lists), (key_in, key), (value_in, value)))
+    ]
+    for copy in copies:
+        copy.start()
+    position, parity = lax.axis_index("blk"), lax.axis_index("head")
+    me = lax.rem(position, KVH)
+    first = (position - me) * 2
+    rows[...] = jnp.full(rows.shape, -1.0, F32)
+    for copy in copies:
+        copy.wait()
+    rows[:2, :TREE_B] = lists[...].astype(F32)
+    row = jnp.where(parity == 0, rows[0:1, :], rows[1:2, :])
+    seen = row >= 0
+    count = jnp.sum(jnp.where(seen, 1.0, 0.0)) - 1.0
+    lane = lax.broadcasted_iota(jnp.int32, row.shape, 1)
+    row = jnp.where(seen, row - first.astype(F32), -1.0)
+    row = jnp.where(lane == COUNT_COL, count, row)
+    row = jnp.where(lane == OWN_COL, (2 * me + parity).astype(F32), row)
+    tile = jnp.broadcast_to(row, (KV_ROWS - LIST_AT, HD)).astype(BF16)
+    for i, chip in enumerate(CHIPS):
+        for k, target in ((chip, kept), (chip + 1, given)):
+            columns = pl.ds(pl.multiple_of((me ^ k) * HD, HD), HD)
+            target[i, :BLOCK, :] = key[:, columns]
+            target[i, BLOCK:LIST_AT, :] = value[:, columns]
+            target[i, LIST_AT:, :] = tile
+
+
+def kv_pack(key_act, value_act, kv_lists):
+    outs = [((len(CHIPS), KV_ROWS, HD), BF16)] * 2
+    args = (key_act, value_act, kv_lists)
+    scratch = [pltpu.VMEM((8, HD), F32), *(pltpu.VMEM(arg.shape, arg.dtype) for arg in args), pltpu.SemaphoreType.DMA((3,))]
+    specs = [pl.BlockSpec(memory_space=pl.ANY)] * 3
+    return call(kv_pack_kernel, "kv_pack", specs, outs, scratch, 1, args, limit=60 << 20)
+
+
+def pair_up_kernel(mine, theirs, *pairs):
+    for i, pair in enumerate(pairs):
+        pair[0] = mine[i]
+        pair[1] = theirs[i]
+
+
+def pair_up(mine, theirs, after=()):
+    outs = [((2, *mine.shape[1:]), mine.dtype)] * mine.shape[0]
+    return call(pair_up_kernel, "pair_up", in_vmem(2), outs, [], 0.5, (mine, theirs), after)
+
+
+def pass_on_kernel(source, target):
+    target[...] = source[...]
+
+
+def pass_on(array, after):
+    return call(pass_on_kernel, "pass_on", in_vmem(1), [(array.shape, array.dtype)], [], 0.2, (array,), after)[0]
+
+
+def kv_sum_kernel(mine, theirs, *sums):
+    for i, ref in enumerate(sums):
+        ref[...] = (mine[i] + theirs[i].astype(F32)).astype(BF16)
+
+
+def kv_sum(mine, theirs):
+    outs = [(mine.shape[1:], BF16)] * mine.shape[0]
+    return call(kv_sum_kernel, "kv_sum", in_vmem(2), outs, [], 0.5, (mine, theirs))
+
+
+def qg_pack_kernel(slots, query, grad, out, totals, *rest):
+    packed, totals_by_group = rest[:-1], rest[-1]
+    me = lax.rem(lax.axis_index("blk"), KVH)
+    totals_by_group[...] = jnp.zeros(totals_by_group.shape, F32)
+    for g in range(KVH):
+        totals_by_group[g, :GROUP, :] = totals[g * GROUP : (g + 1) * GROUP, :]
+    head_of = lax.broadcasted_iota(jnp.int32, (8, Q_ROWS), 1) // HD
+    picks = jnp.where(head_of == lax.broadcasted_iota(jnp.int32, (8, Q_ROWS), 0), 1.0, 0.0).astype(BF16)
+    for message, ks in zip(packed, slots):
+        for n, k in enumerate(ks):
+            columns = pl.ds(pl.multiple_of((me ^ k) * Q_ROWS, Q_ROWS), Q_ROWS)
+            queries, grads = query[:, columns], grad[:, columns]
+            for h in range(GROUP):
+                message[n, h * BLOCK : (h + 1) * BLOCK, :] = queries[:, h * HD : (h + 1) * HD]
+                message[n, Q_ROWS + h * BLOCK : Q_ROWS + (h + 1) * BLOCK, :] = grads[:, h * HD : (h + 1) * HD]
+            product = grads.astype(F32) * out[:, columns].astype(F32)
+            high = product.astype(BF16)
+            low = (product - high.astype(F32)).astype(BF16)
+            delta = dot_nt(picks, high) + dot_nt(picks, low)
+            extras = jnp.concatenate([totals_by_group[me ^ k], delta], axis=0)
+            for i, part in enumerate(three_parts(extras)):
+                message[n, X_AT + 16 * i : X_AT + 16 * (i + 1), :] = part
+
+
+def qg_pack(slots, query_act, grad_out, attn_out, totals, after):
+    outs = [((len(ks), QG_ROWS, HD), BF16) for ks in slots]
+    scratch = [pltpu.VMEM((KVH, 8, HD), F32)]
+    args = (query_act, grad_out, attn_out, totals)
+    return call(functools.partial(qg_pack_kernel, slots), "qg_pack", in_vmem(4), outs, scratch, 1, args, after)
+
+
+def attend_kernel(ks, kind, *refs):
+    refs = list(refs)
+    opens, closes = kind == "first", kind == "last"
+    lists = refs.pop(0)
+    messages = []
+    while len(messages) < len(ks):
+        ref = refs.pop(0)
+        messages += [ref.at[n] for n in range(ref.shape[0])]
+    if opens:
+        kv_own, kv_other = [refs.pop(0) for _ in CHIPS], [refs.pop(0) for _ in CHIPS]
+    else:
+        keys, keys_t, values, sums_in = (refs.pop(0) for _ in range(4))
+    if closes:
+        earlier = refs.pop(0)
+        backs = [refs.pop(0) for _ in ks]
+        for n, back in enumerate(backs):
+            back[0] = earlier[n]
+        query_grads = [back.at[1] for back in backs]
+        mine, others = [refs.pop(0) for _ in range(2)], [refs.pop(0) for _ in range(2)]
+    else:
+        back = refs.pop(0)
+        query_grads = [back.at[n] for n in range(len(ks))]
+    if opens:
+        keys, keys_t, values = (refs.pop(0) for _ in range(3))
+    sums = refs.pop(0)
+    query_sum, probs_held, scores_held = refs
+    me, parity = lists[0, OWN_COL] // 2, lists[0, OWN_COL] % 2
+    spare = 2 * KVH
+
+    if opens:
+        for own, other, chip in zip(kv_own, kv_other, CHIPS):
+            for n in range(2):
+                at = 2 * (me ^ (chip + n))
+                for ref, j in ((own, at + parity), (other, at + 1 - parity)):
+                    keys[j] = ref[n, :BLOCK, :]
+                    values[j] = ref[n, BLOCK:LIST_AT, :]
+                    keys_t[j] = ref[n, :BLOCK, :].T
+        zero = jnp.zeros((BLOCK, HD), BF16)
+        keys[spare], keys_t[spare], values[spare] = zero, zero, zero
+        sums[...] = jnp.zeros(sums.shape, F32)
+    else:
+        sums[...] = sums_in[...]
+
+    def both(ref, pair, axis):
+        return jnp.concatenate([ref[j] for j in pair], axis=axis)
+
+    def produce(n, pair, extras, diagonal):
+        totals, deltas = extras
+        scores = dot_nt(both(keys, pair, 0), messages[n][:Q_ROWS, :])
+        probs = jnp.exp2(scores * (SCALING * math.log2(math.e)) - totals)
+        if diagonal:
+            at_key = lax.broadcasted_iota(jnp.int32, probs.shape, 0) - BLOCK
+            at_query = lax.broadcasted_iota(jnp.int32, probs.shape, 1) % BLOCK
+            probs = jnp.where(at_key <= at_query, probs, 0.0)
+        grad_probs = dot_nt(both(values, pair, 0), messages[n][Q_ROWS:X_AT, :])
+        probs_held[...] = probs.astype(BF16)
+        scores_held[...] = (probs * (grad_probs - deltas)).astype(BF16)
+
+    def consume(n, pair):
+        probs_low, grad_scores = probs_held[...], scores_held[...]
+        value_part = dot_nn(probs_low, messages[n][Q_ROWS:X_AT, :])
+        key_part = dot_nn(grad_scores, messages[n][:Q_ROWS, :])
+        query_sum[...] += dot_nn(both(keys_t, pair, 1), grad_scores)
+        for i, j in enumerate(pair):
+            sums[j, :BLOCK, :] += key_part[i * BLOCK : (i + 1) * BLOCK, :]
+            sums[j, BLOCK:, :] += value_part[i * BLOCK : (i + 1) * BLOCK, :]
+
+    def finish(n):
+        for h in range(GROUP):
+            part = query_sum[:, h * BLOCK : (h + 1) * BLOCK].T
+            query_grads[n][h * BLOCK : (h + 1) * BLOCK, :] = (part * SCALING).astype(BF16)
+
+    pair = None
+    for n, k in enumerate(ks):
+        parts = [messages[n][X_AT + 16 * i : X_AT + 16 * (i + 1), :].astype(F32) for i in range(3)]
+        rows = parts[0] + parts[1] + parts[2]
+        totals = jnp.concatenate([rows[h : h + 1, :] for h in range(GROUP)], axis=1) * math.log2(math.e)
+        deltas = jnp.concatenate([rows[8 + h : 9 + h, :] for h in range(GROUP)], axis=1)
+        extras = (totals, deltas)
+        count = lists[k, COUNT_COL]
+        pairs = count // 2
+        left = jnp.where(count % 2 == 1, lists[k, jnp.maximum(count - 1, 0)], spare)
+        if pair is not None:
+            consume(n - 1, pair)
+        produce(n, (left, lists[k, OWN_COL]), extras, True)
+        if pair is not None:
+            finish(n - 1)
+        query_sum[...] = jnp.zeros(query_sum.shape, F32)
+
+        def visit(t, held):
+            consume(n, held)
+            following = (lists[k, 2 * t], lists[k, 2 * t + 1])
+            produce(n, following, extras, False)
+            return following
+
+        pair = lax.fori_loop(0, pairs, visit, (left, lists[k, OWN_COL]))
+    consume(len(ks) - 1, pair)
+    finish(len(ks) - 1)
+
+    if closes:
+        for half, own, other in zip(BACK_HALVES, mine, others):
+            for i, k in enumerate(half):
+                at = 2 * (me ^ k)
+                own[i, :BLOCK, :] = sums[at + parity, :BLOCK, :] * SCALING
+                own[i, BLOCK:, :] = sums[at + parity, BLOCK:, :]
+                other[i, :BLOCK, :] = (sums[at + 1 - parity, :BLOCK, :] * SCALING).astype(BF16)
+                other[i, BLOCK:, :] = sums[at + 1 - parity, BLOCK:, :].astype(BF16)
+
+
+def attend(name, kind, ks, lists, messages, state, micros):
+    blocks = 2 * KVH + 1
+    sums = ((blocks, 2 * BLOCK, HD), F32)
+    scratch = []
+    if kind == "last":
+        outs = [((2, Q_ROWS, HD), BF16)] * len(ks)
+        outs += [((KVH // 2, 2 * BLOCK, HD), kind) for kind in (F32, F32, BF16, BF16)]
+        scratch = [pltpu.VMEM(*sums)]
+    else:
+        outs = [((len(ks), Q_ROWS, HD), BF16)]
+        if kind == "first":
+            outs += [((blocks, BLOCK, HD), BF16)] * 3
+        outs += [sums]
+    scratch += [pltpu.VMEM((HD, Q_ROWS), F32), pltpu.VMEM((2 * BLOCK, Q_ROWS), BF16), pltpu.VMEM((2 * BLOCK, Q_ROWS), BF16)]
+    specs = [pl.BlockSpec(memory_space=pltpu.SMEM)] + in_vmem(len(messages) + len(state))
+    kernel = functools.partial(attend_kernel, ks, kind)
+    return call(kernel, name, specs, outs, scratch, micros, (lists, *messages, *state))
+
+
+def query_relay_kernel(own, *refs):
+    given = refs[-1]
+    given[0] = own[1]
+    for i, back in enumerate(refs[:-1]):
+        given[i + 1] = back[1]
+
+
+def query_unpack_kernel(*refs):
+    backs, theirs, query_grad = refs[: len(CHIPS)], refs[len(CHIPS)], refs[len(CHIPS) + 1]
+    me = lax.rem(lax.axis_index("blk"), KVH)
+    for i, chip in enumerate(CHIPS):
+        for k, ref, n in ((chip, backs[i], 0), (chip + 1, theirs, i)):
+            for h in range(GROUP):
+                columns = pl.ds(pl.multiple_of(((me ^ k) * GROUP + h) * HD, HD), HD)
+                query_grad[:, columns] = ref[n, h * BLOCK : (h + 1) * BLOCK, :]
+
+
+def kv_unpack_kernel(*refs):
+    key_grad, value_grad = refs[KVH:]
+    me = lax.rem(lax.axis_index("blk"), KVH)
+    for k in range(KVH):
+        columns = pl.ds(pl.multiple_of((me ^ k) * HD, HD), HD)
+        key_grad[:, columns] = refs[k][:BLOCK, :]
+        value_grad[:, columns] = refs[k][BLOCK:, :]
+
+
+CHIPS = (0, 2, 4, 6)
+VISITS = (("first", (0, 1)), ("more", (6, 7)), ("more", (2, 4)), ("last", (3, 5)))
+EXPECTED = (0.5, 0.5, 0.5, 6)
+BACK_HALVES = ((6, 7, 2, 3), (4, 5, 0, 1))
+
+
+def by_trees(query_act, key_act, value_act, attn_out, grad_out, log_sum, kv_lists):
+    size = lax.axis_size("blk")
+
+    def exchanged(array, k):
+        return lax.ppermute(array, "blk", [(i, i ^ k) for i in range(size)])
+
+    def swapped(array):
+        return lax.ppermute(array, "head", [(0, 1), (1, 0)])
+
+    kept, given = kv_pack(key_act, value_act, kv_lists)
+    beside = exchanged(given, 1)
+    paired = pair_up(kept, beside)
+    kv_own = [paired[0], *(exchanged(part, chip) for part, chip in zip(paired[1:], CHIPS[1:]))]
+    kv_other = [swapped(part) for part in kv_own]
+    lists = jnp.concatenate([part[:, LIST_AT, : OWN_COL + 1] for part in kv_own]).astype(jnp.int32)
+
+    qg = (query_act, grad_out, attn_out, log_sum.T)
+    own, far, given = qg_pack(((0,), (6,), (1, 7)), *qg, (beside,))
+    near = exchanged(given, 1)
+    far = pair_up(far, near[1:], (*kv_own[1:], kv_other[0]))[0]
+    here = {0: (own, near[:1]), 1: (exchanged(far, 6),)}
+    sent = dict(zip((2, 4, 3, 5), qg_pack(((2,), (4,), (3,), (5,)), *qg, (far,))))
+    here[2] = tuple(exchanged(sent[k], k) for k in (2, 4))
+    here[3] = tuple(exchanged(sent[k], k) for k in (3, 5))
+
+    state, grads = (*kv_own, *kv_other), []
+    for i, (kind, ks) in enumerate(VISITS):
+        if kind == "last":
+            state = (*state, grads[-1])
+        results = attend(f"attend_{i}", kind, ks, lists, here[i], state, EXPECTED[i])
+        grads.append(results[0])
+        state = tuple(results[1:]) if kind == "first" else (*state[:3], results[-1])
+    far_back = exchanged(grads[1], 6)
+    backs = [exchanged(results[0], 2), exchanged(results[1], 4), far_back]
+    mine, others = results[2:4], results[4:6]
+    theirs = [swapped(pass_on(others[0], (far_back,))), swapped(others[1])]
+    kv_back = {}
+    for half, own, other in zip(BACK_HALVES, mine, theirs):
+        for k, part in zip(half, kv_sum(own, other)):
+            kv_back[k] = exchanged(part, k) if k else part
+    outs = [((4, Q_ROWS, HD), BF16)]
+    given = call(query_relay_kernel, "query_relay", in_vmem(4), outs, [], 0.5, (grads[0], *backs), theirs)[0]
+    args = (grads[0], *backs, exchanged(given, 1))
+    grad_query = call(query_unpack_kernel, "query_unpack", in_vmem(5), [((BLOCK, QH * HD), BF16)], [], 1, args)
+    args = tuple(kv_back[k] for k in range(KVH))
+    grad_kv = call(kv_unpack_kernel, "kv_unpack", in_vmem(KVH), [((BLOCK, KVH * HD), BF16)] * 2, [], 1, args, grad_query)
+    return (*grad_query, *grad_kv)
 
 
 def passed_along(array, axis, by):
@@ -30,7 +393,7 @@
     )
 
 
-def local(query_act, key_act, value_act, attn_out, grad_out, log_sum, kv_lists):
+def by_ring(query_act, key_act, value_act, attn_out, grad_out, log_sum, kv_lists):
     head_count = lax.axis_size("head")
     blk_count = lax.axis_size("blk")
     sent_delta = head_delta(grad_out, attn_out, QH)
@@ -139,19 +502,20 @@
     return (grad_query, grad_key, grad_value)
 
 
+def local(query_act, *others):
+    head_count = lax.axis_size("head")
+    blk_count = lax.axis_size("blk")
+    if query_act.shape[0] == BLOCK and head_count == 2 and blk_count == 2 * KVH and blk_count * head_count == TREE_B:
+        return by_trees(query_act, *others)
+    return by_ring(query_act, *others)
+
+
 def solution(mesh):
+    rows = P(("blk", "head"), None)
     return jax.shard_map(
         local,
         mesh=mesh,
-        in_specs=(
-            P(("blk", "head"), None),
-            P(("blk", "head"), None),
-            P(("blk", "head"), None),
-            P(("blk", "head"), None),
-            P(("blk", "head"), None),
-            P(("blk", "head"), None),
-            P("blk", None),
-        ),
-        out_specs=(P(("blk", "head"), None), P(("blk", "head"), None), P(("blk", "head"), None)),
+        in_specs=(rows,) * 6 + (P("blk", None),),
+        out_specs=(rows,) * 3,
         check_vma=False,
     )

time: 591 us -> 87.3 us (0.15)
  the two profiles are of different devices: /device:TPU:8 before, /device:TPU:0 now
where the time goes in v1:
time: 87.3 us
  waiting for transfers between devices  30.8 us (35%)
  Pallas kernels  27.2 us (31%)
  starting transfers between devices  25.6 us (29%)
  local copies, waits for them, and re-layouts  2.73 us (3%)
    pallas_call x15, Pallas kernels, call(): pl.pallas_call(body, name=name, in_specs=[*in_specs, *[pl.BlockSpec(memor...  27.2 us
    ppermute x21, starting transfers between devices, exchanged(): return lax.ppermute(array, 'blk', [(i, i ^ k) for i in range(size)])  18.2 us
    ppermute x21, waiting for transfers between devices, exchanged(): return lax.ppermute(array, 'blk', [(i, i ^ k) for i in range(size)])  16.7 us
    ppermute x6, waiting for transfers between devices, swapped(): return lax.ppermute(array, 'head', [(0, 1), (1, 0)])  14.2 us
    ppermute x6, starting transfers between devices, swapped(): return lax.ppermute(array, 'head', [(0, 1), (1, 0)])  7.47 us
    unnamed x18, local copies, waits for them, and re-layouts  2.67 us
  transfers between devices with their start and end apart: 27, of which 14 were waited for; matrix products, arithmetic and copies ran while one was open for 0% of the time, Pallas kernels for 27%

profile of v1, /device:TPU:0, one launch (start us, length us, event | category | flops | bytes accessed | tf_op | source)
XLA Modules:
  0.0 87.3 jit_solution(13987578601801465243)
XLA Ops:
  0.7 2.2 %kv_pack.1 = (bf16[4,272,128]{2,1,0:T(8,128)(2,1)}, bf16[4,272,128]{2,1,0:T(8,128)(2,1)}) custom-call(bf16[128,1024]{1,0:T(8,128)(2,1)} %refs_0_.3, bf16[128,1024]{1,0:T(8,128)(2,1)} %refs_1_.3, s32[2,32]{1,0:T(2,128)} %refs_2_.3), custom_call_target="tpu_custom_call" | custom-call | flops 1000000000 | bytes 3000000 | tf_op jit(solution)/shard_map/kv_pack/pallas_call | solution.py:56
  2.9 0.5 collective-permute-start
  3.4 1.4 %collective-permute-done.refs_1_.refs_4_ = bf16[4,272,128]{2,1,0:T(8,128)(2,1)S(1)} collective-permute-done((bf16[4,272,128]{2,1,0:T(8,128)(2,1)}, bf16[4,272,128]{2,1,0:T(8,128)(2,1)S(1)}, u32[]{:S(2)}, u32[]{:S(2)}) %collective-permute-start) | collective-permute-done | bytes 278560 | tf_op jit(solution)/shard_map/ppermute | solution.py:330
  4.8 1.3 %copy-done.2 = bf16[128,5120]{1,0:T(8,128)(2,1)S(1)} copy-done((bf16[128,5120]{1,0:T(8,128)(2,1)S(1)}, bf16[128,5120]{1,0:T(8,128)(2,1)}, u32[]{:S(2)}) %copy-start.2) | copy-done | bytes 1310744
  6.1 0.7 qg_pack.2
  6.8 0.4 collective-permute-start.4
  7.2 2.9 %collective-permute-start.2 = (bf16[2,272,128]{2,1,0:T(8,128)(2,1)S(1)}, bf16[2,272,128]{2,1,0:T(8,128)(2,1)S(1)}, u32[]{:S(2)}, u32[]{:S(2)}) collective-permute-start(bf16[2,272,128]{2,1,0:T(8,128)(2,1)S(1)} %get-tuple-element.45), channel_id=1, source_target_pairs={{0,4},{1,5},{2,6},{3,7},{4,0},{5,1},{6,2},{7,3},{8,12},{9,13},{10,... | collective-permute-start | bytes 417800 | tf_op jit(solution)/shard_map/ppermute | solution.py:330
  10.1 1.5 %collective-permute-start.1 = (bf16[2,272,128]{2,1,0:T(8,128)(2,1)S(1)}, bf16[2,272,128]{2,1,0:T(8,128)(2,1)S(1)}, u32[]{:S(2)}, u32[]{:S(2)}) collective-permute-start(bf16[2,272,128]{2,1,0:T(8,128)(2,1)S(1)} %get-tuple-element.44), channel_id=1, source_target_pairs={{0,2},{1,3},{2,0},{3,1},{4,6},{5,7},{6,4},{7,5},{8,10},{9,11},{10,... | collective-permute-start | bytes 417800 | tf_op jit(solution)/shard_map/ppermute | solution.py:330
  11.6 1.9 %collective-permute-start.5 = (bf16[2,272,128]{2,1,0:T(8,128)(2,1)S(1)}, bf16[2,272,128]{2,1,0:T(8,128)(2,1)S(1)}, u32[]{:S(2)}, u32[]{:S(2)}) collective-permute-start(bf16[2,272,128]{2,1,0:T(8,128)(2,1)S(1)} %get-tuple-element.43.refs_3_), channel_id=1, source_target_pairs={{0,16},{16,0},{1,17},{17,1},{2,18},{18,2},{3,19},{19,3},{4,20},{20... | collective-permute-start | bytes 417800 | tf_op jit(solution)/shard_map/ppermute | solution.py:333
  13.6 1.0 %collective-permute-done.2.refs_5_.refs_3_ = bf16[2,272,128]{2,1,0:T(8,128)(2,1)S(1)} collective-permute-done((bf16[2,272,128]{2,1,0:T(8,128)(2,1)S(1)}, bf16[2,272,128]{2,1,0:T(8,128)(2,1)S(1)}, u32[]{:S(2)}, u32[]{:S(2)}) %collective-permute-start.2) | collective-permute-done | bytes 139296 | tf_op jit(solution)/shard_map/ppermute | solution.py:330
  14.5 4.1 %collective-permute-done.1.refs_4_.refs_2_ = bf16[2,272,128]{2,1,0:T(8,128)(2,1)S(1)} collective-permute-done((bf16[2,272,128]{2,1,0:T(8,128)(2,1)S(1)}, bf16[2,272,128]{2,1,0:T(8,128)(2,1)S(1)}, u32[]{:S(2)}, u32[]{:S(2)}) %collective-permute-start.1) | collective-permute-done | bytes 139296 | tf_op jit(solution)/shard_map/ppermute | solution.py:330
  18.7 1.5 %collective-permute-start.13 = (bf16[2,1328,128]{2,1,0:T(8,128)(2,1)S(1)}, bf16[2,1328,128]{2,1,0:T(8,128)(2,1)S(1)}, u32[]{:S(2)}, u32[]{:S(2)}) collective-permute-start(bf16[2,1328,128]{2,1,0:T(8,128)(2,1)S(1)} %pair_up.3.refs_4_), channel_id=1, source_target_pairs={{0,6},{1,7},{2,4},{3,5},{4,2},{5,3},{6,0},{7,1},{8,14},{9,15},{10,... | collective-permute-start | bytes 2039816 | tf_op jit(solution)/shard_map/ppermute | solution.py:330
  20.2 1.5 %collective-permute-start.6 = (bf16[2,272,128]{2,1,0:T(8,128)(2,1)S(1)}, bf16[2,272,128]{2,1,0:T(8,128)(2,1)S(1)}, u32[]{:S(2)}, u32[]{:S(2)}) collective-permute-start(bf16[2,272,128]{2,1,0:T(8,128)(2,1)S(1)} %collective-permute-done.1.refs_4_.refs_2_), channel_id=1, source_target_pairs={{0,16},{16,0},{1,17},{17,1},{2,18},{18,2},{3,19},{19,3},{4,20},{20... | collective-permute-start | bytes 417800 | tf_op jit(solution)/shard_map/ppermute | solution.py:333
  21.7 0.5 collective-permute-start.7
  22.2 1.5 %collective-permute-start.8 = (bf16[2,272,128]{2,1,0:T(8,128)(2,1)S(1)}, bf16[2,272,128]{2,1,0:T(8,128)(2,1)S(1)}, u32[]{:S(2)}, u32[]{:S(2)}) collective-permute-start(bf16[2,272,128]{2,1,0:T(8,128)(2,1)S(1)} %collective-permute-done.3.refs_6_.refs_4_), channel_id=1, source_target_pairs={{0,16},{16,0},{1,17},{17,1},{2,18},{18,2},{3,19},{19,3},{4,20},{20... | collective-permute-start | bytes 417800 | tf_op jit(solution)/shard_map/ppermute | solution.py:333
  23.7 0.7 qg_pack.3
  24.4 1.3 %collective-permute-start.11 = (bf16[1,1328,128]{2,1,0:T(8,128)(2,1)S(1)}, bf16[1,1328,128]{2,1,0:T(8,128)(2,1)S(1)}, u32[]{:S(2)}, u32[]{:S(2)}) collective-permute-start(bf16[1,1328,128]{2,1,0:T(8,128)(2,1)S(1)} %get-tuple-element.56), channel_id=1, source_target_pairs={{0,2},{1,3},{2,0},{3,1},{4,6},{5,7},{6,4},{7,5},{8,10},{9,11},{10,... | collective-permute-start | bytes 1019912 | tf_op jit(solution)/shard_map/ppermute | solution.py:330
  25.7 1.1 %collective-permute-done.6.refs_8_ = bf16[2,272,128]{2,1,0:T(8,128)(2,1)S(1)} collective-permute-done((bf16[2,272,128]{2,1,0:T(8,128)(2,1)S(1)}, bf16[2,272,128]{2,1,0:T(8,128)(2,1)S(1)}, u32[]{:S(2)}, u32[]{:S(2)}) %collective-permute-start.6) | collective-permute-done | bytes 139296 | tf_op jit(solution)/shard_map/ppermute | solution.py:333
  26.8 1.6 %collective-permute-start.12 = (bf16[1,1328,128]{2,1,0:T(8,128)(2,1)S(1)}, bf16[1,1328,128]{2,1,0:T(8,128)(2,1)S(1)}, u32[]{:S(2)}, u32[]{:S(2)}) collective-permute-start(bf16[1,1328,128]{2,1,0:T(8,128)(2,1)S(1)} %get-tuple-element.57), channel_id=1, source_target_pairs={{0,4},{1,5},{2,6},{3,7},{4,0},{5,1},{6,2},{7,3},{8,12},{9,13},{10,... | collective-permute-start | bytes 1019912 | tf_op jit(solution)/shard_map/ppermute | solution.py:330
  28.4 0.9 collective-permute-done.7.refs_9_
  29.3 1.5 %collective-permute-done.8.refs_10_ = bf16[2,272,128]{2,1,0:T(8,128)(2,1)S(1)} collective-permute-done((bf16[2,272,128]{2,1,0:T(8,128)(2,1)S(1)}, bf16[2,272,128]{2,1,0:T(8,128)(2,1)S(1)}, u32[]{:S(2)}, u32[]{:S(2)}) %collective-permute-start.8) | collective-permute-done | bytes 139296 | tf_op jit(solution)/shard_map/ppermute | solution.py:333
  30.8 0.1 collective-permute-start.9
  30.9 2.8 %attend_0.1 = (bf16[2,640,128]{2,1,0:T(8,128)(2,1)S(1)}, bf16[17,128,128]{2,1,0:T(8,128)(2,1)S(1)}, bf16[17,128,128]{2,1,0:T(8,128)(2,1)S(1)}, bf16[17,128,128]{2,1,0:T(8,128)(2,1)S(1)}, f32[17,256,128]{2,1,0:T(8,128)S(1)}) custom-call(s32[8,34]{1,0:T(8,128)S(1)} %maximum_convert_fusion.refs_0_, bf16[1,1328,128]{2,1,0:T(8,128)(2,1)S(1)} %get-tuple-element.47.refs_1_, ...), custom_call_target="tpu_custom_call" | custom-call | flops 500000000 | bytes 1500000 | tf_op jit(solution)/shard_map/attend_0/pallas_call | solution.py:56
  33.7 4.2 %collective-permute-done.13.refs_1_ = bf16[2,1328,128]{2,1,0:T(8,128)(2,1)S(1)} collective-permute-done((bf16[2,1328,128]{2,1,0:T(8,128)(2,1)S(1)}, bf16[2,1328,128]{2,1,0:T(8,128)(2,1)S(1)}, u32[]{:S(2)}, u32[]{:S(2)}) %collective-permute-start.13) | collective-permute-done | bytes 679968 | tf_op jit(solution)/shard_map/ppermute | solution.py:330
  37.9 7.3 %attend_1.1 = (bf16[2,640,128]{2,1,0:T(8,128)(2,1)S(1)}, f32[17,256,128]{2,1,0:T(8,128)S(1)}) custom-call(s32[8,34]{1,0:T(8,128)S(1)} %maximum_convert_fusion.refs_0_, bf16[2,1328,128]{2,1,0:T(8,128)(2,1)S(1)} %collective-permute-done.13.refs_1_, bf16[17,128,128]{2,1,0:T(8,128)(2,1)S(1)} %get-tuple-element.53.refs_2_.refs_3_, ...), custom_call_target="tpu_custom_call" | custom-call | flops 500000000 | bytes 1500000 | tf_op jit(solution)/shard_map/attend_1/pallas_call | solution.py:56
  45.3 0.1 collective-permute-start.16
  45.4 5.0 %attend_2.1 = (bf16[2,640,128]{2,1,0:T(8,128)(2,1)S(1)}, f32[17,256,128]{2,1,0:T(8,128)S(1)}) custom-call(s32[8,34]{1,0:T(8,128)S(1)} %maximum_convert_fusion.refs_0_, bf16[1,1328,128]{2,1,0:T(8,128)(2,1)S(1)} %collective-permute-done.11.refs_1_, bf16[1,1328,128]{2,1,0:T(8,128)(2,1)S(1)} %collective-permute-done.12.refs_2_, ...), custom_call_target="tpu_custom_call" | custom-call | flops 500000000 | bytes 1500000 | tf_op jit(solution)/shard_map/attend_2/pallas_call | solution.py:56
  50.4 0.1 collective-permute-done.10.refs_2_
  50.5 1.7 %collective-permute-done.9.refs_1_ = bf16[1,1328,128]{2,1,0:T(8,128)(2,1)S(1)} collective-permute-done((bf16[1,1328,128]{2,1,0:T(8,128)(2,1)S(1)}, bf16[1,1328,128]{2,1,0:T(8,128)(2,1)S(1)}, u32[]{:S(2)}, u32[]{:S(2)}) %collective-permute-start.9) | collective-permute-done | bytes 340000 | tf_op jit(solution)/shard_map/ppermute | solution.py:330
  52.2 5.9 %attend_3.1 = (bf16[2,640,128]{2,1,0:T(8,128)(2,1)S(1)}, bf16[2,640,128]{2,1,0:T(8,128)(2,1)S(1)}, f32[4,256,128]{2,1,0:T(8,128)S(1)}, f32[4,256,128]{2,1,0:T(8,...) custom-call(s32[8,34]{1,0:T(8,128)S(1)} %maximum_convert_fusion.refs_0_, ...), custom_call_target="tpu_custom_call" | custom-call | flops 6000000000 | bytes 18000000 | tf_op jit(solution)/shard_map/attend_3/pallas_call | solution.py:56
  58.1 1.6 %collective-permute-start.14 = (bf16[2,640,128]{2,1,0:T(8,128)(2,1)S(1)}, bf16[2,640,128]{2,1,0:T(8,128)(2,1)S(1)}, u32[]{:S(2)}, u32[]{:S(2)}) collective-permute-start(bf16[2,640,128]{2,1,0:T(8,128)(2,1)S(1)} %get-tuple-element.62), channel_id=1, source_target_pairs={{0,2},{1,3},{2,0},{3,1},{4,6},{5,7},{6,4},{7,5},{8,10},{9,11},{10,... | collective-permute-start | bytes 983048 | tf_op jit(solution)/shard_map/ppermute | solution.py:330
  59.7 0.4 collective-permute-start.15
  60.2 1.5 %collective-permute-start.18 = (bf16[4,256,128]{2,1,0:T(8,128)(2,1)S(1)}, bf16[4,256,128]{2,1,0:T(8,128)(2,1)S(1)}, u32[]{:S(2)}, u32[]{:S(2)}) collective-permute-start(bf16[4,256,128]{2,1,0:T(8,128)(2,1)S(1)} %get-tuple-element.66), channel_id=1, source_target_pairs={{0,16},{16,0},{1,17},{17,1},{2,18},{18,2},{3,19},{19,3},{4,20},{20... | collective-permute-start | bytes 786440 | tf_op jit(solution)/shard_map/ppermute | solution.py:333
  61.7 0.6 collective-permute-start.17
  62.3 7.1 %collective-permute-done.18.refs_5_.refs_1_ = bf16[4,256,128]{2,1,0:T(8,128)(2,1)S(1)} collective-permute-done((bf16[4,256,128]{2,1,0:T(8,128)(2,1)S(1)}, bf16[4,256,128]{2,1,0:T(8,128)(2,1)S(1)}, u32[]{:S(2)}, u32[]{:S(2)}) %collective-permute-start.18) | collective-permute-done | bytes 262176 | tf_op jit(solution)/shard_map/ppermute | solution.py:333
  69.4 3.6 %collective-permute-done.17.refs_4_.refs_1_ = bf16[4,256,128]{2,1,0:T(8,128)(2,1)S(1)} collective-permute-done((bf16[4,256,128]{2,1,0:T(8,128)(2,1)S(1)}, bf16[4,256,128]{2,1,0:T(8,128)(2,1)S(1)}, u32[]{:S(2)}, u32[]{:S(2)}) %collective-permute-start.17) | collective-permute-done | bytes 262176 | tf_op jit(solution)/shard_map/ppermute | solution.py:333
  73.2 0.6 collective-permute-start.20
  73.8 1.0 %collective-permute-start.23 = (bf16[256,128]{1,0:T(8,128)(2,1)S(1)}, bf16[256,128]{1,0:T(8,128)(2,1)S(1)}, u32[]{:S(2)}, u32[]{:S(2)}) collective-permute-start(bf16[256,128]{1,0:T(8,128)(2,1)S(1)} %get-tuple-element.73), channel_id=1, source_target_pairs={{0,4},{1,5},{2,6},{3,7},{4,0},{5,1},{6,2},{7,3},{8,12},{9,13},{10,... | collective-permute-start | bytes 196616 | tf_op jit(solution)/shard_map/ppermute | solution.py:330
  74.8 0.4 collective-permute-start.24
  75.3 1.1 %collective-permute-start.21 = (bf16[256,128]{1,0:T(8,128)(2,1)S(1)}, bf16[256,128]{1,0:T(8,128)(2,1)S(1)}, u32[]{:S(2)}, u32[]{:S(2)}) collective-permute-start(bf16[256,128]{1,0:T(8,128)(2,1)S(1)} %get-tuple-element.71), channel_id=1, source_target_pairs={{0,2},{1,3},{2,0},{3,1},{4,6},{5,7},{6,4},{7,5},{8,10},{9,11},{10,... | collective-permute-start | bytes 196616 | tf_op jit(solution)/shard_map/ppermute | solution.py:330
  76.3 1.1 %collective-permute-start.22 = (bf16[256,128]{1,0:T(8,128)(2,1)S(1)}, bf16[256,128]{1,0:T(8,128)(2,1)S(1)}, u32[]{:S(2)}, u32[]{:S(2)}) collective-permute-start(bf16[256,128]{1,0:T(8,128)(2,1)S(1)} %get-tuple-element.72), channel_id=1, source_target_pairs={{0,3},{1,2},{2,1},{3,0},{4,7},{5,6},{6,5},{7,4},{8,11},{9,10},{10,... | collective-permute-start | bytes 196616 | tf_op jit(solution)/shard_map/ppermute | solution.py:330
  77.4 1.0 %collective-permute-done.23.refs_4_ = bf16[256,128]{1,0:T(8,128)(2,1)S(1)} collective-permute-done((bf16[256,128]{1,0:T(8,128)(2,1)S(1)}, bf16[256,128]{1,0:T(8,128)(2,1)S(1)}, u32[]{:S(2)}, u32[]{:S(2)}) %collective-permute-start.23) | collective-permute-done | bytes 65568 | tf_op jit(solution)/shard_map/ppermute | solution.py:330
  78.4 2.0 %collective-permute-start.25 = (bf16[256,128]{1,0:T(8,128)(2,1)S(1)}, bf16[256,128]{1,0:T(8,128)(2,1)S(1)}, u32[]{:S(2)}, u32[]{:S(2)}) collective-permute-start(bf16[256,128]{1,0:T(8,128)(2,1)S(1)} %get-tuple-element.75), channel_id=1, source_target_pairs={{0,6},{1,7},{2,4},{3,5},{4,2},{5,3},{6,0},{7,1},{8,14},{9,15},{10,... | collective-permute-start | bytes 196616 | tf_op jit(solution)/shard_map/ppermute | solution.py:330
  80.4 1.4 %query_unpack.1.refs_8_ = bf16[128,5120]{1,0:T(8,128)(2,1)} custom-call(bf16[2,640,128]{2,1,0:T(8,128)(2,1)S(1)} %get-tuple-element.49.refs_0_, bf16[2,640,128]{2,1,0:T(8,128)(2,1)S(1)} %collective-permute-done.14.refs_1_, bf16[2,640,128]{2,1,0:T(8,128)(2,1)S(1)} %collective-permute-done.15.refs_2_, ...), custom_call_target="tpu_custom_call" | custom-call | flops 1000000000 | bytes 3000000 | tf_op jit(solution)/shard_map/query_unpack/pallas_call | solution.py:56
  81.9 1.7 %collective-permute-done.25.refs_6_ = bf16[256,128]{1,0:T(8,128)(2,1)S(1)} collective-permute-done((bf16[256,128]{1,0:T(8,128)(2,1)S(1)}, bf16[256,128]{1,0:T(8,128)(2,1)S(1)}, u32[]{:S(2)}, u32[]{:S(2)}) %collective-permute-start.25) | collective-permute-done | bytes 65568 | tf_op jit(solution)/shard_map/ppermute | solution.py:330
  83.5 1.5 %collective-permute-done.26.refs_7_ = bf16[256,128]{1,0:T(8,128)(2,1)S(1)} collective-permute-done((bf16[256,128]{1,0:T(8,128)(2,1)S(1)}, bf16[256,128]{1,0:T(8,128)(2,1)S(1)}, u32[]{:S(2)}, u32[]{:S(2)}) %collective-permute-start.26) | collective-permute-done | bytes 65568 | tf_op jit(solution)/shard_map/ppermute | solution.py:330
  85.0 1.3 %copy-done.5 = bf16[128,5120]{1,0:T(8,128)(2,1)S(1)} copy-done((bf16[128,5120]{1,0:T(8,128)(2,1)S(1)}, bf16[128,5120]{1,0:T(8,128)(2,1)}, u32[]{:S(2)}) %copy-start.5) | copy-done | bytes 1310744
  86.3 0.9 %kv_unpack.1 = (bf16[128,1024]{1,0:T(8,128)(2,1)}, bf16[128,1024]{1,0:T(8,128)(2,1)}) custom-call(bf16[256,128]{1,0:T(8,128)(2,1)S(1)} %get-tuple-element.68.refs_0_, bf16[256,128]{1,0:T(8,128)(2,1)S(1)} %collective-permute-done.20.refs_1_, bf16[256,128]{1,0:T(8,128)(2,1)S(1)} %collective-permute-done.21.refs_2_, ...), custom_call_target="tpu_custom_call" | custom-call | flops 1000000000 | bytes 3000000 | tf_op jit(solution)/shard_map/kv_unpack/pallas_call | solution.py:56
  (45 shorter events, 0.6 us)
Async XLA Ops:
  0.6 4.1 %copy-start.4 = (f32[128,40]{0,1:T(8,128)S(1)}, f32[128,40]{0,1:T(8,128)}, u32[]{:S(2)}) copy-start(f32[128,40]{0,1:T(8,128)} %param.12) | copy-start | bytes 61444
  0.6 4.1 %copy-start.1 = (bf16[128,5120]{1,0:T(8,128)(2,1)S(1)}, bf16[128,5120]{1,0:T(8,128)(2,1)}, u32[]{:S(2)}) copy-start(bf16[128,5120]{1,0:T(8,128)(2,1)} %refs_1_.5) | copy-start | bytes 3932164
  0.7 4.1 %copy-start = (bf16[128,5120]{1,0:T(8,128)(2,1)S(1)}, bf16[128,5120]{1,0:T(8,128)(2,1)}, u32[]{:S(2)}) copy-start(bf16[128,5120]{1,0:T(8,128)(2,1)} %refs_0_.5) | copy-start | bytes 3932164
  2.9 1.9 %collective-permute-start = (bf16[4,272,128]{2,1,0:T(8,128)(2,1)}, bf16[4,272,128]{2,1,0:T(8,128)(2,1)S(1)}, u32[]{:S(2)}, u32[]{:S(2)}) collective-permute-start(bf16[4,272,128]{2,1,0:T(8,128)(2,1)} %get-tuple-element.42), channel_id=1, source_target_pairs={{0,1},{1,0},{2,3},{3,2},{4,5},{5,4},{6,7},{7,6},{8,9},{9,8},{10,11... | collective-permute-start | bytes 835592 | tf_op jit(solution)/shard_map/ppermute | solution.py:330
  4.8 1.3 %copy-start.2 = (bf16[128,5120]{1,0:T(8,128)(2,1)S(1)}, bf16[128,5120]{1,0:T(8,128)(2,1)}, u32[]{:S(2)}) copy-start(bf16[128,5120]{1,0:T(8,128)(2,1)} %refs_2_.5) | copy-start | bytes 3932164
  6.1 1.1 %copy-start.6 = (bf16[4,272,128]{2,1,0:T(8,128)(2,1)S(1)}, bf16[4,272,128]{2,1,0:T(8,128)(2,1)}, u32[]{:S(2)}) copy-start(bf16[4,272,128]{2,1,0:T(8,128)(2,1)} %get-tuple-element.41.refs_0_) | copy-start | bytes 835588
  6.8 6.7 %collective-permute-start.4 = (bf16[2,1328,128]{2,1,0:T(8,128)(2,1)S(1)}, bf16[2,1328,128]{2,1,0:T(8,128)(2,1)S(1)}, u32[]{:S(2)}, u32[]{:S(2)}) collective-permute-start(bf16[2,1328,128]{2,1,0:T(8,128)(2,1)S(1)} %get-tuple-element.48), channel_id=1, source_target_pairs={{0,1},{1,0},{2,3},{3,2},{4,5},{5,4},{6,7},{7,6},{8,9},{9,8},{10,11... | collective-permute-start | bytes 2039816 | tf_op jit(solution)/shard_map/ppermute | solution.py:330
  7.2 7.3 %collective-permute-start.2 = (bf16[2,272,128]{2,1,0:T(8,128)(2,1)S(1)}, bf16[2,272,128]{2,1,0:T(8,128)(2,1)S(1)}, u32[]{:S(2)}, u32[]{:S(2)}) collective-permute-start(bf16[2,272,128]{2,1,0:T(8,128)(2,1)S(1)} %get-tuple-element.45), channel_id=1, source_target_pairs={{0,4},{1,5},{2,6},{3,7},{4,0},{5,1},{6,2},{7,3},{8,12},{9,13},{10,... | collective-permute-start | bytes 417800 | tf_op jit(solution)/shard_map/ppermute | solution.py:330
  10.1 8.6 %collective-permute-start.1 = (bf16[2,272,128]{2,1,0:T(8,128)(2,1)S(1)}, bf16[2,272,128]{2,1,0:T(8,128)(2,1)S(1)}, u32[]{:S(2)}, u32[]{:S(2)}) collective-permute-start(bf16[2,272,128]{2,1,0:T(8,128)(2,1)S(1)} %get-tuple-element.44), channel_id=1, source_target_pairs={{0,2},{1,3},{2,0},{3,1},{4,6},{5,7},{6,4},{7,5},{8,10},{9,11},{10,... | collective-permute-start | bytes 417800 | tf_op jit(solution)/shard_map/ppermute | solution.py:330
  11.6 7.1 %collective-permute-start.3 = (bf16[2,272,128]{2,1,0:T(8,128)(2,1)S(1)}, bf16[2,272,128]{2,1,0:T(8,128)(2,1)S(1)}, u32[]{:S(2)}, u32[]{:S(2)}) collective-permute-start(bf16[2,272,128]{2,1,0:T(8,128)(2,1)S(1)} %get-tuple-element.46), channel_id=1, source_target_pairs={{0,6},{1,7},{2,4},{3,5},{4,2},{5,3},{6,0},{7,1},{8,14},{9,15},{10,... | collective-permute-start | bytes 417800 | tf_op jit(solution)/shard_map/ppermute | solution.py:330
  11.6 12.1 %copy-start.3 = (bf16[128,5120]{1,0:T(8,128)(2,1)S(1)}, bf16[128,5120]{1,0:T(8,128)(2,1)}, u32[]{:S(2)}) copy-start(bf16[128,5120]{1,0:T(8,128)(2,1)} %refs_2_.5) | copy-start | bytes 3932164
  11.6 7.0 %collective-permute-start.5 = (bf16[2,272,128]{2,1,0:T(8,128)(2,1)S(1)}, bf16[2,272,128]{2,1,0:T(8,128)(2,1)S(1)}, u32[]{:S(2)}, u32[]{:S(2)}) collective-permute-start(bf16[2,272,128]{2,1,0:T(8,128)(2,1)S(1)} %get-tuple-element.43.refs_3_), channel_id=1, source_target_pairs={{0,16},{16,0},{1,17},{17,1},{2,18},{18,2},{3,19},{19,3},{4,20},{20... | collective-permute-start | bytes 417800 | tf_op jit(solution)/shard_map/ppermute | solution.py:333
  18.7 19.2 %collective-permute-start.13 = (bf16[2,1328,128]{2,1,0:T(8,128)(2,1)S(1)}, bf16[2,1328,128]{2,1,0:T(8,128)(2,1)S(1)}, u32[]{:S(2)}, u32[]{:S(2)}) collective-permute-start(bf16[2,1328,128]{2,1,0:T(8,128)(2,1)S(1)} %pair_up.3.refs_4_), channel_id=1, source_target_pairs={{0,6},{1,7},{2,4},{3,5},{4,2},{5,3},{6,0},{7,1},{8,14},{9,15},{10,... | collective-permute-start | bytes 2039816 | tf_op jit(solution)/shard_map/ppermute | solution.py:330
  20.2 6.6 %collective-permute-start.6 = (bf16[2,272,128]{2,1,0:T(8,128)(2,1)S(1)}, bf16[2,272,128]{2,1,0:T(8,128)(2,1)S(1)}, u32[]{:S(2)}, u32[]{:S(2)}) collective-permute-start(bf16[2,272,128]{2,1,0:T(8,128)(2,1)S(1)} %collective-permute-done.1.refs_4_.refs_2_), channel_id=1, source_target_pairs={{0,16},{16,0},{1,17},{17,1},{2,18},{18,2},{3,19},{19,3},{4,20},{20... | collective-permute-start | bytes 417800 | tf_op jit(solution)/shard_map/ppermute | solution.py:333
  21.7 7.6 %collective-permute-start.7 = (bf16[2,272,128]{2,1,0:T(8,128)(2,1)S(1)}, bf16[2,272,128]{2,1,0:T(8,128)(2,1)S(1)}, u32[]{:S(2)}, u32[]{:S(2)}) collective-permute-start(bf16[2,272,128]{2,1,0:T(8,128)(2,1)S(1)} %collective-permute-done.2.refs_5_.refs_3_), channel_id=1, source_target_pairs={{0,16},{16,0},{1,17},{17,1},{2,18},{18,2},{3,19},{19,3},{4,20},{20... | collective-permute-start | bytes 417800 | tf_op jit(solution)/shard_map/ppermute | solution.py:333
  22.2 8.5 %collective-permute-start.8 = (bf16[2,272,128]{2,1,0:T(8,128)(2,1)S(1)}, bf16[2,272,128]{2,1,0:T(8,128)(2,1)S(1)}, u32[]{:S(2)}, u32[]{:S(2)}) collective-permute-start(bf16[2,272,128]{2,1,0:T(8,128)(2,1)S(1)} %collective-permute-done.3.refs_6_.refs_4_), channel_id=1, source_target_pairs={{0,16},{16,0},{1,17},{17,1},{2,18},{18,2},{3,19},{19,3},{4,20},{20... | collective-permute-start | bytes 417800 | tf_op jit(solution)/shard_map/ppermute | solution.py:333
  24.4 21.0 %collective-permute-start.11 = (bf16[1,1328,128]{2,1,0:T(8,128)(2,1)S(1)}, bf16[1,1328,128]{2,1,0:T(8,128)(2,1)S(1)}, u32[]{:S(2)}, u32[]{:S(2)}) collective-permute-start(bf16[1,1328,128]{2,1,0:T(8,128)(2,1)S(1)} %get-tuple-element.56), channel_id=1, source_target_pairs={{0,2},{1,3},{2,0},{3,1},{4,6},{5,7},{6,4},{7,5},{8,10},{9,11},{10,... | collective-permute-start | bytes 1019912 | tf_op jit(solution)/shard_map/ppermute | solution.py:330
  26.8 18.6 %collective-permute-start.12 = (bf16[1,1328,128]{2,1,0:T(8,128)(2,1)S(1)}, bf16[1,1328,128]{2,1,0:T(8,128)(2,1)S(1)}, u32[]{:S(2)}, u32[]{:S(2)}) collective-permute-start(bf16[1,1328,128]{2,1,0:T(8,128)(2,1)S(1)} %get-tuple-element.57), channel_id=1, source_target_pairs={{0,4},{1,5},{2,6},{3,7},{4,0},{5,1},{6,2},{7,3},{8,12},{9,13},{10,... | collective-permute-start | bytes 1019912 | tf_op jit(solution)/shard_map/ppermute | solution.py:330
  29.3 21.3 %collective-permute-start.10 = (bf16[1,1328,128]{2,1,0:T(8,128)(2,1)S(1)}, bf16[1,1328,128]{2,1,0:T(8,128)(2,1)S(1)}, u32[]{:S(2)}, u32[]{:S(2)}) collective-permute-start(bf16[1,1328,128]{2,1,0:T(8,128)(2,1)S(1)} %get-tuple-element.52), channel_id=1, source_target_pairs={{0,5},{1,4},{2,7},{3,6},{4,1},{5,0},{6,3},{7,2},{8,13},{9,12},{10,... | collective-permute-start | bytes 1019912 | tf_op jit(solution)/shard_map/ppermute | solution.py:330
  30.8 21.5 %collective-permute-start.9 = (bf16[1,1328,128]{2,1,0:T(8,128)(2,1)S(1)}, bf16[1,1328,128]{2,1,0:T(8,128)(2,1)S(1)}, u32[]{:S(2)}, u32[]{:S(2)}) collective-permute-start(bf16[1,1328,128]{2,1,0:T(8,128)(2,1)S(1)} %get-tuple-element.51), channel_id=1, source_target_pairs={{0,3},{1,2},{2,1},{3,0},{4,7},{5,6},{6,5},{7,4},{8,11},{9,10},{10,... | collective-permute-start | bytes 1019912 | tf_op jit(solution)/shard_map/ppermute | solution.py:330
  45.3 16.4 %collective-permute-start.16 = (bf16[2,640,128]{2,1,0:T(8,128)(2,1)S(1)}, bf16[2,640,128]{2,1,0:T(8,128)(2,1)S(1)}, u32[]{:S(2)}, u32[]{:S(2)}) collective-permute-start(bf16[2,640,128]{2,1,0:T(8,128)(2,1)S(1)} %get-tuple-element.64), channel_id=1, source_target_pairs={{0,6},{1,7},{2,4},{3,5},{4,2},{5,3},{6,0},{7,1},{8,14},{9,15},{10,... | collective-permute-start | bytes 983048 | tf_op jit(solution)/shard_map/ppermute | solution.py:330
  58.1 11.3 %collective-permute-start.14 = (bf16[2,640,128]{2,1,0:T(8,128)(2,1)S(1)}, bf16[2,640,128]{2,1,0:T(8,128)(2,1)S(1)}, u32[]{:S(2)}, u32[]{:S(2)}) collective-permute-start(bf16[2,640,128]{2,1,0:T(8,128)(2,1)S(1)} %get-tuple-element.62), channel_id=1, source_target_pairs={{0,2},{1,3},{2,0},{3,1},{4,6},{5,7},{6,4},{7,5},{8,10},{9,11},{10,... | collective-permute-start | bytes 983048 | tf_op jit(solution)/shard_map/ppermute | solution.py:330
  59.7 9.7 %collective-permute-start.15 = (bf16[2,640,128]{2,1,0:T(8,128)(2,1)S(1)}, bf16[2,640,128]{2,1,0:T(8,128)(2,1)S(1)}, u32[]{:S(2)}, u32[]{:S(2)}) collective-permute-start(bf16[2,640,128]{2,1,0:T(8,128)(2,1)S(1)} %get-tuple-element.63), channel_id=1, source_target_pairs={{0,4},{1,5},{2,6},{3,7},{4,0},{5,1},{6,2},{7,3},{8,12},{9,13},{10,... | collective-permute-start | bytes 983048 | tf_op jit(solution)/shard_map/ppermute | solution.py:330
  60.2 9.2 %collective-permute-start.18 = (bf16[4,256,128]{2,1,0:T(8,128)(2,1)S(1)}, bf16[4,256,128]{2,1,0:T(8,128)(2,1)S(1)}, u32[]{:S(2)}, u32[]{:S(2)}) collective-permute-start(bf16[4,256,128]{2,1,0:T(8,128)(2,1)S(1)} %get-tuple-element.66), channel_id=1, source_target_pairs={{0,16},{16,0},{1,17},{17,1},{2,18},{18,2},{3,19},{19,3},{4,20},{20... | collective-permute-start | bytes 786440 | tf_op jit(solution)/shard_map/ppermute | solution.py:333
  61.7 11.3 %collective-permute-start.17 = (bf16[4,256,128]{2,1,0:T(8,128)(2,1)S(1)}, bf16[4,256,128]{2,1,0:T(8,128)(2,1)S(1)}, u32[]{:S(2)}, u32[]{:S(2)}) collective-permute-start(bf16[4,256,128]{2,1,0:T(8,128)(2,1)S(1)} %pass_on.1), channel_id=1, source_target_pairs={{0,16},{16,0},{1,17},{17,1},{2,18},{18,2},{3,19},{19,3},{4,20},{20... | collective-permute-start | bytes 786440 | tf_op jit(solution)/shard_map/ppermute | solution.py:333
  73.0 7.4 %collective-permute-start.19 = (bf16[4,640,128]{2,1,0:T(8,128)(2,1)S(1)}, bf16[4,640,128]{2,1,0:T(8,128)(2,1)S(1)}, u32[]{:S(2)}, u32[]{:S(2)}) collective-permute-start(bf16[4,640,128]{2,1,0:T(8,128)(2,1)S(1)} %query_relay.1), channel_id=1, source_target_pairs={{0,1},{1,0},{2,3},{3,2},{4,5},{5,4},{6,7},{7,6},{8,9},{9,8},{10,11... | collective-permute-start | bytes 1966088 | tf_op jit(solution)/shard_map/ppermute | solution.py:330
  73.2 3.1 %collective-permute-start.20 = (bf16[256,128]{1,0:T(8,128)(2,1)S(1)}, bf16[256,128]{1,0:T(8,128)(2,1)S(1)}, u32[]{:S(2)}, u32[]{:S(2)}) collective-permute-start(bf16[256,128]{1,0:T(8,128)(2,1)S(1)} %get-tuple-element.69), channel_id=1, source_target_pairs={{0,1},{1,0},{2,3},{3,2},{4,5},{5,4},{6,7},{7,6},{8,9},{9,8},{10,11... | collective-permute-start | bytes 196616 | tf_op jit(solution)/shard_map/ppermute | solution.py:330
  73.8 4.6 %collective-permute-start.23 = (bf16[256,128]{1,0:T(8,128)(2,1)S(1)}, bf16[256,128]{1,0:T(8,128)(2,1)S(1)}, u32[]{:S(2)}, u32[]{:S(2)}) collective-permute-start(bf16[256,128]{1,0:T(8,128)(2,1)S(1)} %get-tuple-element.73), channel_id=1, source_target_pairs={{0,4},{1,5},{2,6},{3,7},{4,0},{5,1},{6,2},{7,3},{8,12},{9,13},{10,... | collective-permute-start | bytes 196616 | tf_op jit(solution)/shard_map/ppermute | solution.py:330
  74.8 7.1 %collective-permute-start.24 = (bf16[256,128]{1,0:T(8,128)(2,1)S(1)}, bf16[256,128]{1,0:T(8,128)(2,1)S(1)}, u32[]{:S(2)}, u32[]{:S(2)}) collective-permute-start(bf16[256,128]{1,0:T(8,128)(2,1)S(1)} %get-tuple-element.74), channel_id=1, source_target_pairs={{0,5},{1,4},{2,7},{3,6},{4,1},{5,0},{6,3},{7,2},{8,13},{9,12},{10,... | collective-permute-start | bytes 196616 | tf_op jit(solution)/shard_map/ppermute | solution.py:330
  75.3 6.6 %collective-permute-start.21 = (bf16[256,128]{1,0:T(8,128)(2,1)S(1)}, bf16[256,128]{1,0:T(8,128)(2,1)S(1)}, u32[]{:S(2)}, u32[]{:S(2)}) collective-permute-start(bf16[256,128]{1,0:T(8,128)(2,1)S(1)} %get-tuple-element.71), channel_id=1, source_target_pairs={{0,2},{1,3},{2,0},{3,1},{4,6},{5,7},{6,4},{7,5},{8,10},{9,11},{10,... | collective-permute-start | bytes 196616 | tf_op jit(solution)/shard_map/ppermute | solution.py:330
  76.3 5.5 %collective-permute-start.22 = (bf16[256,128]{1,0:T(8,128)(2,1)S(1)}, bf16[256,128]{1,0:T(8,128)(2,1)S(1)}, u32[]{:S(2)}, u32[]{:S(2)}) collective-permute-start(bf16[256,128]{1,0:T(8,128)(2,1)S(1)} %get-tuple-element.72), channel_id=1, source_target_pairs={{0,3},{1,2},{2,1},{3,0},{4,7},{5,6},{6,5},{7,4},{8,11},{9,10},{10,... | collective-permute-start | bytes 196616 | tf_op jit(solution)/shard_map/ppermute | solution.py:330
  78.4 5.2 %collective-permute-start.25 = (bf16[256,128]{1,0:T(8,128)(2,1)S(1)}, bf16[256,128]{1,0:T(8,128)(2,1)S(1)}, u32[]{:S(2)}, u32[]{:S(2)}) collective-permute-start(bf16[256,128]{1,0:T(8,128)(2,1)S(1)} %get-tuple-element.75), channel_id=1, source_target_pairs={{0,6},{1,7},{2,4},{3,5},{4,2},{5,3},{6,0},{7,1},{8,14},{9,15},{10,... | collective-permute-start | bytes 196616 | tf_op jit(solution)/shard_map/ppermute | solution.py:330
  80.4 4.6 %collective-permute-start.26 = (bf16[256,128]{1,0:T(8,128)(2,1)S(1)}, bf16[256,128]{1,0:T(8,128)(2,1)S(1)}, u32[]{:S(2)}, u32[]{:S(2)}) collective-permute-start(bf16[256,128]{1,0:T(8,128)(2,1)S(1)} %get-tuple-element.76), channel_id=1, source_target_pairs={{0,7},{1,6},{2,5},{3,4},{4,3},{5,2},{6,1},{7,0},{8,15},{9,14},{10,... | collective-permute-start | bytes 196616 | tf_op jit(solution)/shard_map/ppermute | solution.py:330
  85.0 1.3 %copy-start.5 = (bf16[128,5120]{1,0:T(8,128)(2,1)S(1)}, bf16[128,5120]{1,0:T(8,128)(2,1)}, u32[]{:S(2)}) copy-start(bf16[128,5120]{1,0:T(8,128)(2,1)} %query_unpack.1.refs_8_) | copy-start | bytes 3932164

commit v2 on v1

--- a/solution.py
+++ b/solution.py
@@ -25,7 +25,7 @@
 QG_ROWS = X_AT + 48
 COUNT_COL = TREE_B
 OWN_COL = TREE_B + 1
-VMEM_LIMIT = 20 << 20
+VMEM_LIMIT = 14 << 20
 
 
 def dot_nt(a, b):
@@ -65,19 +65,11 @@
     )(*args, *after)
 
 
-def kv_pack_kernel(key_in, value_in, lists_in, kept, given, rows, key, value, lists, arrived):
-    copies = [
-        pltpu.make_async_copy(source, target, arrived.at[i])
-        for i, (source, target) in enumerate(((lists_in, lists), (key_in, key), (value_in, value)))
-    ]
-    for copy in copies:
-        copy.start()
+def list_row(lists, rows):
     position, parity = lax.axis_index("blk"), lax.axis_index("head")
     me = lax.rem(position, KVH)
     first = (position - me) * 2
     rows[...] = jnp.full(rows.shape, -1.0, F32)
-    for copy in copies:
-        copy.wait()
     rows[:2, :TREE_B] = lists[...].astype(F32)
     row = jnp.where(parity == 0, rows[0:1, :], rows[1:2, :])
     seen = row >= 0
@@ -86,21 +78,49 @@
     row = jnp.where(seen, row - first.astype(F32), -1.0)
     row = jnp.where(lane == COUNT_COL, count, row)
     row = jnp.where(lane == OWN_COL, (2 * me + parity).astype(F32), row)
-    tile = jnp.broadcast_to(row, (KV_ROWS - LIST_AT, HD)).astype(BF16)
+    return me, jnp.broadcast_to(row, (KV_ROWS - LIST_AT, HD)).astype(BF16)
+
+
+def kv_pack_kernel(key_in, value_in, lists_in, given, rows, key, value, lists, arrived):
+    copies = [
+        pltpu.make_async_copy(source, target, arrived.at[i])
+        for i, (source, target) in enumerate(((lists_in, lists), (key_in, key), (value_in, value)))
+    ]
+    for copy in copies:
+        copy.start()
+    for copy in copies:
+        copy.wait()
+    me, tile = list_row(lists, rows)
     for i, chip in enumerate(CHIPS):
-        for k, target in ((chip, kept), (chip + 1, given)):
-            columns = pl.ds(pl.multiple_of((me ^ k) * HD, HD), HD)
-            target[i, :BLOCK, :] = key[:, columns]
-            target[i, BLOCK:LIST_AT, :] = value[:, columns]
-            target[i, LIST_AT:, :] = tile
+        columns = pl.ds(pl.multiple_of((me ^ (chip + 1)) * HD, HD), HD)
+        given[i, :BLOCK, :] = key[:, columns]
+        given[i, BLOCK:LIST_AT, :] = value[:, columns]
+        given[i, LIST_AT:, :] = tile
 
 
 def kv_pack(key_act, value_act, kv_lists):
-    outs = [((len(CHIPS), KV_ROWS, HD), BF16)] * 2
+    outs = [((len(CHIPS), KV_ROWS, HD), BF16)]
     args = (key_act, value_act, kv_lists)
     scratch = [pltpu.VMEM((8, HD), F32), *(pltpu.VMEM(arg.shape, arg.dtype) for arg in args), pltpu.SemaphoreType.DMA((3,))]
     specs = [pl.BlockSpec(memory_space=pl.ANY)] * 3
-    return call(kv_pack_kernel, "kv_pack", specs, outs, scratch, 1, args, limit=60 << 20)
+    return call(kv_pack_kernel, "kv_pack", specs, outs, scratch, 1, args, limit=60 << 20)[0]
+
+
+def kv_pair_kernel(key, value, lists, theirs, *rest):
+    pairs, rows = rest[:-1], rest[-1]
+    me, tile = list_row(lists, rows)
+    for i, (chip, pair) in enumerate(zip(CHIPS, pairs)):
+        columns = pl.ds(pl.multiple_of((me ^ chip) * HD, HD), HD)
+        pair[0, :BLOCK, :] = key[:, columns]
+        pair[0, BLOCK:LIST_AT, :] = value[:, columns]
+        pair[0, LIST_AT:, :] = tile
+        pair[1] = theirs[i]
+
+
+def kv_pair(key_act, value_act, kv_lists, theirs):
+    outs = [((2, KV_ROWS, HD), BF16)] * len(CHIPS)
+    args = (key_act, value_act, kv_lists, theirs)
+    return call(kv_pair_kernel, "kv_pair", in_vmem(4), outs, [pltpu.VMEM((8, HD), F32)], 0.5, args)
 
 
 def pair_up_kernel(mine, theirs, *pairs):
@@ -122,13 +142,14 @@
     return call(pass_on_kernel, "pass_on", in_vmem(1), [(array.shape, array.dtype)], [], 0.2, (array,), after)[0]
 
 
-def kv_sum_kernel(mine, theirs, *sums):
-    for i, ref in enumerate(sums):
-        ref[...] = (mine[i] + theirs[i].astype(F32)).astype(BF16)
+def kv_sum_kernel(mine, theirs, kept, given):
+    for i in range(mine.shape[0]):
+        target = given if i % 2 else kept
+        target[i // 2] = (mine[i] + theirs[i].astype(F32)).astype(BF16)
 
 
 def kv_sum(mine, theirs):
-    outs = [(mine.shape[1:], BF16)] * mine.shape[0]
+    outs = [((mine.shape[0] // 2, *mine.shape[1:]), BF16)] * 2
     return call(kv_sum_kernel, "kv_sum", in_vmem(2), outs, [], 0.5, (mine, theirs))
 
 
@@ -165,7 +186,7 @@
 
 def attend_kernel(ks, kind, *refs):
     refs = list(refs)
-    opens, closes = kind == "first", kind == "last"
+    opens, joins, closes = kind == "first", kind in ("join", "last"), kind == "last"
     lists = refs.pop(0)
     messages = []
     while len(messages) < len(ks):
@@ -175,16 +196,17 @@
         kv_own, kv_other = [refs.pop(0) for _ in CHIPS], [refs.pop(0) for _ in CHIPS]
     else:
         keys, keys_t, values, sums_in = (refs.pop(0) for _ in range(4))
-    if closes:
+    if joins:
         earlier = refs.pop(0)
         backs = [refs.pop(0) for _ in ks]
         for n, back in enumerate(backs):
             back[0] = earlier[n]
         query_grads = [back.at[1] for back in backs]
-        mine, others = [refs.pop(0) for _ in range(2)], [refs.pop(0) for _ in range(2)]
     else:
         back = refs.pop(0)
         query_grads = [back.at[n] for n in range(len(ks))]
+    if closes:
+        mine, others = [refs.pop(0) for _ in BACK_HALVES], [refs.pop(0) for _ in BACK_HALVES]
     if opens:
         keys, keys_t, values = (refs.pop(0) for _ in range(3))
     sums = refs.pop(0)
@@ -276,14 +298,16 @@
     blocks = 2 * KVH + 1
     sums = ((blocks, 2 * BLOCK, HD), F32)
     scratch = []
+    if kind in ("join", "last"):
+        outs = [((2, Q_ROWS, HD), BF16)] * len(ks)
+    else:
+        outs = [((len(ks), Q_ROWS, HD), BF16)]
+    if kind == "first":
+        outs += [((blocks, BLOCK, HD), BF16)] * 3
     if kind == "last":
-        outs = [((2, Q_ROWS, HD), BF16)] * len(ks)
         outs += [((KVH // 2, 2 * BLOCK, HD), kind) for kind in (F32, F32, BF16, BF16)]
         scratch = [pltpu.VMEM(*sums)]
     else:
-        outs = [((len(ks), Q_ROWS, HD), BF16)]
-        if kind == "first":
-            outs += [((blocks, BLOCK, HD), BF16)] * 3
         outs += [sums]
     scratch += [pltpu.VMEM((HD, Q_ROWS), F32), pltpu.VMEM((2 * BLOCK, Q_ROWS), BF16), pltpu.VMEM((2 * BLOCK, Q_ROWS), BF16)]
     specs = [pl.BlockSpec(memory_space=pltpu.SMEM)] + in_vmem(len(messages) + len(state))
@@ -299,7 +323,8 @@
 
 
 def query_unpack_kernel(*refs):
-    backs, theirs, query_grad = refs[: len(CHIPS)], refs[len(CHIPS)], refs[len(CHIPS) + 1]
+    backs, theirs, query_grad, done = refs[: len(CHIPS)], *refs[len(CHIPS) :]
+    done[...] = jnp.zeros(done.shape, F32)
     me = lax.rem(lax.axis_index("blk"), KVH)
     for i, chip in enumerate(CHIPS):
         for k, ref, n in ((chip, backs[i], 0), (chip + 1, theirs, i)):
@@ -309,14 +334,16 @@
 
 
 def kv_unpack_kernel(*refs):
-    key_grad, value_grad = refs[KVH:]
+    key_grad, value_grad = refs[len(CHIPS) :]
     me = lax.rem(lax.axis_index("blk"), KVH)
-    for k in range(KVH):
-        columns = pl.ds(pl.multiple_of((me ^ k) * HD, HD), HD)
-        key_grad[:, columns] = refs[k][:BLOCK, :]
-        value_grad[:, columns] = refs[k][BLOCK:, :]
-
-
+    for i, chip in enumerate(CHIPS):
+        for n in range(2):
+            columns = pl.ds(pl.multiple_of((me ^ (chip + n)) * HD, HD), HD)
+            key_grad[:, columns] = refs[i][n, :BLOCK, :]
+            value_grad[:, columns] = refs[i][n, BLOCK:, :]
+
+
+CHIPS = (0, 2, 4, 6)
 CHIPS = (0, 2, 4, 6)
 VISITS = (("first", (0, 1)), ("more", (6, 7)), ("more", (2, 4)), ("last", (3, 5)))
 EXPECTED = (0.5, 0.5, 0.5, 6)
@@ -332,21 +359,20 @@
     def swapped(array):
         return lax.ppermute(array, "head", [(0, 1), (1, 0)])
 
-    kept, given = kv_pack(key_act, value_act, kv_lists)
-    beside = exchanged(given, 1)
-    paired = pair_up(kept, beside)
+    given = kv_pack(key_act, value_act, kv_lists)
+    paired = kv_pair(key_act, value_act, kv_lists, exchanged(given, 1))
     kv_own = [paired[0], *(exchanged(part, chip) for part, chip in zip(paired[1:], CHIPS[1:]))]
     kv_other = [swapped(part) for part in kv_own]
     lists = jnp.concatenate([part[:, LIST_AT, : OWN_COL + 1] for part in kv_own]).astype(jnp.int32)
 
     qg = (query_act, grad_out, attn_out, log_sum.T)
-    own, far, given = qg_pack(((0,), (6,), (1, 7)), *qg, (beside,))
-    near = exchanged(given, 1)
-    far = pair_up(far, near[1:], (*kv_own[1:], kv_other[0]))[0]
-    here = {0: (own, near[:1]), 1: (exchanged(far, 6),)}
-    sent = dict(zip((2, 4, 3, 5), qg_pack(((2,), (4,), (3,), (5,)), *qg, (far,))))
-    here[2] = tuple(exchanged(sent[k], k) for k in (2, 4))
-    here[3] = tuple(exchanged(sent[k], k) for k in (3, 5))
+    own, far, given = qg_pack(((0,), (6,), (1, 7)), *qg, (paired[1],))
+    beside = exchanged(given, 1)
+    far = pair_up(far, beside[1:], (*kv_own[1:], kv_other[0]))[0]
+    here = [[own, beside[:1]], [exchanged(far, 6)]]
+    for ks, after in (((2, 4), kv_other[2]), ((3, 5), kv_other[3])):
+        sent = qg_pack([(k,) for k in ks], *qg, (after,))
+        here.append([exchanged(message, k) for k, message in zip(ks, sent)])
 
     state, grads = (*kv_own, *kv_other), []
     for i, (kind, ks) in enumerate(VISITS):
@@ -357,19 +383,22 @@
         state = tuple(results[1:]) if kind == "first" else (*state[:3], results[-1])
     far_back = exchanged(grads[1], 6)
     backs = [exchanged(results[0], 2), exchanged(results[1], 4), far_back]
-    mine, others = results[2:4], results[4:6]
-    theirs = [swapped(pass_on(others[0], (far_back,))), swapped(others[1])]
-    kv_back = {}
-    for half, own, other in zip(BACK_HALVES, mine, theirs):
-        for k, part in zip(half, kv_sum(own, other)):
-            kv_back[k] = exchanged(part, k) if k else part
+    others = (pass_on(results[4], (far_back,)), results[5])
+    theirs = [swapped(other) for other in others]
+    sums = [kv_sum(mine, other) for mine, other in zip(results[2:4], theirs)]
+    kv_back, order = {}, [theirs[1]]
+    for half, (kept, given) in zip(BACK_HALVES, sums):
+        paired = pair_up(kept, exchanged(given, 1), order[:1])
+        order.append(paired[0])
+        kv_back.update((chip, exchanged(pair, chip) if chip else pair) for chip, pair in zip(half[::2], paired))
     outs = [((4, Q_ROWS, HD), BF16)]
-    given = call(query_relay_kernel, "query_relay", in_vmem(4), outs, [], 0.5, (grads[0], *backs), theirs)[0]
+    given = call(query_relay_kernel, "query_relay", in_vmem(4), outs, [], 0.5, (grads[0], *backs), order[1:2])[0]
     args = (grads[0], *backs, exchanged(given, 1))
-    grad_query = call(query_unpack_kernel, "query_unpack", in_vmem(5), [((BLOCK, QH * HD), BF16)], [], 1, args)
-    args = tuple(kv_back[k] for k in range(KVH))
-    grad_kv = call(kv_unpack_kernel, "kv_unpack", in_vmem(KVH), [((BLOCK, KVH * HD), BF16)] * 2, [], 1, args, grad_query)
-    return (*grad_query, *grad_kv)
+    outs = [((BLOCK, QH * HD), BF16), ((8, HD), F32)]
+    grad_query, done = call(query_unpack_kernel, "query_unpack", in_vmem(5), outs, [], 1, args)
+    outs = [((BLOCK, KVH * HD), BF16)] * 2
+    grad_key, grad_value = call(kv_unpack_kernel, "kv_unpack", in_vmem(4), outs, [], 1, [kv_back[chip] for chip in CHIPS], (done,))
+    return grad_query, grad_key, grad_value
 
 
 def passed_along(array, axis, by):

time: 87.3 us -> 83.6 us (0.958); the launches traced: 87.3 us -> 84.5 us
  Pallas kernels: 27.2 us -> 31.2 us
  waiting for transfers between devices: 30.8 us -> 27.3 us
  local copies, waits for them, and re-layouts: 2.73 us -> 0.12 us
    pallas_call x15 -> x18, Pallas kernels: 27.2 us -> 31.2 us  [call(): pl.pallas_call(body, name=name, in_specs=[*in_specs, *[pl.BlockSpec(memor...]
    unnamed x18, local copies, waits for them, and re-layouts: 2.67 us -> 0.05 us
    ppermute x6, waiting for transfers between devices: 14.2 us -> 12.4 us  [swapped(): return lax.ppermute(array, 'head', [(0, 1), (1, 0)])]
    ppermute x21 -> x19, waiting for transfers between devices: 16.7 us -> 15 us  [exchanged(): return lax.ppermute(array, 'blk', [(i, i ^ k) for i in range(size)])]
    ppermute x21 -> x19, starting transfers between devices: 18.2 us -> 17.3 us  [exchanged(): return lax.ppermute(array, 'blk', [(i, i ^ k) for i in range(size)])]
  transfers between devices with their start and end apart: 27 -> 25, of which waited for: 14 -> 13; matrix products, arithmetic and copies ran while one was open for 0% -> 0% of each run, Pallas kernels for 27% -> 32%
where the time goes in v2:
time: 83.6 us; the launch traced here: 84.5 us
  Pallas kernels  31.2 us (37%)
  waiting for transfers between devices  27.3 us (33%)
  starting transfers between devices  24.8 us (30%)
  between operations  0.95 us (1%)
    pallas_call x18, Pallas kernels, call(): pl.pallas_call(body, name=name, in_specs=[*in_specs, *[pl.BlockSpec(memor...  31.2 us
    ppermute x19, starting transfers between devices, exchanged(): return lax.ppermute(array, 'blk', [(i, i ^ k) for i in range(size)])  17.3 us
    ppermute x19, waiting for transfers between devices, exchanged(): return lax.ppermute(array, 'blk', [(i, i ^ k) for i in range(size)])  15 us
    ppermute x6, waiting for transfers between devices, swapped(): return lax.ppermute(array, 'head', [(0, 1), (1, 0)])  12.4 us
    ppermute x6, starting transfers between devices, swapped(): return lax.ppermute(array, 'head', [(0, 1), (1, 0)])  7.48 us
  transfers between devices with their start and end apart: 25, of which 13 were waited for; matrix products, arithmetic and copies ran while one was open for 0% of the time, Pallas kernels for 32%

profile of v2, /device:TPU:0, one launch (start us, length us, event | category | flops | bytes accessed | tf_op | source)
XLA Modules:
  0.0 84.5 jit_solution(3383224834510215514)
XLA Ops:
  0.7 2.1 %kv_pack.1 = bf16[4,272,128]{2,1,0:T(8,128)(2,1)} custom-call(bf16[128,1024]{1,0:T(8,128)(2,1)} %refs_0_.6, bf16[128,1024]{1,0:T(8,128)(2,1)} %refs_1_.6, s32[2,32]{1,0:T(2,128)} %refs_2_.6), custom_call_target="tpu_custom_call" | custom-call | flops 1000000000 | bytes 3000000 | tf_op jit(solution)/shard_map/kv_pack/pallas_call | solution.py:56
  2.8 0.5 collective-permute-start
  3.3 1.4 %collective-permute-done.refs_3_ = bf16[4,272,128]{2,1,0:T(8,128)(2,1)S(1)} collective-permute-done((bf16[4,272,128]{2,1,0:T(8,128)(2,1)}, bf16[4,272,128]{2,1,0:T(8,128)(2,1)S(1)}, u32[]{:S(2)}, u32[]{:S(2)}) %collective-permute-start) | collective-permute-done | bytes 278560 | tf_op jit(solution)/shard_map/ppermute | solution.py:357
  4.7 0.1 kv_pair.1
  4.9 0.7 qg_pack.3
  5.6 0.4 collective-permute-start.4
  6.0 2.7 %collective-permute-start.1 = (bf16[2,272,128]{2,1,0:T(8,128)(2,1)S(1)}, bf16[2,272,128]{2,1,0:T(8,128)(2,1)S(1)}, u32[]{:S(2)}, u32[]{:S(2)}) collective-permute-start(bf16[2,272,128]{2,1,0:T(8,128)(2,1)S(1)} %get-tuple-element.42.refs_4_), channel_id=1, source_target_pairs={{0,2},{1,3},{2,0},{3,1},{4,6},{5,7},{6,4},{7,5},{8,10},{9,11},{10,... | collective-permute-start | bytes 417800 | tf_op jit(solution)/shard_map/ppermute | solution.py:357
  8.7 1.6 %collective-permute-start.2 = (bf16[2,272,128]{2,1,0:T(8,128)(2,1)S(1)}, bf16[2,272,128]{2,1,0:T(8,128)(2,1)S(1)}, u32[]{:S(2)}, u32[]{:S(2)}) collective-permute-start(bf16[2,272,128]{2,1,0:T(8,128)(2,1)S(1)} %get-tuple-element.43), channel_id=1, source_target_pairs={{0,4},{1,5},{2,6},{3,7},{4,0},{5,1},{6,2},{7,3},{8,12},{9,13},{10,... | collective-permute-start | bytes 417800 | tf_op jit(solution)/shard_map/ppermute | solution.py:357
  10.3 1.9 %collective-permute-start.5 = (bf16[2,272,128]{2,1,0:T(8,128)(2,1)S(1)}, bf16[2,272,128]{2,1,0:T(8,128)(2,1)S(1)}, u32[]{:S(2)}, u32[]{:S(2)}) collective-permute-start(bf16[2,272,128]{2,1,0:T(8,128)(2,1)S(1)} %get-tuple-element.41.refs_3_), channel_id=1, source_target_pairs={{0,16},{16,0},{1,17},{17,1},{2,18},{18,2},{3,19},{19,3},{4,20},{20... | collective-permute-start | bytes 417800 | tf_op jit(solution)/shard_map/ppermute | solution.py:360
  12.2 0.7 collective-permute-done.1.refs_4_.refs_2_
  12.9 2.3 %collective-permute-done.2.refs_5_.refs_3_ = bf16[2,272,128]{2,1,0:T(8,128)(2,1)S(1)} collective-permute-done((bf16[2,272,128]{2,1,0:T(8,128)(2,1)S(1)}, bf16[2,272,128]{2,1,0:T(8,128)(2,1)S(1)}, u32[]{:S(2)}, u32[]{:S(2)}) %collective-permute-start.2) | collective-permute-done | bytes 139296 | tf_op jit(solution)/shard_map/ppermute | solution.py:357
  15.2 1.9 %collective-permute-done.3.refs_6_.refs_4_ = bf16[2,272,128]{2,1,0:T(8,128)(2,1)S(1)} collective-permute-done((bf16[2,272,128]{2,1,0:T(8,128)(2,1)S(1)}, bf16[2,272,128]{2,1,0:T(8,128)(2,1)S(1)}, u32[]{:S(2)}, u32[]{:S(2)}) %collective-permute-start.3) | collective-permute-done | bytes 139296 | tf_op jit(solution)/shard_map/ppermute | solution.py:357
  17.1 2.8 %collective-permute-start.13 = (bf16[2,1328,128]{2,1,0:T(8,128)(2,1)S(1)}, bf16[2,1328,128]{2,1,0:T(8,128)(2,1)S(1)}, u32[]{:S(2)}, u32[]{:S(2)}) collective-permute-start(bf16[2,1328,128]{2,1,0:T(8,128)(2,1)S(1)} %pair_up.3), channel_id=1, source_target_pairs={{0,6},{1,7},{2,4},{3,5},{4,2},{5,3},{6,0},{7,1},{8,14},{9,15},{10,... | collective-permute-start | bytes 2039816 | tf_op jit(solution)/shard_map/ppermute | solution.py:357
  19.9 1.5 %collective-permute-start.7 = (bf16[2,272,128]{2,1,0:T(8,128)(2,1)S(1)}, bf16[2,272,128]{2,1,0:T(8,128)(2,1)S(1)}, u32[]{:S(2)}, u32[]{:S(2)}) collective-permute-start(bf16[2,272,128]{2,1,0:T(8,128)(2,1)S(1)} %collective-permute-done.2.refs_5_.refs_3_), channel_id=1, source_target_pairs={{0,16},{16,0},{1,17},{17,1},{2,18},{18,2},{3,19},{19,3},{4,20},{20... | collective-permute-start | bytes 417800 | tf_op jit(solution)/shard_map/ppermute | solution.py:360
  21.4 0.5 collective-permute-start.8
  21.9 1.5 %collective-permute-start.6 = (bf16[2,272,128]{2,1,0:T(8,128)(2,1)S(1)}, bf16[2,272,128]{2,1,0:T(8,128)(2,1)S(1)}, u32[]{:S(2)}, u32[]{:S(2)}) collective-permute-start(bf16[2,272,128]{2,1,0:T(8,128)(2,1)S(1)} %collective-permute-done.1.refs_4_.refs_2_), channel_id=1, source_target_pairs={{0,16},{16,0},{1,17},{17,1},{2,18},{18,2},{3,19},{19,3},{4,20},{20... | collective-permute-start | bytes 417800 | tf_op jit(solution)/shard_map/ppermute | solution.py:360
  23.4 3.1 %collective-permute-done.7.refs_9_.refs_4_ = bf16[2,272,128]{2,1,0:T(8,128)(2,1)S(1)} collective-permute-done((bf16[2,272,128]{2,1,0:T(8,128)(2,1)S(1)}, bf16[2,272,128]{2,1,0:T(8,128)(2,1)S(1)}, u32[]{:S(2)}, u32[]{:S(2)}) %collective-permute-start.7) | collective-permute-done | bytes 139296 | tf_op jit(solution)/shard_map/ppermute | solution.py:360
  26.5 0.4 qg_pack.5
  26.9 0.5 collective-permute-start.11
  27.5 0.3 collective-permute-start.12
  27.7 1.2 %collective-permute-done.8.refs_10_.refs_4_ = bf16[2,272,128]{2,1,0:T(8,128)(2,1)S(1)} collective-permute-done((bf16[2,272,128]{2,1,0:T(8,128)(2,1)S(1)}, bf16[2,272,128]{2,1,0:T(8,128)(2,1)S(1)}, u32[]{:S(2)}, u32[]{:S(2)}) %collective-permute-start.8) | collective-permute-done | bytes 139296 | tf_op jit(solution)/shard_map/ppermute | solution.py:360
  28.9 0.4 qg_pack.4
  29.4 1.1 %collective-permute-done.6.refs_8_ = bf16[2,272,128]{2,1,0:T(8,128)(2,1)S(1)} collective-permute-done((bf16[2,272,128]{2,1,0:T(8,128)(2,1)S(1)}, bf16[2,272,128]{2,1,0:T(8,128)(2,1)S(1)}, u32[]{:S(2)}, u32[]{:S(2)}) %collective-permute-start.6) | collective-permute-done | bytes 139296 | tf_op jit(solution)/shard_map/ppermute | solution.py:360
  30.4 0.7 collective-permute-start.9
  31.3 2.8 %attend_0.1 = (bf16[2,640,128]{2,1,0:T(8,128)(2,1)S(1)}, bf16[17,128,128]{2,1,0:T(8,128)(2,1)S(1)}, bf16[17,128,128]{2,1,0:T(8,128)(2,1)S(1)}, bf16[17,128,128]{2,1,0:T(8,128)(2,1)S(1)}, f32[17,256,128]{2,1,0:T(8,128)S(1)}) custom-call(s32[8,34]{1,0:T(8,128)S(1)} %maximum_convert_fusion.refs_0_, bf16[1,1328,128]{2,1,0:T(8,128)(2,1)S(1)} %get-tuple-element.45.refs_1_, ...), custom_call_target="tpu_custom_call" | custom-call | flops 500000000 | bytes 1500000 | tf_op jit(solution)/shard_map/attend_0/pallas_call | solution.py:56
  34.1 2.3 %collective-permute-done.13.refs_1_ = bf16[2,1328,128]{2,1,0:T(8,128)(2,1)S(1)} collective-permute-done((bf16[2,1328,128]{2,1,0:T(8,128)(2,1)S(1)}, bf16[2,1328,128]{2,1,0:T(8,128)(2,1)S(1)}, u32[]{:S(2)}, u32[]{:S(2)}) %collective-permute-start.13) | collective-permute-done | bytes 679968 | tf_op jit(solution)/shard_map/ppermute | solution.py:357
  36.3 9.5 %attend_1.1 = (bf16[2,640,128]{2,1,0:T(8,128)(2,1)S(1)}, f32[17,256,128]{2,1,0:T(8,128)S(1)}) custom-call(s32[8,34]{1,0:T(8,128)S(1)} %maximum_convert_fusion.refs_0_, bf16[2,1328,128]{2,1,0:T(8,128)(2,1)S(1)} %collective-permute-done.13.refs_1_, bf16[17,128,128]{2,1,0:T(8,128)(2,1)S(1)} %get-tuple-element.50.refs_2_.refs_3_, ...), custom_call_target="tpu_custom_call" | custom-call | flops 500000000 | bytes 1500000 | tf_op jit(solution)/shard_map/attend_1/pallas_call | solution.py:56
  45.8 0.1 collective-permute-start.16
  45.9 5.6 %attend_2.1 = (bf16[2,640,128]{2,1,0:T(8,128)(2,1)S(1)}, f32[17,256,128]{2,1,0:T(8,128)S(1)}) custom-call(s32[8,34]{1,0:T(8,128)S(1)} %maximum_convert_fusion.refs_0_, bf16[1,1328,128]{2,1,0:T(8,128)(2,1)S(1)} %collective-permute-done.11.refs_1_, bf16[1,1328,128]{2,1,0:T(8,128)(2,1)S(1)} %collective-permute-done.12.refs_2_, ...), custom_call_target="tpu_custom_call" | custom-call | flops 500000000 | bytes 1500000 | tf_op jit(solution)/shard_map/attend_2/pallas_call | solution.py:56
  51.6 7.0 %attend_3.1 = (bf16[2,640,128]{2,1,0:T(8,128)(2,1)S(1)}, bf16[2,640,128]{2,1,0:T(8,128)(2,1)S(1)}, f32[4,256,128]{2,1,0:T(8,128)S(1)}, f32[4,256,128]{2,1,0:T(8,...) custom-call(s32[8,34]{1,0:T(8,128)S(1)} %maximum_convert_fusion.refs_0_, ...), custom_call_target="tpu_custom_call" | custom-call | flops 6000000000 | bytes 18000000 | tf_op jit(solution)/shard_map/attend_3/pallas_call | solution.py:56
  58.6 1.7 %collective-permute-start.17 = (bf16[4,256,128]{2,1,0:T(8,128)(2,1)S(1)}, bf16[4,256,128]{2,1,0:T(8,128)(2,1)S(1)}, u32[]{:S(2)}, u32[]{:S(2)}) collective-permute-start(bf16[4,256,128]{2,1,0:T(8,128)(2,1)S(1)} %pass_on.1), channel_id=1, source_target_pairs={{0,16},{16,0},{1,17},{17,1},{2,18},{18,2},{3,19},{19,3},{4,20},{20... | collective-permute-start | bytes 786440 | tf_op jit(solution)/shard_map/ppermute | solution.py:360
  60.3 0.6 collective-permute-start.14
  60.9 2.9 %collective-permute-start.15 = (bf16[2,640,128]{2,1,0:T(8,128)(2,1)S(1)}, bf16[2,640,128]{2,1,0:T(8,128)(2,1)S(1)}, u32[]{:S(2)}, u32[]{:S(2)}) collective-permute-start(bf16[2,640,128]{2,1,0:T(8,128)(2,1)S(1)} %get-tuple-element.61), channel_id=1, source_target_pairs={{0,4},{1,5},{2,6},{3,7},{4,0},{5,1},{6,2},{7,3},{8,12},{9,13},{10,... | collective-permute-start | bytes 983048 | tf_op jit(solution)/shard_map/ppermute | solution.py:357
  63.8 0.4 collective-permute-start.19
  64.2 3.7 %collective-permute-done.17.refs_1_ = bf16[4,256,128]{2,1,0:T(8,128)(2,1)S(1)} collective-permute-done((bf16[4,256,128]{2,1,0:T(8,128)(2,1)S(1)}, bf16[4,256,128]{2,1,0:T(8,128)(2,1)S(1)}, u32[]{:S(2)}, u32[]{:S(2)}) %collective-permute-start.17) | collective-permute-done | bytes 262176 | tf_op jit(solution)/shard_map/ppermute | solution.py:360
  67.9 0.1 kv_sum.2
  68.0 0.1 collective-permute-start.18
  68.1 3.3 %collective-permute-done.19.refs_2_.refs_1_ = bf16[4,256,128]{2,1,0:T(8,128)(2,1)S(1)} collective-permute-done((bf16[4,256,128]{2,1,0:T(8,128)(2,1)S(1)}, bf16[4,256,128]{2,1,0:T(8,128)(2,1)S(1)}, u32[]{:S(2)}, u32[]{:S(2)}) %collective-permute-start.19) | collective-permute-done | bytes 262176 | tf_op jit(solution)/shard_map/ppermute | solution.py:360
  71.4 0.1 collective-permute-start.20
  71.6 0.6 collective-permute-start.21
  72.1 1.7 %collective-permute-done.21.refs_1_ = bf16[2,256,128]{2,1,0:T(8,128)(2,1)S(1)} collective-permute-done((bf16[2,256,128]{2,1,0:T(8,128)(2,1)S(1)}, bf16[2,256,128]{2,1,0:T(8,128)(2,1)S(1)}, u32[]{:S(2)}, u32[]{:S(2)}) %collective-permute-start.21) | collective-permute-done | bytes 131104 | tf_op jit(solution)/shard_map/ppermute | solution.py:357
  73.8 1.6 %collective-permute-start.23 = (bf16[2,256,128]{2,1,0:T(8,128)(2,1)S(1)}, bf16[2,256,128]{2,1,0:T(8,128)(2,1)S(1)}, u32[]{:S(2)}, u32[]{:S(2)}) collective-permute-start(bf16[2,256,128]{2,1,0:T(8,128)(2,1)S(1)} %get-tuple-element.75), channel_id=1, source_target_pairs={{0,4},{1,5},{2,6},{3,7},{4,0},{5,1},{6,2},{7,3},{8,12},{9,13},{10,... | collective-permute-start | bytes 393224 | tf_op jit(solution)/shard_map/ppermute | solution.py:357
  75.4 0.9 %collective-permute-start.22 = (bf16[2,256,128]{2,1,0:T(8,128)(2,1)S(1)}, bf16[2,256,128]{2,1,0:T(8,128)(2,1)S(1)}, u32[]{:S(2)}, u32[]{:S(2)}) collective-permute-start(bf16[2,256,128]{2,1,0:T(8,128)(2,1)S(1)} %get-tuple-element.74), channel_id=1, source_target_pairs={{0,2},{1,3},{2,0},{3,1},{4,6},{5,7},{6,4},{7,5},{8,10},{9,11},{10,... | collective-permute-start | bytes 393224 | tf_op jit(solution)/shard_map/ppermute | solution.py:357
  76.4 1.0 %collective-permute-start.24 = (bf16[2,256,128]{2,1,0:T(8,128)(2,1)S(1)}, bf16[2,256,128]{2,1,0:T(8,128)(2,1)S(1)}, u32[]{:S(2)}, u32[]{:S(2)}) collective-permute-start(bf16[2,256,128]{2,1,0:T(8,128)(2,1)S(1)} %get-tuple-element.68.refs_4_), channel_id=1, source_target_pairs={{0,6},{1,7},{2,4},{3,5},{4,2},{5,3},{6,0},{7,1},{8,14},{9,15},{10,... | collective-permute-start | bytes 393224 | tf_op jit(solution)/shard_map/ppermute | solution.py:357
  77.4 1.4 %query_unpack.1 = (bf16[128,5120]{1,0:T(8,128)(2,1)}, f32[8,128]{1,0:T(8,128)S(1)}) custom-call(bf16[2,640,128]{2,1,0:T(8,128)(2,1)S(1)} %get-tuple-element.47.refs_0_, bf16[2,640,128]{2,1,0:T(8,128)(2,1)S(1)} %collective-permute-done.14.refs_1_, bf16[2,640,128]{2,1,0:T(8,128)(2,1)S(1)} %collective-permute-done.15.refs_2_, ...), custom_call_target="tpu_custom_call" | custom-call | flops 1000000000 | bytes 3000000 | tf_op jit(solution)/shard_map/query_unpack/pallas_call | solution.py:56
  78.8 0.9 %collective-permute-done.23.refs_2_ = bf16[2,256,128]{2,1,0:T(8,128)(2,1)S(1)} collective-permute-done((bf16[2,256,128]{2,1,0:T(8,128)(2,1)S(1)}, bf16[2,256,128]{2,1,0:T(8,128)(2,1)S(1)}, u32[]{:S(2)}, u32[]{:S(2)}) %collective-permute-start.23) | collective-permute-done | bytes 131104 | tf_op jit(solution)/shard_map/ppermute | solution.py:357
  79.7 3.8 %collective-permute-done.22.refs_1_ = bf16[2,256,128]{2,1,0:T(8,128)(2,1)S(1)} collective-permute-done((bf16[2,256,128]{2,1,0:T(8,128)(2,1)S(1)}, bf16[2,256,128]{2,1,0:T(8,128)(2,1)S(1)}, u32[]{:S(2)}, u32[]{:S(2)}) %collective-permute-start.22) | collective-permute-done | bytes 131104 | tf_op jit(solution)/shard_map/ppermute | solution.py:357
  83.5 0.9 %kv_unpack.1 = (bf16[128,1024]{1,0:T(8,128)(2,1)}, bf16[128,1024]{1,0:T(8,128)(2,1)}) custom-call(bf16[2,256,128]{2,1,0:T(8,128)(2,1)S(1)} %get-tuple-element.73.refs_0_, bf16[2,256,128]{2,1,0:T(8,128)(2,1)S(1)} %collective-permute-done.22.refs_1_, bf16[2,256,128]{2,1,0:T(8,128)(2,1)S(1)} %collective-permute-done.23.refs_2_, ...), custom_call_target="tpu_custom_call" | custom-call | flops 1000000000 | bytes 3000000 | tf_op jit(solution)/shard_map/kv_unpack/pallas_call | solution.py:56
  (44 shorter events, 0.4 us)
Async XLA Ops:
  0.6 4.1 %copy-start.6 = (s32[2,32]{1,0:T(2,128)S(1)}, s32[2,32]{1,0:T(2,128)}, u32[]{:S(2)}) copy-start(s32[2,32]{1,0:T(2,128)} %refs_2_.6) | copy-start | bytes 772
  0.6 4.1 %copy-start.4 = (bf16[128,1024]{1,0:T(8,128)(2,1)S(1)}, bf16[128,1024]{1,0:T(8,128)(2,1)}, u32[]{:S(2)}) copy-start(bf16[128,1024]{1,0:T(8,128)(2,1)} %refs_0_.6) | copy-start | bytes 786436
  0.7 4.0 %copy-start.5 = (bf16[128,1024]{1,0:T(8,128)(2,1)S(1)}, bf16[128,1024]{1,0:T(8,128)(2,1)}, u32[]{:S(2)}) copy-start(bf16[128,1024]{1,0:T(8,128)(2,1)} %refs_1_.6) | copy-start | bytes 786436
  0.7 4.2 %copy-start.1 = (bf16[128,5120]{1,0:T(8,128)(2,1)S(1)}, bf16[128,5120]{1,0:T(8,128)(2,1)}, u32[]{:S(2)}) copy-start(bf16[128,5120]{1,0:T(8,128)(2,1)} %refs_1_.9) | copy-start | bytes 3932164
  0.7 4.2 %copy-start.2 = (bf16[128,5120]{1,0:T(8,128)(2,1)S(1)}, bf16[128,5120]{1,0:T(8,128)(2,1)}, u32[]{:S(2)}) copy-start(bf16[128,5120]{1,0:T(8,128)(2,1)} %refs_2_.9) | copy-start | bytes 3932164
  2.7 2.1 %copy-start = (bf16[128,5120]{1,0:T(8,128)(2,1)S(1)}, bf16[128,5120]{1,0:T(8,128)(2,1)}, u32[]{:S(2)}) copy-start(bf16[128,5120]{1,0:T(8,128)(2,1)} %refs_0_.9) | copy-start | bytes 3932164
  2.8 2.1 %copy-start.3 = (f32[128,40]{0,1:T(8,128)S(1)}, f32[128,40]{0,1:T(8,128)}, u32[]{:S(2)}) copy-start(f32[128,40]{0,1:T(8,128)} %param.12) | copy-start | bytes 61444
  2.8 1.9 %collective-permute-start = (bf16[4,272,128]{2,1,0:T(8,128)(2,1)}, bf16[4,272,128]{2,1,0:T(8,128)(2,1)S(1)}, u32[]{:S(2)}, u32[]{:S(2)}) collective-permute-start(bf16[4,272,128]{2,1,0:T(8,128)(2,1)} %kv_pack.1), channel_id=1, source_target_pairs={{0,1},{1,0},{2,3},{3,2},{4,5},{5,4},{6,7},{7,6},{8,9},{9,8},{10,11... | collective-permute-start | bytes 835592 | tf_op jit(solution)/shard_map/ppermute | solution.py:357
  5.6 6.6 %collective-permute-start.4 = (bf16[2,1328,128]{2,1,0:T(8,128)(2,1)S(1)}, bf16[2,1328,128]{2,1,0:T(8,128)(2,1)S(1)}, u32[]{:S(2)}, u32[]{:S(2)}) collective-permute-start(bf16[2,1328,128]{2,1,0:T(8,128)(2,1)S(1)} %get-tuple-element.46), channel_id=1, source_target_pairs={{0,1},{1,0},{2,3},{3,2},{4,5},{5,4},{6,7},{7,6},{8,9},{9,8},{10,11... | collective-permute-start | bytes 2039816 | tf_op jit(solution)/shard_map/ppermute | solution.py:357
  6.0 6.9 %collective-permute-start.1 = (bf16[2,272,128]{2,1,0:T(8,128)(2,1)S(1)}, bf16[2,272,128]{2,1,0:T(8,128)(2,1)S(1)}, u32[]{:S(2)}, u32[]{:S(2)}) collective-permute-start(bf16[2,272,128]{2,1,0:T(8,128)(2,1)S(1)} %get-tuple-element.42.refs_4_), channel_id=1, source_target_pairs={{0,2},{1,3},{2,0},{3,1},{4,6},{5,7},{6,4},{7,5},{8,10},{9,11},{10,... | collective-permute-start | bytes 417800 | tf_op jit(solution)/shard_map/ppermute | solution.py:357
  8.7 6.5 %collective-permute-start.2 = (bf16[2,272,128]{2,1,0:T(8,128)(2,1)S(1)}, bf16[2,272,128]{2,1,0:T(8,128)(2,1)S(1)}, u32[]{:S(2)}, u32[]{:S(2)}) collective-permute-start(bf16[2,272,128]{2,1,0:T(8,128)(2,1)S(1)} %get-tuple-element.43), channel_id=1, source_target_pairs={{0,4},{1,5},{2,6},{3,7},{4,0},{5,1},{6,2},{7,3},{8,12},{9,13},{10,... | collective-permute-start | bytes 417800 | tf_op jit(solution)/shard_map/ppermute | solution.py:357
  10.3 6.8 %collective-permute-start.3 = (bf16[2,272,128]{2,1,0:T(8,128)(2,1)S(1)}, bf16[2,272,128]{2,1,0:T(8,128)(2,1)S(1)}, u32[]{:S(2)}, u32[]{:S(2)}) collective-permute-start(bf16[2,272,128]{2,1,0:T(8,128)(2,1)S(1)} %get-tuple-element.44), channel_id=1, source_target_pairs={{0,6},{1,7},{2,4},{3,5},{4,2},{5,3},{6,0},{7,1},{8,14},{9,15},{10,... | collective-permute-start | bytes 417800 | tf_op jit(solution)/shard_map/ppermute | solution.py:357
  10.3 6.8 %collective-permute-start.5 = (bf16[2,272,128]{2,1,0:T(8,128)(2,1)S(1)}, bf16[2,272,128]{2,1,0:T(8,128)(2,1)S(1)}, u32[]{:S(2)}, u32[]{:S(2)}) collective-permute-start(bf16[2,272,128]{2,1,0:T(8,128)(2,1)S(1)} %get-tuple-element.41.refs_3_), channel_id=1, source_target_pairs={{0,16},{16,0},{1,17},{17,1},{2,18},{18,2},{3,19},{19,3},{4,20},{20... | collective-permute-start | bytes 417800 | tf_op jit(solution)/shard_map/ppermute | solution.py:360
  17.1 19.2 %collective-permute-start.13 = (bf16[2,1328,128]{2,1,0:T(8,128)(2,1)S(1)}, bf16[2,1328,128]{2,1,0:T(8,128)(2,1)S(1)}, u32[]{:S(2)}, u32[]{:S(2)}) collective-permute-start(bf16[2,1328,128]{2,1,0:T(8,128)(2,1)S(1)} %pair_up.3), channel_id=1, source_target_pairs={{0,6},{1,7},{2,4},{3,5},{4,2},{5,3},{6,0},{7,1},{8,14},{9,15},{10,... | collective-permute-start | bytes 2039816 | tf_op jit(solution)/shard_map/ppermute | solution.py:357
  19.9 6.6 %collective-permute-start.7 = (bf16[2,272,128]{2,1,0:T(8,128)(2,1)S(1)}, bf16[2,272,128]{2,1,0:T(8,128)(2,1)S(1)}, u32[]{:S(2)}, u32[]{:S(2)}) collective-permute-start(bf16[2,272,128]{2,1,0:T(8,128)(2,1)S(1)} %collective-permute-done.2.refs_5_.refs_3_), channel_id=1, source_target_pairs={{0,16},{16,0},{1,17},{17,1},{2,18},{18,2},{3,19},{19,3},{4,20},{20... | collective-permute-start | bytes 417800 | tf_op jit(solution)/shard_map/ppermute | solution.py:360
  21.4 7.5 %collective-permute-start.8 = (bf16[2,272,128]{2,1,0:T(8,128)(2,1)S(1)}, bf16[2,272,128]{2,1,0:T(8,128)(2,1)S(1)}, u32[]{:S(2)}, u32[]{:S(2)}) collective-permute-start(bf16[2,272,128]{2,1,0:T(8,128)(2,1)S(1)} %collective-permute-done.3.refs_6_.refs_4_), channel_id=1, source_target_pairs={{0,16},{16,0},{1,17},{17,1},{2,18},{18,2},{3,19},{19,3},{4,20},{20... | collective-permute-start | bytes 417800 | tf_op jit(solution)/shard_map/ppermute | solution.py:360
  21.9 8.5 %collective-permute-start.6 = (bf16[2,272,128]{2,1,0:T(8,128)(2,1)S(1)}, bf16[2,272,128]{2,1,0:T(8,128)(2,1)S(1)}, u32[]{:S(2)}, u32[]{:S(2)}) collective-permute-start(bf16[2,272,128]{2,1,0:T(8,128)(2,1)S(1)} %collective-permute-done.1.refs_4_.refs_2_), channel_id=1, source_target_pairs={{0,16},{16,0},{1,17},{17,1},{2,18},{18,2},{3,19},{19,3},{4,20},{20... | collective-permute-start | bytes 417800 | tf_op jit(solution)/shard_map/ppermute | solution.py:360
  26.9 19.0 %collective-permute-start.11 = (bf16[1,1328,128]{2,1,0:T(8,128)(2,1)S(1)}, bf16[1,1328,128]{2,1,0:T(8,128)(2,1)S(1)}, u32[]{:S(2)}, u32[]{:S(2)}) collective-permute-start(bf16[1,1328,128]{2,1,0:T(8,128)(2,1)S(1)} %get-tuple-element.53), channel_id=1, source_target_pairs={{0,2},{1,3},{2,0},{3,1},{4,6},{5,7},{6,4},{7,5},{8,10},{9,11},{10,... | collective-permute-start | bytes 1019912 | tf_op jit(solution)/shard_map/ppermute | solution.py:357
  27.5 18.5 %collective-permute-start.12 = (bf16[1,1328,128]{2,1,0:T(8,128)(2,1)S(1)}, bf16[1,1328,128]{2,1,0:T(8,128)(2,1)S(1)}, u32[]{:S(2)}, u32[]{:S(2)}) collective-permute-start(bf16[1,1328,128]{2,1,0:T(8,128)(2,1)S(1)} %get-tuple-element.54), channel_id=1, source_target_pairs={{0,4},{1,5},{2,6},{3,7},{4,0},{5,1},{6,2},{7,3},{8,12},{9,13},{10,... | collective-permute-start | bytes 1019912 | tf_op jit(solution)/shard_map/ppermute | solution.py:357
  29.3 22.2 %collective-permute-start.10 = (bf16[1,1328,128]{2,1,0:T(8,128)(2,1)S(1)}, bf16[1,1328,128]{2,1,0:T(8,128)(2,1)S(1)}, u32[]{:S(2)}, u32[]{:S(2)}) collective-permute-start(bf16[1,1328,128]{2,1,0:T(8,128)(2,1)S(1)} %get-tuple-element.49), channel_id=1, source_target_pairs={{0,5},{1,4},{2,7},{3,6},{4,1},{5,0},{6,3},{7,2},{8,13},{9,12},{10,... | collective-permute-start | bytes 1019912 | tf_op jit(solution)/shard_map/ppermute | solution.py:357
  30.4 21.1 %collective-permute-start.9 = (bf16[1,1328,128]{2,1,0:T(8,128)(2,1)S(1)}, bf16[1,1328,128]{2,1,0:T(8,128)(2,1)S(1)}, u32[]{:S(2)}, u32[]{:S(2)}) collective-permute-start(bf16[1,1328,128]{2,1,0:T(8,128)(2,1)S(1)} %get-tuple-element.48), channel_id=1, source_target_pairs={{0,3},{1,2},{2,1},{3,0},{4,7},{5,6},{6,5},{7,4},{8,11},{9,10},{10,... | collective-permute-start | bytes 1019912 | tf_op jit(solution)/shard_map/ppermute | solution.py:357
  45.8 12.7 %collective-permute-start.16 = (bf16[2,640,128]{2,1,0:T(8,128)(2,1)S(1)}, bf16[2,640,128]{2,1,0:T(8,128)(2,1)S(1)}, u32[]{:S(2)}, u32[]{:S(2)}) collective-permute-start(bf16[2,640,128]{2,1,0:T(8,128)(2,1)S(1)} %get-tuple-element.62), channel_id=1, source_target_pairs={{0,6},{1,7},{2,4},{3,5},{4,2},{5,3},{6,0},{7,1},{8,14},{9,15},{10,... | collective-permute-start | bytes 983048 | tf_op jit(solution)/shard_map/ppermute | solution.py:357
  58.6 9.3 %collective-permute-start.17 = (bf16[4,256,128]{2,1,0:T(8,128)(2,1)S(1)}, bf16[4,256,128]{2,1,0:T(8,128)(2,1)S(1)}, u32[]{:S(2)}, u32[]{:S(2)}) collective-permute-start(bf16[4,256,128]{2,1,0:T(8,128)(2,1)S(1)} %pass_on.1), channel_id=1, source_target_pairs={{0,16},{16,0},{1,17},{17,1},{2,18},{18,2},{3,19},{19,3},{4,20},{20... | collective-permute-start | bytes 786440 | tf_op jit(solution)/shard_map/ppermute | solution.py:360
  60.3 11.0 %collective-permute-start.14 = (bf16[2,640,128]{2,1,0:T(8,128)(2,1)S(1)}, bf16[2,640,128]{2,1,0:T(8,128)(2,1)S(1)}, u32[]{:S(2)}, u32[]{:S(2)}) collective-permute-start(bf16[2,640,128]{2,1,0:T(8,128)(2,1)S(1)} %get-tuple-element.60), channel_id=1, source_target_pairs={{0,2},{1,3},{2,0},{3,1},{4,6},{5,7},{6,4},{7,5},{8,10},{9,11},{10,... | collective-permute-start | bytes 983048 | tf_op jit(solution)/shard_map/ppermute | solution.py:357
  60.9 10.5 %collective-permute-start.15 = (bf16[2,640,128]{2,1,0:T(8,128)(2,1)S(1)}, bf16[2,640,128]{2,1,0:T(8,128)(2,1)S(1)}, u32[]{:S(2)}, u32[]{:S(2)}) collective-permute-start(bf16[2,640,128]{2,1,0:T(8,128)(2,1)S(1)} %get-tuple-element.61), channel_id=1, source_target_pairs={{0,4},{1,5},{2,6},{3,7},{4,0},{5,1},{6,2},{7,3},{8,12},{9,13},{10,... | collective-permute-start | bytes 983048 | tf_op jit(solution)/shard_map/ppermute | solution.py:357
  63.8 7.5 %collective-permute-start.19 = (bf16[4,256,128]{2,1,0:T(8,128)(2,1)S(1)}, bf16[4,256,128]{2,1,0:T(8,128)(2,1)S(1)}, u32[]{:S(2)}, u32[]{:S(2)}) collective-permute-start(bf16[4,256,128]{2,1,0:T(8,128)(2,1)S(1)} %get-tuple-element.67), channel_id=1, source_target_pairs={{0,16},{16,0},{1,17},{17,1},{2,18},{18,2},{3,19},{19,3},{4,20},{20... | collective-permute-start | bytes 786440 | tf_op jit(solution)/shard_map/ppermute | solution.py:360
  68.0 3.4 %collective-permute-start.18 = (bf16[2,256,128]{2,1,0:T(8,128)(2,1)S(1)}, bf16[2,256,128]{2,1,0:T(8,128)(2,1)S(1)}, u32[]{:S(2)}, u32[]{:S(2)}) collective-permute-start(bf16[2,256,128]{2,1,0:T(8,128)(2,1)S(1)} %get-tuple-element.66), channel_id=1, source_target_pairs={{0,1},{1,0},{2,3},{3,2},{4,5},{5,4},{6,7},{7,6},{8,9},{9,8},{10,11... | collective-permute-start | bytes 393224 | tf_op jit(solution)/shard_map/ppermute | solution.py:357
  71.4 5.9 %collective-permute-start.20 = (bf16[4,640,128]{2,1,0:T(8,128)(2,1)S(1)}, bf16[4,640,128]{2,1,0:T(8,128)(2,1)S(1)}, u32[]{:S(2)}, u32[]{:S(2)}) collective-permute-start(bf16[4,640,128]{2,1,0:T(8,128)(2,1)S(1)} %query_relay.1), channel_id=1, source_target_pairs={{0,1},{1,0},{2,3},{3,2},{4,5},{5,4},{6,7},{7,6},{8,9},{9,8},{10,11... | collective-permute-start | bytes 1966088 | tf_op jit(solution)/shard_map/ppermute | solution.py:357
  71.6 2.2 %collective-permute-start.21 = (bf16[2,256,128]{2,1,0:T(8,128)(2,1)S(1)}, bf16[2,256,128]{2,1,0:T(8,128)(2,1)S(1)}, u32[]{:S(2)}, u32[]{:S(2)}) collective-permute-start(bf16[2,256,128]{2,1,0:T(8,128)(2,1)S(1)} %get-tuple-element.72), channel_id=1, source_target_pairs={{0,1},{1,0},{2,3},{3,2},{4,5},{5,4},{6,7},{7,6},{8,9},{9,8},{10,11... | collective-permute-start | bytes 393224 | tf_op jit(solution)/shard_map/ppermute | solution.py:357
  73.8 5.9 %collective-permute-start.23 = (bf16[2,256,128]{2,1,0:T(8,128)(2,1)S(1)}, bf16[2,256,128]{2,1,0:T(8,128)(2,1)S(1)}, u32[]{:S(2)}, u32[]{:S(2)}) collective-permute-start(bf16[2,256,128]{2,1,0:T(8,128)(2,1)S(1)} %get-tuple-element.75), channel_id=1, source_target_pairs={{0,4},{1,5},{2,6},{3,7},{4,0},{5,1},{6,2},{7,3},{8,12},{9,13},{10,... | collective-permute-start | bytes 393224 | tf_op jit(solution)/shard_map/ppermute | solution.py:357
  75.4 8.1 %collective-permute-start.22 = (bf16[2,256,128]{2,1,0:T(8,128)(2,1)S(1)}, bf16[2,256,128]{2,1,0:T(8,128)(2,1)S(1)}, u32[]{:S(2)}, u32[]{:S(2)}) collective-permute-start(bf16[2,256,128]{2,1,0:T(8,128)(2,1)S(1)} %get-tuple-element.74), channel_id=1, source_target_pairs={{0,2},{1,3},{2,0},{3,1},{4,6},{5,7},{6,4},{7,5},{8,10},{9,11},{10,... | collective-permute-start | bytes 393224 | tf_op jit(solution)/shard_map/ppermute | solution.py:357
  76.4 7.1 %collective-permute-start.24 = (bf16[2,256,128]{2,1,0:T(8,128)(2,1)S(1)}, bf16[2,256,128]{2,1,0:T(8,128)(2,1)S(1)}, u32[]{:S(2)}, u32[]{:S(2)}) collective-permute-start(bf16[2,256,128]{2,1,0:T(8,128)(2,1)S(1)} %get-tuple-element.68.refs_4_), channel_id=1, source_target_pairs={{0,6},{1,7},{2,4},{3,5},{4,2},{5,3},{6,0},{7,1},{8,14},{9,15},{10,... | collective-permute-start | bytes 393224 | tf_op jit(solution)/shard_map/ppermute | solution.py:357

commit v3 on v2

--- a/solution.py
+++ b/solution.py
@@ -142,15 +142,13 @@
     return call(pass_on_kernel, "pass_on", in_vmem(1), [(array.shape, array.dtype)], [], 0.2, (array,), after)[0]
 
 
-def kv_sum_kernel(mine, theirs, kept, given):
+def kv_sum_kernel(mine, theirs, total):
     for i in range(mine.shape[0]):
-        target = given if i % 2 else kept
-        target[i // 2] = (mine[i] + theirs[i].astype(F32)).astype(BF16)
+        total[i] = (mine[i] + theirs[i].astype(F32)).astype(BF16)
 
 
 def kv_sum(mine, theirs):
-    outs = [((mine.shape[0] // 2, *mine.shape[1:]), BF16)] * 2
-    return call(kv_sum_kernel, "kv_sum", in_vmem(2), outs, [], 0.5, (mine, theirs))
+    return call(kv_sum_kernel, "kv_sum", in_vmem(2), [(mine.shape, BF16)], [], 0.5, (mine, theirs))[0]
 
 
 def qg_pack_kernel(slots, query, grad, out, totals, *rest):
@@ -347,7 +345,7 @@
 CHIPS = (0, 2, 4, 6)
 VISITS = (("first", (0, 1)), ("more", (6, 7)), ("more", (2, 4)), ("last", (3, 5)))
 EXPECTED = (0.5, 0.5, 0.5, 6)
-BACK_HALVES = ((6, 7, 2, 3), (4, 5, 0, 1))
+BACK_HALVES = ((1, 3, 5, 7), CHIPS)
 
 
 def by_trees(query_act, key_act, value_act, attn_out, grad_out, log_sum, kv_lists):
@@ -366,8 +364,8 @@
     lists = jnp.concatenate([part[:, LIST_AT, : OWN_COL + 1] for part in kv_own]).astype(jnp.int32)
 
     qg = (query_act, grad_out, attn_out, log_sum.T)
-    own, far, given = qg_pack(((0,), (6,), (1, 7)), *qg, (paired[1],))
-    beside = exchanged(given, 1)
+    beside = exchanged(qg_pack(((1, 7),), *qg, (paired[1],))[0], 1)
+    own, far = qg_pack(((0,), (6,)), *qg, (kv_other[0],))
     far = pair_up(far, beside[1:], (*kv_own[1:], kv_other[0]))[0]
     here = [[own, beside[:1]], [exchanged(far, 6)]]
     for ks, after in (((2, 4), kv_other[2]), ((3, 5), kv_other[3])):
@@ -385,19 +383,16 @@
     backs = [exchanged(results[0], 2), exchanged(results[1], 4), far_back]
     others = (pass_on(results[4], (far_back,)), results[5])
     theirs = [swapped(other) for other in others]
-    sums = [kv_sum(mine, other) for mine, other in zip(results[2:4], theirs)]
-    kv_back, order = {}, [theirs[1]]
-    for half, (kept, given) in zip(BACK_HALVES, sums):
-        paired = pair_up(kept, exchanged(given, 1), order[:1])
-        order.append(paired[0])
-        kv_back.update((chip, exchanged(pair, chip) if chip else pair) for chip, pair in zip(half[::2], paired))
+    given, kept = [kv_sum(mine, other) for mine, other in zip(results[2:4], theirs)]
+    paired = pair_up(kept, exchanged(given, 1))
+    kv_back = [paired[0], *(exchanged(pair, chip) for pair, chip in zip(paired[1:], CHIPS[1:]))]
     outs = [((4, Q_ROWS, HD), BF16)]
-    given = call(query_relay_kernel, "query_relay", in_vmem(4), outs, [], 0.5, (grads[0], *backs), order[1:2])[0]
+    given = call(query_relay_kernel, "query_relay", in_vmem(4), outs, [], 0.5, (grads[0], *backs), paired[:1])[0]
     args = (grads[0], *backs, exchanged(given, 1))
     outs = [((BLOCK, QH * HD), BF16), ((8, HD), F32)]
     grad_query, done = call(query_unpack_kernel, "query_unpack", in_vmem(5), outs, [], 1, args)
     outs = [((BLOCK, KVH * HD), BF16)] * 2
-    grad_key, grad_value = call(kv_unpack_kernel, "kv_unpack", in_vmem(4), outs, [], 1, [kv_back[chip] for chip in CHIPS], (done,))
+    grad_key, grad_value = call(kv_unpack_kernel, "kv_unpack", in_vmem(4), outs, [], 1, kv_back, (done,))
     return grad_query, grad_key, grad_value
 
 

time: 83.6 us -> 82.5 us (0.987); the launches traced: 84.5 us -> 81.8 us
  Pallas kernels: 31.2 us -> 23.9 us
  waiting for transfers between devices: 27.3 us -> 33.9 us
  starting transfers between devices: 24.8 us -> 23 us
    pallas_call x18, Pallas kernels: 31.2 us -> 23.9 us  [call(): pl.pallas_call(body, name=name, in_specs=[*in_specs, *[pl.BlockSpec(memor...]
    ppermute x19 -> x18, waiting for transfers between devices: 15 us -> 18.9 us  [exchanged(): return lax.ppermute(array, 'blk', [(i, i ^ k) for i in range(size)])]
    ppermute x6, waiting for transfers between devices: 12.4 us -> 15 us  [swapped(): return lax.ppermute(array, 'head', [(0, 1), (1, 0)])]
    ppermute x19 -> x18, starting transfers between devices: 17.3 us -> 15.7 us  [exchanged(): return lax.ppermute(array, 'blk', [(i, i ^ k) for i in range(size)])]
  transfers between devices with their start and end apart: 25 -> 24, of which waited for: 13 -> 19; matrix products, arithmetic and copies ran while one was open for 0% -> 0% of each run, Pallas kernels for 32% -> 25%
where the time goes in v3:
time: 82.5 us; the launch traced here: 81.8 us
  waiting for transfers between devices  33.9 us (41%)
  Pallas kernels  23.9 us (29%)
  starting transfers between devices  23 us (28%)
  between operations  0.9 us (1%)
    pallas_call x18, Pallas kernels, call(): pl.pallas_call(body, name=name, in_specs=[*in_specs, *[pl.BlockSpec(memor...  23.9 us
    ppermute x18, waiting for transfers between devices, exchanged(): return lax.ppermute(array, 'blk', [(i, i ^ k) for i in range(size)])  18.9 us
    ppermute x18, starting transfers between devices, exchanged(): return lax.ppermute(array, 'blk', [(i, i ^ k) for i in range(size)])  15.7 us
    ppermute x6, waiting for transfers between devices, swapped(): return lax.ppermute(array, 'head', [(0, 1), (1, 0)])  15 us
    ppermute x6, starting transfers between devices, swapped(): return lax.ppermute(array, 'head', [(0, 1), (1, 0)])  7.29 us
  transfers between devices with their start and end apart: 24, of which 19 were waited for; matrix products, arithmetic and copies ran while one was open for 0% of the time, Pallas kernels for 25%

profile of v3, /device:TPU:0, one launch (start us, length us, event | category | flops | bytes accessed | tf_op | source)
XLA Modules:
  0.0 81.8 jit_solution(7333488045175056699)
XLA Ops:
  0.7 2.1 %kv_pack.1 = bf16[4,272,128]{2,1,0:T(8,128)(2,1)} custom-call(bf16[128,1024]{1,0:T(8,128)(2,1)} %refs_0_.7, bf16[128,1024]{1,0:T(8,128)(2,1)} %refs_1_.7, s32[2,32]{1,0:T(2,128)} %refs_2_.7), custom_call_target="tpu_custom_call" | custom-call | flops 1000000000 | bytes 3000000 | tf_op jit(solution)/shard_map/kv_pack/pallas_call | solution.py:56
  2.8 0.5 collective-permute-start
  3.3 1.4 %collective-permute-done.refs_3_ = bf16[4,272,128]{2,1,0:T(8,128)(2,1)S(1)} collective-permute-done((bf16[4,272,128]{2,1,0:T(8,128)(2,1)}, bf16[4,272,128]{2,1,0:T(8,128)(2,1)S(1)}, u32[]{:S(2)}, u32[]{:S(2)}) %collective-permute-start) | collective-permute-done | bytes 278560 | tf_op jit(solution)/shard_map/ppermute | solution.py:355
  4.9 0.4 qg_pack.5
  5.3 0.4 collective-permute-start.5
  5.7 2.6 %collective-permute-start.4 = (bf16[2,272,128]{2,1,0:T(8,128)(2,1)S(1)}, bf16[2,272,128]{2,1,0:T(8,128)(2,1)S(1)}, u32[]{:S(2)}, u32[]{:S(2)}) collective-permute-start(bf16[2,272,128]{2,1,0:T(8,128)(2,1)S(1)} %get-tuple-element.36.refs_3_), channel_id=1, source_target_pairs={{0,16},{16,0},{1,17},{17,1},{2,18},{18,2},{3,19},{19,3},{4,20},{20... | collective-permute-start | bytes 417800 | tf_op jit(solution)/shard_map/ppermute | solution.py:358
  8.3 1.5 %collective-permute-start.1 = (bf16[2,272,128]{2,1,0:T(8,128)(2,1)S(1)}, bf16[2,272,128]{2,1,0:T(8,128)(2,1)S(1)}, u32[]{:S(2)}, u32[]{:S(2)}) collective-permute-start(bf16[2,272,128]{2,1,0:T(8,128)(2,1)S(1)} %get-tuple-element.37.refs_4_), channel_id=1, source_target_pairs={{0,2},{1,3},{2,0},{3,1},{4,6},{5,7},{6,4},{7,5},{8,10},{9,11},{10,... | collective-permute-start | bytes 417800 | tf_op jit(solution)/shard_map/ppermute | solution.py:355
  9.9 1.6 %collective-permute-start.2 = (bf16[2,272,128]{2,1,0:T(8,128)(2,1)S(1)}, bf16[2,272,128]{2,1,0:T(8,128)(2,1)S(1)}, u32[]{:S(2)}, u32[]{:S(2)}) collective-permute-start(bf16[2,272,128]{2,1,0:T(8,128)(2,1)S(1)} %get-tuple-element.38), channel_id=1, source_target_pairs={{0,4},{1,5},{2,6},{3,7},{4,0},{5,1},{6,2},{7,3},{8,12},{9,13},{10,... | collective-permute-start | bytes 417800 | tf_op jit(solution)/shard_map/ppermute | solution.py:355
  11.4 0.4 collective-permute-start.3
  11.8 0.7 collective-permute-done.4.refs_4_.refs_7_.refs_5_
  12.5 0.4 qg_pack.4
  13.0 1.0 %collective-permute-done.1.refs_4_.refs_2_ = bf16[2,272,128]{2,1,0:T(8,128)(2,1)S(1)} collective-permute-done((bf16[2,272,128]{2,1,0:T(8,128)(2,1)S(1)}, bf16[2,272,128]{2,1,0:T(8,128)(2,1)S(1)}, u32[]{:S(2)}, u32[]{:S(2)}) %collective-permute-start.1) | collective-permute-done | bytes 139296 | tf_op jit(solution)/shard_map/ppermute | solution.py:355
  14.0 2.4 %collective-permute-done.2.refs_5_.refs_3_ = bf16[2,272,128]{2,1,0:T(8,128)(2,1)S(1)} collective-permute-done((bf16[2,272,128]{2,1,0:T(8,128)(2,1)S(1)}, bf16[2,272,128]{2,1,0:T(8,128)(2,1)S(1)}, u32[]{:S(2)}, u32[]{:S(2)}) %collective-permute-start.2) | collective-permute-done | bytes 139296 | tf_op jit(solution)/shard_map/ppermute | solution.py:355
  16.4 1.7 %collective-permute-done.3.refs_6_.refs_4_ = bf16[2,272,128]{2,1,0:T(8,128)(2,1)S(1)} collective-permute-done((bf16[2,272,128]{2,1,0:T(8,128)(2,1)S(1)}, bf16[2,272,128]{2,1,0:T(8,128)(2,1)S(1)}, u32[]{:S(2)}, u32[]{:S(2)}) %collective-permute-start.3) | collective-permute-done | bytes 139296 | tf_op jit(solution)/shard_map/ppermute | solution.py:355
  18.2 2.6 %collective-permute-start.13 = (bf16[2,1328,128]{2,1,0:T(8,128)(2,1)S(1)}, bf16[2,1328,128]{2,1,0:T(8,128)(2,1)S(1)}, u32[]{:S(2)}, u32[]{:S(2)}) collective-permute-start(bf16[2,1328,128]{2,1,0:T(8,128)(2,1)S(1)} %pair_up.2), channel_id=1, source_target_pairs={{0,6},{1,7},{2,4},{3,5},{4,2},{5,3},{6,0},{7,1},{8,14},{9,15},{10,... | collective-permute-start | bytes 2039816 | tf_op jit(solution)/shard_map/ppermute | solution.py:355
  20.8 0.5 collective-permute-start.7
  21.3 1.5 %collective-permute-start.8 = (bf16[2,272,128]{2,1,0:T(8,128)(2,1)S(1)}, bf16[2,272,128]{2,1,0:T(8,128)(2,1)S(1)}, u32[]{:S(2)}, u32[]{:S(2)}) collective-permute-start(bf16[2,272,128]{2,1,0:T(8,128)(2,1)S(1)} %collective-permute-done.3.refs_6_.refs_4_), channel_id=1, source_target_pairs={{0,16},{16,0},{1,17},{17,1},{2,18},{18,2},{3,19},{19,3},{4,20},{20... | collective-permute-start | bytes 417800 | tf_op jit(solution)/shard_map/ppermute | solution.py:358
  22.8 0.5 collective-permute-start.6
  23.4 4.0 %collective-permute-done.7.refs_9_.refs_4_ = bf16[2,272,128]{2,1,0:T(8,128)(2,1)S(1)} collective-permute-done((bf16[2,272,128]{2,1,0:T(8,128)(2,1)S(1)}, bf16[2,272,128]{2,1,0:T(8,128)(2,1)S(1)}, u32[]{:S(2)}, u32[]{:S(2)}) %collective-permute-start.7) | collective-permute-done | bytes 139296 | tf_op jit(solution)/shard_map/ppermute | solution.py:358
  27.4 0.4 qg_pack.7
  27.8 0.5 collective-permute-start.11
  28.4 0.5 collective-permute-start.12
  28.8 0.7 collective-permute-done.8.refs_10_.refs_4_
  29.5 0.4 qg_pack.6
  29.9 1.1 %collective-permute-done.6.refs_8_ = bf16[2,272,128]{2,1,0:T(8,128)(2,1)S(1)} collective-permute-done((bf16[2,272,128]{2,1,0:T(8,128)(2,1)S(1)}, bf16[2,272,128]{2,1,0:T(8,128)(2,1)S(1)}, u32[]{:S(2)}, u32[]{:S(2)}) %collective-permute-start.6) | collective-permute-done | bytes 139296 | tf_op jit(solution)/shard_map/ppermute | solution.py:358
  31.0 1.1 %collective-permute-start.9 = (bf16[1,1328,128]{2,1,0:T(8,128)(2,1)S(1)}, bf16[1,1328,128]{2,1,0:T(8,128)(2,1)S(1)}, u32[]{:S(2)}, u32[]{:S(2)}) collective-permute-start(bf16[1,1328,128]{2,1,0:T(8,128)(2,1)S(1)} %get-tuple-element.42), channel_id=1, source_target_pairs={{0,3},{1,2},{2,1},{3,0},{4,7},{5,6},{6,5},{7,4},{8,11},{9,10},{10,... | collective-permute-start | bytes 1019912 | tf_op jit(solution)/shard_map/ppermute | solution.py:355
  32.1 2.8 %attend_0.1 = (bf16[2,640,128]{2,1,0:T(8,128)(2,1)S(1)}, bf16[17,128,128]{2,1,0:T(8,128)(2,1)S(1)}, bf16[17,128,128]{2,1,0:T(8,128)(2,1)S(1)}, bf16[17,128,128]{2,1,0:T(8,128)(2,1)S(1)}, f32[17,256,128]{2,1,0:T(8,128)S(1)}) custom-call(s32[8,34]{1,0:T(8,128)S(1)} %maximum_convert_fusion.refs_0_, bf16[1,1328,128]{2,1,0:T(8,128)(2,1)S(1)} %get-tuple-element.40.refs_1_, ...), custom_call_target="tpu_custom_call" | custom-call | flops 500000000 | bytes 1500000 | tf_op jit(solution)/shard_map/attend_0/pallas_call | solution.py:56
  35.0 2.4 %collective-permute-done.13.refs_1_ = bf16[2,1328,128]{2,1,0:T(8,128)(2,1)S(1)} collective-permute-done((bf16[2,1328,128]{2,1,0:T(8,128)(2,1)S(1)}, bf16[2,1328,128]{2,1,0:T(8,128)(2,1)S(1)}, u32[]{:S(2)}, u32[]{:S(2)}) %collective-permute-start.13) | collective-permute-done | bytes 679968 | tf_op jit(solution)/shard_map/ppermute | solution.py:355
  37.4 5.0 %attend_1.1 = (bf16[2,640,128]{2,1,0:T(8,128)(2,1)S(1)}, f32[17,256,128]{2,1,0:T(8,128)S(1)}) custom-call(s32[8,34]{1,0:T(8,128)S(1)} %maximum_convert_fusion.refs_0_, bf16[2,1328,128]{2,1,0:T(8,128)(2,1)S(1)} %collective-permute-done.13.refs_1_, bf16[17,128,128]{2,1,0:T(8,128)(2,1)S(1)} %get-tuple-element.44.refs_2_.refs_3_, ...), custom_call_target="tpu_custom_call" | custom-call | flops 500000000 | bytes 1500000 | tf_op jit(solution)/shard_map/attend_1/pallas_call | solution.py:56
  42.7 0.4 collective-permute-done.11.refs_1_
  43.1 1.6 %collective-permute-done.12.refs_2_ = bf16[1,1328,128]{2,1,0:T(8,128)(2,1)S(1)} collective-permute-done((bf16[1,1328,128]{2,1,0:T(8,128)(2,1)S(1)}, bf16[1,1328,128]{2,1,0:T(8,128)(2,1)S(1)}, u32[]{:S(2)}, u32[]{:S(2)}) %collective-permute-start.12) | collective-permute-done | bytes 340000 | tf_op jit(solution)/shard_map/ppermute | solution.py:355
  44.8 4.5 %attend_2.1 = (bf16[2,640,128]{2,1,0:T(8,128)(2,1)S(1)}, f32[17,256,128]{2,1,0:T(8,128)S(1)}) custom-call(s32[8,34]{1,0:T(8,128)S(1)} %maximum_convert_fusion.refs_0_, bf16[1,1328,128]{2,1,0:T(8,128)(2,1)S(1)} %collective-permute-done.11.refs_1_, bf16[1,1328,128]{2,1,0:T(8,128)(2,1)S(1)} %collective-permute-done.12.refs_2_, ...), custom_call_target="tpu_custom_call" | custom-call | flops 500000000 | bytes 1500000 | tf_op jit(solution)/shard_map/attend_2/pallas_call | solution.py:56
  49.2 1.9 %collective-permute-done.10.refs_2_ = bf16[1,1328,128]{2,1,0:T(8,128)(2,1)S(1)} collective-permute-done((bf16[1,1328,128]{2,1,0:T(8,128)(2,1)S(1)}, bf16[1,1328,128]{2,1,0:T(8,128)(2,1)S(1)}, u32[]{:S(2)}, u32[]{:S(2)}) %collective-permute-start.10) | collective-permute-done | bytes 340000 | tf_op jit(solution)/shard_map/ppermute | solution.py:355
  51.1 0.6 collective-permute-done.9.refs_1_
  51.7 5.1 %attend_3.1 = (bf16[2,640,128]{2,1,0:T(8,128)(2,1)S(1)}, bf16[2,640,128]{2,1,0:T(8,128)(2,1)S(1)}, f32[4,256,128]{2,1,0:T(8,128)S(1)}, f32[4,256,128]{2,1,0:T(8,...) custom-call(s32[8,34]{1,0:T(8,128)S(1)} %maximum_convert_fusion.refs_0_, ...), custom_call_target="tpu_custom_call" | custom-call | flops 6000000000 | bytes 18000000 | tf_op jit(solution)/shard_map/attend_3/pallas_call | solution.py:56
  56.9 0.5 collective-permute-done.16.refs_1_.refs_3_
  57.6 1.9 %collective-permute-start.17 = (bf16[4,256,128]{2,1,0:T(8,128)(2,1)S(1)}, bf16[4,256,128]{2,1,0:T(8,128)(2,1)S(1)}, u32[]{:S(2)}, u32[]{:S(2)}) collective-permute-start(bf16[4,256,128]{2,1,0:T(8,128)(2,1)S(1)} %get-tuple-element.58), channel_id=1, source_target_pairs={{0,16},{16,0},{1,17},{17,1},{2,18},{18,2},{3,19},{19,3},{4,20},{20... | collective-permute-start | bytes 786440 | tf_op jit(solution)/shard_map/ppermute | solution.py:358
  59.5 1.1 %collective-permute-start.14 = (bf16[2,640,128]{2,1,0:T(8,128)(2,1)S(1)}, bf16[2,640,128]{2,1,0:T(8,128)(2,1)S(1)}, u32[]{:S(2)}, u32[]{:S(2)}) collective-permute-start(bf16[2,640,128]{2,1,0:T(8,128)(2,1)S(1)} %get-tuple-element.54), channel_id=1, source_target_pairs={{0,2},{1,3},{2,0},{3,1},{4,6},{5,7},{6,4},{7,5},{8,10},{9,11},{10,... | collective-permute-start | bytes 983048 | tf_op jit(solution)/shard_map/ppermute | solution.py:355
  60.5 1.6 %collective-permute-start.15 = (bf16[2,640,128]{2,1,0:T(8,128)(2,1)S(1)}, bf16[2,640,128]{2,1,0:T(8,128)(2,1)S(1)}, u32[]{:S(2)}, u32[]{:S(2)}) collective-permute-start(bf16[2,640,128]{2,1,0:T(8,128)(2,1)S(1)} %get-tuple-element.55), channel_id=1, source_target_pairs={{0,4},{1,5},{2,6},{3,7},{4,0},{5,1},{6,2},{7,3},{8,12},{9,13},{10,... | collective-permute-start | bytes 983048 | tf_op jit(solution)/shard_map/ppermute | solution.py:355
  62.1 4.6 %collective-permute-done.18.refs_1_ = bf16[4,256,128]{2,1,0:T(8,128)(2,1)S(1)} collective-permute-done((bf16[4,256,128]{2,1,0:T(8,128)(2,1)S(1)}, bf16[4,256,128]{2,1,0:T(8,128)(2,1)S(1)}, u32[]{:S(2)}, u32[]{:S(2)}) %collective-permute-start.18) | collective-permute-done | bytes 262176 | tf_op jit(solution)/shard_map/ppermute | solution.py:358
  66.8 3.8 %collective-permute-done.17.refs_1_ = bf16[4,256,128]{2,1,0:T(8,128)(2,1)S(1)} collective-permute-done((bf16[4,256,128]{2,1,0:T(8,128)(2,1)S(1)}, bf16[4,256,128]{2,1,0:T(8,128)(2,1)S(1)}, u32[]{:S(2)}, u32[]{:S(2)}) %collective-permute-start.17) | collective-permute-done | bytes 262176 | tf_op jit(solution)/shard_map/ppermute | solution.py:358
  71.0 2.7 %collective-permute-start.22 = (bf16[2,256,128]{2,1,0:T(8,128)(2,1)S(1)}, bf16[2,256,128]{2,1,0:T(8,128)(2,1)S(1)}, u32[]{:S(2)}, u32[]{:S(2)}) collective-permute-start(bf16[2,256,128]{2,1,0:T(8,128)(2,1)S(1)} %get-tuple-element.64), channel_id=1, source_target_pairs={{0,4},{1,5},{2,6},{3,7},{4,0},{5,1},{6,2},{7,3},{8,12},{9,13},{10,... | collective-permute-start | bytes 393224 | tf_op jit(solution)/shard_map/ppermute | solution.py:355
  73.8 0.7 collective-permute-start.23
  74.5 1.4 %query_unpack.1 = (bf16[128,5120]{1,0:T(8,128)(2,1)}, f32[8,128]{1,0:T(8,128)S(1)}) custom-call(bf16[2,640,128]{2,1,0:T(8,128)(2,1)S(1)} %get-tuple-element.41.refs_0_, bf16[2,640,128]{2,1,0:T(8,128)(2,1)S(1)} %collective-permute-done.14.refs_1_, bf16[2,640,128]{2,1,0:T(8,128)(2,1)S(1)} %collective-permute-done.15.refs_2_, ...), custom_call_target="tpu_custom_call" | custom-call | flops 1000000000 | bytes 3000000 | tf_op jit(solution)/shard_map/query_unpack/pallas_call | solution.py:56
  75.9 0.9 %collective-permute-done.21.refs_1_ = bf16[2,256,128]{2,1,0:T(8,128)(2,1)S(1)} collective-permute-done((bf16[2,256,128]{2,1,0:T(8,128)(2,1)S(1)}, bf16[2,256,128]{2,1,0:T(8,128)(2,1)S(1)}, u32[]{:S(2)}, u32[]{:S(2)}) %collective-permute-start.21) | collective-permute-done | bytes 131104 | tf_op jit(solution)/shard_map/ppermute | solution.py:355
  76.8 1.2 %collective-permute-done.22.refs_2_ = bf16[2,256,128]{2,1,0:T(8,128)(2,1)S(1)} collective-permute-done((bf16[2,256,128]{2,1,0:T(8,128)(2,1)S(1)}, bf16[2,256,128]{2,1,0:T(8,128)(2,1)S(1)}, u32[]{:S(2)}, u32[]{:S(2)}) %collective-permute-start.22) | collective-permute-done | bytes 131104 | tf_op jit(solution)/shard_map/ppermute | solution.py:355
  78.0 2.8 %collective-permute-done.23.refs_3_ = bf16[2,256,128]{2,1,0:T(8,128)(2,1)S(1)} collective-permute-done((bf16[2,256,128]{2,1,0:T(8,128)(2,1)S(1)}, bf16[2,256,128]{2,1,0:T(8,128)(2,1)S(1)}, u32[]{:S(2)}, u32[]{:S(2)}) %collective-permute-start.23) | collective-permute-done | bytes 131104 | tf_op jit(solution)/shard_map/ppermute | solution.py:355
  80.8 0.9 %kv_unpack.1 = (bf16[128,1024]{1,0:T(8,128)(2,1)}, bf16[128,1024]{1,0:T(8,128)(2,1)}) custom-call(bf16[2,256,128]{2,1,0:T(8,128)(2,1)S(1)} %get-tuple-element.61.refs_4_.refs_0_, bf16[2,256,128]{2,1,0:T(8,128)(2,1)S(1)} %collective-permute-done.21.refs_1_, bf16[2,256,128]{2,1,0:T(8,128)(2,1)S(1)} %collective-permute-done.22.refs_2_, ...), custom_call_target="tpu_custom_call" | custom-call | flops 1000000000 | bytes 3000000 | tf_op jit(solution)/shard_map/kv_unpack/pallas_call | solution.py:56
  (42 shorter events, 1.3 us)
Async XLA Ops:
  0.6 4.1 %copy-start.6 = (s32[2,32]{1,0:T(2,128)S(1)}, s32[2,32]{1,0:T(2,128)}, u32[]{:S(2)}) copy-start(s32[2,32]{1,0:T(2,128)} %refs_2_.7) | copy-start | bytes 772
  0.6 4.1 %copy-start.4 = (bf16[128,1024]{1,0:T(8,128)(2,1)S(1)}, bf16[128,1024]{1,0:T(8,128)(2,1)}, u32[]{:S(2)}) copy-start(bf16[128,1024]{1,0:T(8,128)(2,1)} %refs_0_.7) | copy-start | bytes 786436
  0.7 4.0 %copy-start.5 = (bf16[128,1024]{1,0:T(8,128)(2,1)S(1)}, bf16[128,1024]{1,0:T(8,128)(2,1)}, u32[]{:S(2)}) copy-start(bf16[128,1024]{1,0:T(8,128)(2,1)} %refs_1_.7) | copy-start | bytes 786436
  0.7 4.2 %copy-start.1 = (bf16[128,5120]{1,0:T(8,128)(2,1)S(1)}, bf16[128,5120]{1,0:T(8,128)(2,1)}, u32[]{:S(2)}) copy-start(bf16[128,5120]{1,0:T(8,128)(2,1)} %refs_1_.11) | copy-start | bytes 3932164
  0.7 4.2 %copy-start.2 = (bf16[128,5120]{1,0:T(8,128)(2,1)S(1)}, bf16[128,5120]{1,0:T(8,128)(2,1)}, u32[]{:S(2)}) copy-start(bf16[128,5120]{1,0:T(8,128)(2,1)} %refs_2_.11) | copy-start | bytes 3932164
  2.7 2.1 %copy-start = (bf16[128,5120]{1,0:T(8,128)(2,1)S(1)}, bf16[128,5120]{1,0:T(8,128)(2,1)}, u32[]{:S(2)}) copy-start(bf16[128,5120]{1,0:T(8,128)(2,1)} %refs_0_.11) | copy-start | bytes 3932164
  2.8 2.1 %copy-start.3 = (f32[128,40]{0,1:T(8,128)S(1)}, f32[128,40]{0,1:T(8,128)}, u32[]{:S(2)}) copy-start(f32[128,40]{0,1:T(8,128)} %param.12) | copy-start | bytes 61444
  2.8 1.9 %collective-permute-start = (bf16[4,272,128]{2,1,0:T(8,128)(2,1)}, bf16[4,272,128]{2,1,0:T(8,128)(2,1)S(1)}, u32[]{:S(2)}, u32[]{:S(2)}) collective-permute-start(bf16[4,272,128]{2,1,0:T(8,128)(2,1)} %kv_pack.1), channel_id=1, source_target_pairs={{0,1},{1,0},{2,3},{3,2},{4,5},{5,4},{6,7},{7,6},{8,9},{9,8},{10,11... | collective-permute-start | bytes 835592 | tf_op jit(solution)/shard_map/ppermute | solution.py:355
  5.3 7.6 %collective-permute-start.5 = (bf16[2,1328,128]{2,1,0:T(8,128)(2,1)S(1)}, bf16[2,1328,128]{2,1,0:T(8,128)(2,1)S(1)}, u32[]{:S(2)}, u32[]{:S(2)}) collective-permute-start(bf16[2,1328,128]{2,1,0:T(8,128)(2,1)S(1)} %qg_pack.5), channel_id=1, source_target_pairs={{0,1},{1,0},{2,3},{3,2},{4,5},{5,4},{6,7},{7,6},{8,9},{9,8},{10,11... | collective-permute-start | bytes 2039816 | tf_op jit(solution)/shard_map/ppermute | solution.py:355
  5.7 6.8 %collective-permute-start.4 = (bf16[2,272,128]{2,1,0:T(8,128)(2,1)S(1)}, bf16[2,272,128]{2,1,0:T(8,128)(2,1)S(1)}, u32[]{:S(2)}, u32[]{:S(2)}) collective-permute-start(bf16[2,272,128]{2,1,0:T(8,128)(2,1)S(1)} %get-tuple-element.36.refs_3_), channel_id=1, source_target_pairs={{0,16},{16,0},{1,17},{17,1},{2,18},{18,2},{3,19},{19,3},{4,20},{20... | collective-permute-start | bytes 417800 | tf_op jit(solution)/shard_map/ppermute | solution.py:358
  8.3 5.7 %collective-permute-start.1 = (bf16[2,272,128]{2,1,0:T(8,128)(2,1)S(1)}, bf16[2,272,128]{2,1,0:T(8,128)(2,1)S(1)}, u32[]{:S(2)}, u32[]{:S(2)}) collective-permute-start(bf16[2,272,128]{2,1,0:T(8,128)(2,1)S(1)} %get-tuple-element.37.refs_4_), channel_id=1, source_target_pairs={{0,2},{1,3},{2,0},{3,1},{4,6},{5,7},{6,4},{7,5},{8,10},{9,11},{10,... | collective-permute-start | bytes 417800 | tf_op jit(solution)/shard_map/ppermute | solution.py:355
  9.9 6.6 %collective-permute-start.2 = (bf16[2,272,128]{2,1,0:T(8,128)(2,1)S(1)}, bf16[2,272,128]{2,1,0:T(8,128)(2,1)S(1)}, u32[]{:S(2)}, u32[]{:S(2)}) collective-permute-start(bf16[2,272,128]{2,1,0:T(8,128)(2,1)S(1)} %get-tuple-element.38), channel_id=1, source_target_pairs={{0,4},{1,5},{2,6},{3,7},{4,0},{5,1},{6,2},{7,3},{8,12},{9,13},{10,... | collective-permute-start | bytes 417800 | tf_op jit(solution)/shard_map/ppermute | solution.py:355
  11.4 6.7 %collective-permute-start.3 = (bf16[2,272,128]{2,1,0:T(8,128)(2,1)S(1)}, bf16[2,272,128]{2,1,0:T(8,128)(2,1)S(1)}, u32[]{:S(2)}, u32[]{:S(2)}) collective-permute-start(bf16[2,272,128]{2,1,0:T(8,128)(2,1)S(1)} %get-tuple-element.39), channel_id=1, source_target_pairs={{0,6},{1,7},{2,4},{3,5},{4,2},{5,3},{6,0},{7,1},{8,14},{9,15},{10,... | collective-permute-start | bytes 417800 | tf_op jit(solution)/shard_map/ppermute | solution.py:355
  18.2 19.2 %collective-permute-start.13 = (bf16[2,1328,128]{2,1,0:T(8,128)(2,1)S(1)}, bf16[2,1328,128]{2,1,0:T(8,128)(2,1)S(1)}, u32[]{:S(2)}, u32[]{:S(2)}) collective-permute-start(bf16[2,1328,128]{2,1,0:T(8,128)(2,1)S(1)} %pair_up.2), channel_id=1, source_target_pairs={{0,6},{1,7},{2,4},{3,5},{4,2},{5,3},{6,0},{7,1},{8,14},{9,15},{10,... | collective-permute-start | bytes 2039816 | tf_op jit(solution)/shard_map/ppermute | solution.py:355
  20.8 6.6 %collective-permute-start.7 = (bf16[2,272,128]{2,1,0:T(8,128)(2,1)S(1)}, bf16[2,272,128]{2,1,0:T(8,128)(2,1)S(1)}, u32[]{:S(2)}, u32[]{:S(2)}) collective-permute-start(bf16[2,272,128]{2,1,0:T(8,128)(2,1)S(1)} %collective-permute-done.2.refs_5_.refs_3_), channel_id=1, source_target_pairs={{0,16},{16,0},{1,17},{17,1},{2,18},{18,2},{3,19},{19,3},{4,20},{20... | collective-permute-start | bytes 417800 | tf_op jit(solution)/shard_map/ppermute | solution.py:358
  21.3 8.2 %collective-permute-start.8 = (bf16[2,272,128]{2,1,0:T(8,128)(2,1)S(1)}, bf16[2,272,128]{2,1,0:T(8,128)(2,1)S(1)}, u32[]{:S(2)}, u32[]{:S(2)}) collective-permute-start(bf16[2,272,128]{2,1,0:T(8,128)(2,1)S(1)} %collective-permute-done.3.refs_6_.refs_4_), channel_id=1, source_target_pairs={{0,16},{16,0},{1,17},{17,1},{2,18},{18,2},{3,19},{19,3},{4,20},{20... | collective-permute-start | bytes 417800 | tf_op jit(solution)/shard_map/ppermute | solution.py:358
  22.8 8.2 %collective-permute-start.6 = (bf16[2,272,128]{2,1,0:T(8,128)(2,1)S(1)}, bf16[2,272,128]{2,1,0:T(8,128)(2,1)S(1)}, u32[]{:S(2)}, u32[]{:S(2)}) collective-permute-start(bf16[2,272,128]{2,1,0:T(8,128)(2,1)S(1)} %collective-permute-done.1.refs_4_.refs_2_), channel_id=1, source_target_pairs={{0,16},{16,0},{1,17},{17,1},{2,18},{18,2},{3,19},{19,3},{4,20},{20... | collective-permute-start | bytes 417800 | tf_op jit(solution)/shard_map/ppermute | solution.py:358
  27.8 15.3 %collective-permute-start.11 = (bf16[1,1328,128]{2,1,0:T(8,128)(2,1)S(1)}, bf16[1,1328,128]{2,1,0:T(8,128)(2,1)S(1)}, u32[]{:S(2)}, u32[]{:S(2)}) collective-permute-start(bf16[1,1328,128]{2,1,0:T(8,128)(2,1)S(1)} %get-tuple-element.47), channel_id=1, source_target_pairs={{0,2},{1,3},{2,0},{3,1},{4,6},{5,7},{6,4},{7,5},{8,10},{9,11},{10,... | collective-permute-start | bytes 1019912 | tf_op jit(solution)/shard_map/ppermute | solution.py:355
  28.4 16.4 %collective-permute-start.12 = (bf16[1,1328,128]{2,1,0:T(8,128)(2,1)S(1)}, bf16[1,1328,128]{2,1,0:T(8,128)(2,1)S(1)}, u32[]{:S(2)}, u32[]{:S(2)}) collective-permute-start(bf16[1,1328,128]{2,1,0:T(8,128)(2,1)S(1)} %get-tuple-element.48), channel_id=1, source_target_pairs={{0,4},{1,5},{2,6},{3,7},{4,0},{5,1},{6,2},{7,3},{8,12},{9,13},{10,... | collective-permute-start | bytes 1019912 | tf_op jit(solution)/shard_map/ppermute | solution.py:355
  29.9 21.2 %collective-permute-start.10 = (bf16[1,1328,128]{2,1,0:T(8,128)(2,1)S(1)}, bf16[1,1328,128]{2,1,0:T(8,128)(2,1)S(1)}, u32[]{:S(2)}, u32[]{:S(2)}) collective-permute-start(bf16[1,1328,128]{2,1,0:T(8,128)(2,1)S(1)} %get-tuple-element.43), channel_id=1, source_target_pairs={{0,5},{1,4},{2,7},{3,6},{4,1},{5,0},{6,3},{7,2},{8,13},{9,12},{10,... | collective-permute-start | bytes 1019912 | tf_op jit(solution)/shard_map/ppermute | solution.py:355
  31.0 20.7 %collective-permute-start.9 = (bf16[1,1328,128]{2,1,0:T(8,128)(2,1)S(1)}, bf16[1,1328,128]{2,1,0:T(8,128)(2,1)S(1)}, u32[]{:S(2)}, u32[]{:S(2)}) collective-permute-start(bf16[1,1328,128]{2,1,0:T(8,128)(2,1)S(1)} %get-tuple-element.42), channel_id=1, source_target_pairs={{0,3},{1,2},{2,1},{3,0},{4,7},{5,6},{6,5},{7,4},{8,11},{9,10},{10,... | collective-permute-start | bytes 1019912 | tf_op jit(solution)/shard_map/ppermute | solution.py:355
  42.4 15.0 %collective-permute-start.16 = (bf16[2,640,128]{2,1,0:T(8,128)(2,1)S(1)}, bf16[2,640,128]{2,1,0:T(8,128)(2,1)S(1)}, u32[]{:S(2)}, u32[]{:S(2)}) collective-permute-start(bf16[2,640,128]{2,1,0:T(8,128)(2,1)S(1)} %get-tuple-element.56), channel_id=1, source_target_pairs={{0,6},{1,7},{2,4},{3,5},{4,2},{5,3},{6,0},{7,1},{8,14},{9,15},{10,... | collective-permute-start | bytes 983048 | tf_op jit(solution)/shard_map/ppermute | solution.py:355
  57.4 9.3 %collective-permute-start.18 = (bf16[4,256,128]{2,1,0:T(8,128)(2,1)S(1)}, bf16[4,256,128]{2,1,0:T(8,128)(2,1)S(1)}, u32[]{:S(2)}, u32[]{:S(2)}) collective-permute-start(bf16[4,256,128]{2,1,0:T(8,128)(2,1)S(1)} %pass_on.1), channel_id=1, source_target_pairs={{0,16},{16,0},{1,17},{17,1},{2,18},{18,2},{3,19},{19,3},{4,20},{20... | collective-permute-start | bytes 786440 | tf_op jit(solution)/shard_map/ppermute | solution.py:358
  57.6 13.1 %collective-permute-start.17 = (bf16[4,256,128]{2,1,0:T(8,128)(2,1)S(1)}, bf16[4,256,128]{2,1,0:T(8,128)(2,1)S(1)}, u32[]{:S(2)}, u32[]{:S(2)}) collective-permute-start(bf16[4,256,128]{2,1,0:T(8,128)(2,1)S(1)} %get-tuple-element.58), channel_id=1, source_target_pairs={{0,16},{16,0},{1,17},{17,1},{2,18},{18,2},{3,19},{19,3},{4,20},{20... | collective-permute-start | bytes 786440 | tf_op jit(solution)/shard_map/ppermute | solution.py:358
  59.5 11.3 %collective-permute-start.14 = (bf16[2,640,128]{2,1,0:T(8,128)(2,1)S(1)}, bf16[2,640,128]{2,1,0:T(8,128)(2,1)S(1)}, u32[]{:S(2)}, u32[]{:S(2)}) collective-permute-start(bf16[2,640,128]{2,1,0:T(8,128)(2,1)S(1)} %get-tuple-element.54), channel_id=1, source_target_pairs={{0,2},{1,3},{2,0},{3,1},{4,6},{5,7},{6,4},{7,5},{8,10},{9,11},{10,... | collective-permute-start | bytes 983048 | tf_op jit(solution)/shard_map/ppermute | solution.py:355
  60.5 10.3 %collective-permute-start.15 = (bf16[2,640,128]{2,1,0:T(8,128)(2,1)S(1)}, bf16[2,640,128]{2,1,0:T(8,128)(2,1)S(1)}, u32[]{:S(2)}, u32[]{:S(2)}) collective-permute-start(bf16[2,640,128]{2,1,0:T(8,128)(2,1)S(1)} %get-tuple-element.55), channel_id=1, source_target_pairs={{0,4},{1,5},{2,6},{3,7},{4,0},{5,1},{6,2},{7,3},{8,12},{9,13},{10,... | collective-permute-start | bytes 983048 | tf_op jit(solution)/shard_map/ppermute | solution.py:355
  66.7 4.0 %collective-permute-start.19 = (bf16[4,256,128]{2,1,0:T(8,128)(2,1)S(1)}, bf16[4,256,128]{2,1,0:T(8,128)(2,1)S(1)}, u32[]{:S(2)}, u32[]{:S(2)}) collective-permute-start(bf16[4,256,128]{2,1,0:T(8,128)(2,1)S(1)} %kv_sum.3), channel_id=1, source_target_pairs={{0,1},{1,0},{2,3},{3,2},{4,5},{5,4},{6,7},{7,6},{8,9},{9,8},{10,11... | collective-permute-start | bytes 786440 | tf_op jit(solution)/shard_map/ppermute | solution.py:355
  70.9 3.6 %collective-permute-start.20 = (bf16[4,640,128]{2,1,0:T(8,128)(2,1)S(1)}, bf16[4,640,128]{2,1,0:T(8,128)(2,1)S(1)}, u32[]{:S(2)}, u32[]{:S(2)}) collective-permute-start(bf16[4,640,128]{2,1,0:T(8,128)(2,1)S(1)} %query_relay.1), channel_id=1, source_target_pairs={{0,1},{1,0},{2,3},{3,2},{4,5},{5,4},{6,7},{7,6},{8,9},{9,8},{10,11... | collective-permute-start | bytes 1966088 | tf_op jit(solution)/shard_map/ppermute | solution.py:355
  70.9 5.9 %collective-permute-start.21 = (bf16[2,256,128]{2,1,0:T(8,128)(2,1)S(1)}, bf16[2,256,128]{2,1,0:T(8,128)(2,1)S(1)}, u32[]{:S(2)}, u32[]{:S(2)}) collective-permute-start(bf16[2,256,128]{2,1,0:T(8,128)(2,1)S(1)} %get-tuple-element.63), channel_id=1, source_target_pairs={{0,2},{1,3},{2,0},{3,1},{4,6},{5,7},{6,4},{7,5},{8,10},{9,11},{10,... | collective-permute-start | bytes 393224 | tf_op jit(solution)/shard_map/ppermute | solution.py:355
  71.0 7.0 %collective-permute-start.22 = (bf16[2,256,128]{2,1,0:T(8,128)(2,1)S(1)}, bf16[2,256,128]{2,1,0:T(8,128)(2,1)S(1)}, u32[]{:S(2)}, u32[]{:S(2)}) collective-permute-start(bf16[2,256,128]{2,1,0:T(8,128)(2,1)S(1)} %get-tuple-element.64), channel_id=1, source_target_pairs={{0,4},{1,5},{2,6},{3,7},{4,0},{5,1},{6,2},{7,3},{8,12},{9,13},{10,... | collective-permute-start | bytes 393224 | tf_op jit(solution)/shard_map/ppermute | solution.py:355
  73.8 7.1 %collective-permute-start.23 = (bf16[2,256,128]{2,1,0:T(8,128)(2,1)S(1)}, bf16[2,256,128]{2,1,0:T(8,128)(2,1)S(1)}, u32[]{:S(2)}, u32[]{:S(2)}) collective-permute-start(bf16[2,256,128]{2,1,0:T(8,128)(2,1)S(1)} %get-tuple-element.65), channel_id=1, source_target_pairs={{0,6},{1,7},{2,4},{3,5},{4,2},{5,3},{6,0},{7,1},{8,14},{9,15},{10,... | collective-permute-start | bytes 393224 | tf_op jit(solution)/shard_map/ppermute | solution.py:355

commit v4 on v3

--- a/solution.py
+++ b/solution.py
@@ -334,11 +334,11 @@
 def kv_unpack_kernel(*refs):
     key_grad, value_grad = refs[len(CHIPS) :]
     me = lax.rem(lax.axis_index("blk"), KVH)
-    for i, chip in enumerate(CHIPS):
+    for chip, pair in zip(reversed(CHIPS), refs):
         for n in range(2):
             columns = pl.ds(pl.multiple_of((me ^ (chip + n)) * HD, HD), HD)
-            key_grad[:, columns] = refs[i][n, :BLOCK, :]
-            value_grad[:, columns] = refs[i][n, BLOCK:, :]
+            key_grad[:, columns] = pair[n, :BLOCK, :]
+            value_grad[:, columns] = pair[n, BLOCK:, :]
 
 
 CHIPS = (0, 2, 4, 6)
@@ -357,16 +357,20 @@
     def swapped(array):
         return lax.ppermute(array, "head", [(0, 1), (1, 0)])
 
+    def by_chip(pairs):
+        moved = {chip: exchanged(pair, chip) for chip, pair in reversed(list(zip(CHIPS, pairs))) if chip}
+        return [moved.get(chip, pair) for chip, pair in zip(CHIPS, pairs)]
+
     given = kv_pack(key_act, value_act, kv_lists)
     paired = kv_pair(key_act, value_act, kv_lists, exchanged(given, 1))
-    kv_own = [paired[0], *(exchanged(part, chip) for part, chip in zip(paired[1:], CHIPS[1:]))]
+    kv_own = by_chip(paired)
     kv_other = [swapped(part) for part in kv_own]
     lists = jnp.concatenate([part[:, LIST_AT, : OWN_COL + 1] for part in kv_own]).astype(jnp.int32)
 
     qg = (query_act, grad_out, attn_out, log_sum.T)
     beside = exchanged(qg_pack(((1, 7),), *qg, (paired[1],))[0], 1)
     own, far = qg_pack(((0,), (6,)), *qg, (kv_other[0],))
-    far = pair_up(far, beside[1:], (*kv_own[1:], kv_other[0]))[0]
+    far = pair_up(far, beside[1:], (*kv_own[:0:-1], kv_other[0]))[0]
     here = [[own, beside[:1]], [exchanged(far, 6)]]
     for ks, after in (((2, 4), kv_other[2]), ((3, 5), kv_other[3])):
         sent = qg_pack([(k,) for k in ks], *qg, (after,))
@@ -385,14 +389,14 @@
     theirs = [swapped(other) for other in others]
     given, kept = [kv_sum(mine, other) for mine, other in zip(results[2:4], theirs)]
     paired = pair_up(kept, exchanged(given, 1))
-    kv_back = [paired[0], *(exchanged(pair, chip) for pair, chip in zip(paired[1:], CHIPS[1:]))]
+    kv_back = by_chip(paired)
     outs = [((4, Q_ROWS, HD), BF16)]
     given = call(query_relay_kernel, "query_relay", in_vmem(4), outs, [], 0.5, (grads[0], *backs), paired[:1])[0]
     args = (grads[0], *backs, exchanged(given, 1))
     outs = [((BLOCK, QH * HD), BF16), ((8, HD), F32)]
     grad_query, done = call(query_unpack_kernel, "query_unpack", in_vmem(5), outs, [], 1, args)
     outs = [((BLOCK, KVH * HD), BF16)] * 2
-    grad_key, grad_value = call(kv_unpack_kernel, "kv_unpack", in_vmem(4), outs, [], 1, kv_back, (done,))
+    grad_key, grad_value = call(kv_unpack_kernel, "kv_unpack", in_vmem(4), outs, [], 1, kv_back[::-1], (done,))
     return grad_query, grad_key, grad_value
 
 

time: 82.5 us -> 81.6 us (0.989)
  waiting for transfers between devices: 33.9 us -> 32.9 us
  transfers between devices with their start and end apart: 24 -> 24, of which waited for: 19 -> 16; matrix products, arithmetic and copies ran while one was open for 0% -> 0% of each run, Pallas kernels for 25% -> 26%
where the time goes in v4:
time: 81.6 us; the launch traced here: 81.2 us
  waiting for transfers between devices  32.9 us (40%)
  Pallas kernels  24.4 us (30%)
  starting transfers between devices  22.9 us (28%)
  between operations  0.92 us (1%)
    pallas_call x18, Pallas kernels, call(): pl.pallas_call(body, name=name, in_specs=[*in_specs, *[pl.BlockSpec(memor...  24.4 us
    ppermute x18, waiting for transfers between devices, exchanged(): return lax.ppermute(array, 'blk', [(i, i ^ k) for i in range(size)])  18.5 us
    ppermute x18, starting transfers between devices, exchanged(): return lax.ppermute(array, 'blk', [(i, i ^ k) for i in range(size)])  15.6 us
    ppermute x6, waiting for transfers between devices, swapped(): return lax.ppermute(array, 'head', [(0, 1), (1, 0)])  14.4 us
    ppermute x6, starting transfers between devices, swapped(): return lax.ppermute(array, 'head', [(0, 1), (1, 0)])  7.29 us
  transfers between devices with their start and end apart: 24, of which 16 were waited for; matrix products, arithmetic and copies ran while one was open for 0% of the time, Pallas kernels for 26%

profile of v4, /device:TPU:0, one launch (start us, length us, event | category | flops | bytes accessed | tf_op | source)
XLA Modules:
  0.0 81.2 jit_solution(9864272332074790712)
XLA Ops:
  0.7 2.1 %kv_pack.1 = bf16[4,272,128]{2,1,0:T(8,128)(2,1)} custom-call(bf16[128,1024]{1,0:T(8,128)(2,1)} %refs_0_.7, bf16[128,1024]{1,0:T(8,128)(2,1)} %refs_1_.7, s32[2,32]{1,0:T(2,128)} %refs_2_.7), custom_call_target="tpu_custom_call" | custom-call | flops 1000000000 | bytes 3000000 | tf_op jit(solution)/shard_map/kv_pack/pallas_call | solution.py:56
  2.8 0.5 collective-permute-start
  3.3 1.4 %collective-permute-done.refs_3_ = bf16[4,272,128]{2,1,0:T(8,128)(2,1)S(1)} collective-permute-done((bf16[4,272,128]{2,1,0:T(8,128)(2,1)}, bf16[4,272,128]{2,1,0:T(8,128)(2,1)S(1)}, u32[]{:S(2)}, u32[]{:S(2)}) %collective-permute-start) | collective-permute-done | bytes 278560 | tf_op jit(solution)/shard_map/ppermute | solution.py:355
  4.7 0.1 kv_pair.1
  4.9 0.4 qg_pack.5
  5.3 0.4 collective-permute-start.5
  5.7 2.6 %collective-permute-start.4 = (bf16[2,272,128]{2,1,0:T(8,128)(2,1)S(1)}, bf16[2,272,128]{2,1,0:T(8,128)(2,1)S(1)}, u32[]{:S(2)}, u32[]{:S(2)}) collective-permute-start(bf16[2,272,128]{2,1,0:T(8,128)(2,1)S(1)} %get-tuple-element.36.refs_3_), channel_id=1, source_target_pairs={{0,16},{16,0},{1,17},{17,1},{2,18},{18,2},{3,19},{19,3},{4,20},{20... | collective-permute-start | bytes 417800 | tf_op jit(solution)/shard_map/ppermute | solution.py:358
  8.3 1.5 %collective-permute-start.1 = (bf16[2,272,128]{2,1,0:T(8,128)(2,1)S(1)}, bf16[2,272,128]{2,1,0:T(8,128)(2,1)S(1)}, u32[]{:S(2)}, u32[]{:S(2)}) collective-permute-start(bf16[2,272,128]{2,1,0:T(8,128)(2,1)S(1)} %get-tuple-element.37.refs_4_), channel_id=1, source_target_pairs={{0,2},{1,3},{2,0},{3,1},{4,6},{5,7},{6,4},{7,5},{8,10},{9,11},{10,... | collective-permute-start | bytes 417800 | tf_op jit(solution)/shard_map/ppermute | solution.py:355
  9.9 1.6 %collective-permute-start.2 = (bf16[2,272,128]{2,1,0:T(8,128)(2,1)S(1)}, bf16[2,272,128]{2,1,0:T(8,128)(2,1)S(1)}, u32[]{:S(2)}, u32[]{:S(2)}) collective-permute-start(bf16[2,272,128]{2,1,0:T(8,128)(2,1)S(1)} %get-tuple-element.38), channel_id=1, source_target_pairs={{0,4},{1,5},{2,6},{3,7},{4,0},{5,1},{6,2},{7,3},{8,12},{9,13},{10,... | collective-permute-start | bytes 417800 | tf_op jit(solution)/shard_map/ppermute | solution.py:355
  11.4 0.4 collective-permute-start.3
  11.8 0.7 collective-permute-done.4.refs_4_.refs_7_.refs_5_
  12.5 0.4 qg_pack.4
  13.0 1.0 %collective-permute-done.1.refs_4_ = bf16[2,272,128]{2,1,0:T(8,128)(2,1)S(1)} collective-permute-done((bf16[2,272,128]{2,1,0:T(8,128)(2,1)S(1)}, bf16[2,272,128]{2,1,0:T(8,128)(2,1)S(1)}, u32[]{:S(2)}, u32[]{:S(2)}) %collective-permute-start.1) | collective-permute-done | bytes 139296 | tf_op jit(solution)/shard_map/ppermute | solution.py:355
  14.0 2.4 %collective-permute-done.2.refs_5_.refs_3_ = bf16[2,272,128]{2,1,0:T(8,128)(2,1)S(1)} collective-permute-done((bf16[2,272,128]{2,1,0:T(8,128)(2,1)S(1)}, bf16[2,272,128]{2,1,0:T(8,128)(2,1)S(1)}, u32[]{:S(2)}, u32[]{:S(2)}) %collective-permute-start.2) | collective-permute-done | bytes 139296 | tf_op jit(solution)/shard_map/ppermute | solution.py:355
  16.4 1.7 %collective-permute-done.3.refs_6_.refs_2_ = bf16[2,272,128]{2,1,0:T(8,128)(2,1)S(1)} collective-permute-done((bf16[2,272,128]{2,1,0:T(8,128)(2,1)S(1)}, bf16[2,272,128]{2,1,0:T(8,128)(2,1)S(1)}, u32[]{:S(2)}, u32[]{:S(2)}) %collective-permute-start.3) | collective-permute-done | bytes 139296 | tf_op jit(solution)/shard_map/ppermute | solution.py:355
  18.2 2.6 %collective-permute-start.13 = (bf16[2,1328,128]{2,1,0:T(8,128)(2,1)S(1)}, bf16[2,1328,128]{2,1,0:T(8,128)(2,1)S(1)}, u32[]{:S(2)}, u32[]{:S(2)}) collective-permute-start(bf16[2,1328,128]{2,1,0:T(8,128)(2,1)S(1)} %pair_up.2), channel_id=1, source_target_pairs={{0,6},{1,7},{2,4},{3,5},{4,2},{5,3},{6,0},{7,1},{8,14},{9,15},{10,... | collective-permute-start | bytes 2039816 | tf_op jit(solution)/shard_map/ppermute | solution.py:355
  20.8 0.5 collective-permute-start.7
  21.3 1.5 %collective-permute-start.8 = (bf16[2,272,128]{2,1,0:T(8,128)(2,1)S(1)}, bf16[2,272,128]{2,1,0:T(8,128)(2,1)S(1)}, u32[]{:S(2)}, u32[]{:S(2)}) collective-permute-start(bf16[2,272,128]{2,1,0:T(8,128)(2,1)S(1)} %collective-permute-done.3.refs_6_.refs_2_), channel_id=1, source_target_pairs={{0,16},{16,0},{1,17},{17,1},{2,18},{18,2},{3,19},{19,3},{4,20},{20... | collective-permute-start | bytes 417800 | tf_op jit(solution)/shard_map/ppermute | solution.py:358
  22.8 0.5 collective-permute-start.6
  23.4 4.0 %collective-permute-done.7.refs_9_.refs_4_ = bf16[2,272,128]{2,1,0:T(8,128)(2,1)S(1)} collective-permute-done((bf16[2,272,128]{2,1,0:T(8,128)(2,1)S(1)}, bf16[2,272,128]{2,1,0:T(8,128)(2,1)S(1)}, u32[]{:S(2)}, u32[]{:S(2)}) %collective-permute-start.7) | collective-permute-done | bytes 139296 | tf_op jit(solution)/shard_map/ppermute | solution.py:358
  27.4 0.4 qg_pack.7
  27.8 0.5 collective-permute-start.11
  28.4 0.5 collective-permute-start.12
  28.8 0.7 collective-permute-done.8.refs_10_.refs_4_
  29.5 0.4 qg_pack.6
  29.9 1.1 %collective-permute-done.6.refs_8_ = bf16[2,272,128]{2,1,0:T(8,128)(2,1)S(1)} collective-permute-done((bf16[2,272,128]{2,1,0:T(8,128)(2,1)S(1)}, bf16[2,272,128]{2,1,0:T(8,128)(2,1)S(1)}, u32[]{:S(2)}, u32[]{:S(2)}) %collective-permute-start.6) | collective-permute-done | bytes 139296 | tf_op jit(solution)/shard_map/ppermute | solution.py:358
  31.0 1.1 %collective-permute-start.9 = (bf16[1,1328,128]{2,1,0:T(8,128)(2,1)S(1)}, bf16[1,1328,128]{2,1,0:T(8,128)(2,1)S(1)}, u32[]{:S(2)}, u32[]{:S(2)}) collective-permute-start(bf16[1,1328,128]{2,1,0:T(8,128)(2,1)S(1)} %get-tuple-element.42), channel_id=1, source_target_pairs={{0,3},{1,2},{2,1},{3,0},{4,7},{5,6},{6,5},{7,4},{8,11},{9,10},{10,... | collective-permute-start | bytes 1019912 | tf_op jit(solution)/shard_map/ppermute | solution.py:355
  32.1 2.3 %attend_0.1 = (bf16[2,640,128]{2,1,0:T(8,128)(2,1)S(1)}, bf16[17,128,128]{2,1,0:T(8,128)(2,1)S(1)}, bf16[17,128,128]{2,1,0:T(8,128)(2,1)S(1)}, bf16[17,128,128]{2,1,0:T(8,128)(2,1)S(1)}, f32[17,256,128]{2,1,0:T(8,128)S(1)}) custom-call(s32[8,34]{1,0:T(8,128)S(1)} %maximum_convert_fusion.refs_0_, bf16[1,1328,128]{2,1,0:T(8,128)(2,1)S(1)} %get-tuple-element.40.refs_1_, ...), custom_call_target="tpu_custom_call" | custom-call | flops 500000000 | bytes 1500000 | tf_op jit(solution)/shard_map/attend_0/pallas_call | solution.py:56
  34.4 3.0 %collective-permute-done.13.refs_1_ = bf16[2,1328,128]{2,1,0:T(8,128)(2,1)S(1)} collective-permute-done((bf16[2,1328,128]{2,1,0:T(8,128)(2,1)S(1)}, bf16[2,1328,128]{2,1,0:T(8,128)(2,1)S(1)}, u32[]{:S(2)}, u32[]{:S(2)}) %collective-permute-start.13) | collective-permute-done | bytes 679968 | tf_op jit(solution)/shard_map/ppermute | solution.py:355
  37.4 7.2 %attend_1.1 = (bf16[2,640,128]{2,1,0:T(8,128)(2,1)S(1)}, f32[17,256,128]{2,1,0:T(8,128)S(1)}) custom-call(s32[8,34]{1,0:T(8,128)S(1)} %maximum_convert_fusion.refs_0_, bf16[2,1328,128]{2,1,0:T(8,128)(2,1)S(1)} %collective-permute-done.13.refs_1_, bf16[17,128,128]{2,1,0:T(8,128)(2,1)S(1)} %get-tuple-element.44.refs_2_.refs_3_, ...), custom_call_target="tpu_custom_call" | custom-call | flops 500000000 | bytes 1500000 | tf_op jit(solution)/shard_map/attend_1/pallas_call | solution.py:56
  44.8 3.9 %attend_2.1 = (bf16[2,640,128]{2,1,0:T(8,128)(2,1)S(1)}, f32[17,256,128]{2,1,0:T(8,128)S(1)}) custom-call(s32[8,34]{1,0:T(8,128)S(1)} %maximum_convert_fusion.refs_0_, bf16[1,1328,128]{2,1,0:T(8,128)(2,1)S(1)} %collective-permute-done.11.refs_1_, bf16[1,1328,128]{2,1,0:T(8,128)(2,1)S(1)} %collective-permute-done.12.refs_2_, ...), custom_call_target="tpu_custom_call" | custom-call | flops 500000000 | bytes 1500000 | tf_op jit(solution)/shard_map/attend_2/pallas_call | solution.py:56
  48.6 2.5 %collective-permute-done.10.refs_2_ = bf16[1,1328,128]{2,1,0:T(8,128)(2,1)S(1)} collective-permute-done((bf16[1,1328,128]{2,1,0:T(8,128)(2,1)S(1)}, bf16[1,1328,128]{2,1,0:T(8,128)(2,1)S(1)}, u32[]{:S(2)}, u32[]{:S(2)}) %collective-permute-start.10) | collective-permute-done | bytes 340000 | tf_op jit(solution)/shard_map/ppermute | solution.py:355
  51.1 0.6 collective-permute-done.9.refs_1_
  51.7 4.6 %attend_3.1 = (bf16[2,640,128]{2,1,0:T(8,128)(2,1)S(1)}, bf16[2,640,128]{2,1,0:T(8,128)(2,1)S(1)}, f32[4,256,128]{2,1,0:T(8,128)S(1)}, f32[4,256,128]{2,1,0:T(8,...) custom-call(s32[8,34]{1,0:T(8,128)S(1)} %maximum_convert_fusion.refs_0_, ...), custom_call_target="tpu_custom_call" | custom-call | flops 6000000000 | bytes 18000000 | tf_op jit(solution)/shard_map/attend_3/pallas_call | solution.py:56
  56.3 1.1 %collective-permute-done.16.refs_1_.refs_3_ = bf16[2,640,128]{2,1,0:T(8,128)(2,1)S(1)} collective-permute-done((bf16[2,640,128]{2,1,0:T(8,128)(2,1)S(1)}, bf16[2,640,128]{2,1,0:T(8,128)(2,1)S(1)}, u32[]{:S(2)}, u32[]{:S(2)}) %collective-permute-start.16) | collective-permute-done | bytes 327712 | tf_op jit(solution)/shard_map/ppermute | solution.py:355
  57.4 0.2 collective-permute-start.18
  57.6 1.9 %collective-permute-start.17 = (bf16[4,256,128]{2,1,0:T(8,128)(2,1)S(1)}, bf16[4,256,128]{2,1,0:T(8,128)(2,1)S(1)}, u32[]{:S(2)}, u32[]{:S(2)}) collective-permute-start(bf16[4,256,128]{2,1,0:T(8,128)(2,1)S(1)} %get-tuple-element.58), channel_id=1, source_target_pairs={{0,16},{16,0},{1,17},{17,1},{2,18},{18,2},{3,19},{19,3},{4,20},{20... | collective-permute-start | bytes 786440 | tf_op jit(solution)/shard_map/ppermute | solution.py:358
  59.5 1.1 %collective-permute-start.14 = (bf16[2,640,128]{2,1,0:T(8,128)(2,1)S(1)}, bf16[2,640,128]{2,1,0:T(8,128)(2,1)S(1)}, u32[]{:S(2)}, u32[]{:S(2)}) collective-permute-start(bf16[2,640,128]{2,1,0:T(8,128)(2,1)S(1)} %get-tuple-element.54), channel_id=1, source_target_pairs={{0,2},{1,3},{2,0},{3,1},{4,6},{5,7},{6,4},{7,5},{8,10},{9,11},{10,... | collective-permute-start | bytes 983048 | tf_op jit(solution)/shard_map/ppermute | solution.py:355
  60.5 1.6 %collective-permute-start.15 = (bf16[2,640,128]{2,1,0:T(8,128)(2,1)S(1)}, bf16[2,640,128]{2,1,0:T(8,128)(2,1)S(1)}, u32[]{:S(2)}, u32[]{:S(2)}) collective-permute-start(bf16[2,640,128]{2,1,0:T(8,128)(2,1)S(1)} %get-tuple-element.55), channel_id=1, source_target_pairs={{0,4},{1,5},{2,6},{3,7},{4,0},{5,1},{6,2},{7,3},{8,12},{9,13},{10,... | collective-permute-start | bytes 983048 | tf_op jit(solution)/shard_map/ppermute | solution.py:355
  62.1 4.6 %collective-permute-done.18.refs_1_ = bf16[4,256,128]{2,1,0:T(8,128)(2,1)S(1)} collective-permute-done((bf16[4,256,128]{2,1,0:T(8,128)(2,1)S(1)}, bf16[4,256,128]{2,1,0:T(8,128)(2,1)S(1)}, u32[]{:S(2)}, u32[]{:S(2)}) %collective-permute-start.18) | collective-permute-done | bytes 262176 | tf_op jit(solution)/shard_map/ppermute | solution.py:358
  66.8 3.3 %collective-permute-done.17.refs_1_ = bf16[4,256,128]{2,1,0:T(8,128)(2,1)S(1)} collective-permute-done((bf16[4,256,128]{2,1,0:T(8,128)(2,1)S(1)}, bf16[4,256,128]{2,1,0:T(8,128)(2,1)S(1)}, u32[]{:S(2)}, u32[]{:S(2)}) %collective-permute-start.17) | collective-permute-done | bytes 262176 | tf_op jit(solution)/shard_map/ppermute | solution.py:358
  70.4 2.3 %collective-permute-start.21 = (bf16[2,256,128]{2,1,0:T(8,128)(2,1)S(1)}, bf16[2,256,128]{2,1,0:T(8,128)(2,1)S(1)}, u32[]{:S(2)}, u32[]{:S(2)}) collective-permute-start(bf16[2,256,128]{2,1,0:T(8,128)(2,1)S(1)} %get-tuple-element.63), channel_id=1, source_target_pairs={{0,6},{1,7},{2,4},{3,5},{4,2},{5,3},{6,0},{7,1},{8,14},{9,15},{10,... | collective-permute-start | bytes 393224 | tf_op jit(solution)/shard_map/ppermute | solution.py:355
  72.6 1.0 %collective-permute-start.22 = (bf16[2,256,128]{2,1,0:T(8,128)(2,1)S(1)}, bf16[2,256,128]{2,1,0:T(8,128)(2,1)S(1)}, u32[]{:S(2)}, u32[]{:S(2)}) collective-permute-start(bf16[2,256,128]{2,1,0:T(8,128)(2,1)S(1)} %get-tuple-element.64), channel_id=1, source_target_pairs={{0,4},{1,5},{2,6},{3,7},{4,0},{5,1},{6,2},{7,3},{8,12},{9,13},{10,... | collective-permute-start | bytes 393224 | tf_op jit(solution)/shard_map/ppermute | solution.py:355
  73.6 0.5 collective-permute-start.23
  74.1 1.4 %query_unpack.1 = (bf16[128,5120]{1,0:T(8,128)(2,1)}, f32[8,128]{1,0:T(8,128)S(1)}) custom-call(bf16[2,640,128]{2,1,0:T(8,128)(2,1)S(1)} %get-tuple-element.41.refs_0_, bf16[2,640,128]{2,1,0:T(8,128)(2,1)S(1)} %collective-permute-done.14.refs_1_, bf16[2,640,128]{2,1,0:T(8,128)(2,1)S(1)} %collective-permute-done.15.refs_2_, ...), custom_call_target="tpu_custom_call" | custom-call | flops 1000000000 | bytes 3000000 | tf_op jit(solution)/shard_map/query_unpack/pallas_call | solution.py:56
  75.5 2.1 %collective-permute-done.21.refs_0_ = bf16[2,256,128]{2,1,0:T(8,128)(2,1)S(1)} collective-permute-done((bf16[2,256,128]{2,1,0:T(8,128)(2,1)S(1)}, bf16[2,256,128]{2,1,0:T(8,128)(2,1)S(1)}, u32[]{:S(2)}, u32[]{:S(2)}) %collective-permute-start.21) | collective-permute-done | bytes 131104 | tf_op jit(solution)/shard_map/ppermute | solution.py:355
  77.6 2.6 %collective-permute-done.22.refs_1_ = bf16[2,256,128]{2,1,0:T(8,128)(2,1)S(1)} collective-permute-done((bf16[2,256,128]{2,1,0:T(8,128)(2,1)S(1)}, bf16[2,256,128]{2,1,0:T(8,128)(2,1)S(1)}, u32[]{:S(2)}, u32[]{:S(2)}) %collective-permute-start.22) | collective-permute-done | bytes 131104 | tf_op jit(solution)/shard_map/ppermute | solution.py:355
  80.3 0.9 %kv_unpack.1 = (bf16[128,1024]{1,0:T(8,128)(2,1)}, bf16[128,1024]{1,0:T(8,128)(2,1)}) custom-call(bf16[2,256,128]{2,1,0:T(8,128)(2,1)S(1)} %collective-permute-done.21.refs_0_, bf16[2,256,128]{2,1,0:T(8,128)(2,1)S(1)} %collective-permute-done.22.refs_1_, bf16[2,256,128]{2,1,0:T(8,128)(2,1)S(1)} %collective-permute-done.23.refs_2_, ...), custom_call_target="tpu_custom_call" | custom-call | flops 1000000000 | bytes 3000000 | tf_op jit(solution)/shard_map/kv_unpack/pallas_call | solution.py:56
  (42 shorter events, 0.6 us)
Async XLA Ops:
  0.6 4.1 %copy-start.6 = (s32[2,32]{1,0:T(2,128)S(1)}, s32[2,32]{1,0:T(2,128)}, u32[]{:S(2)}) copy-start(s32[2,32]{1,0:T(2,128)} %refs_2_.7) | copy-start | bytes 772
  0.6 4.1 %copy-start.4 = (bf16[128,1024]{1,0:T(8,128)(2,1)S(1)}, bf16[128,1024]{1,0:T(8,128)(2,1)}, u32[]{:S(2)}) copy-start(bf16[128,1024]{1,0:T(8,128)(2,1)} %refs_0_.7) | copy-start | bytes 786436
  0.7 4.0 %copy-start.5 = (bf16[128,1024]{1,0:T(8,128)(2,1)S(1)}, bf16[128,1024]{1,0:T(8,128)(2,1)}, u32[]{:S(2)}) copy-start(bf16[128,1024]{1,0:T(8,128)(2,1)} %refs_1_.7) | copy-start | bytes 786436
  0.7 4.2 %copy-start.1 = (bf16[128,5120]{1,0:T(8,128)(2,1)S(1)}, bf16[128,5120]{1,0:T(8,128)(2,1)}, u32[]{:S(2)}) copy-start(bf16[128,5120]{1,0:T(8,128)(2,1)} %refs_1_.11) | copy-start | bytes 3932164
  0.7 4.2 %copy-start.2 = (bf16[128,5120]{1,0:T(8,128)(2,1)S(1)}, bf16[128,5120]{1,0:T(8,128)(2,1)}, u32[]{:S(2)}) copy-start(bf16[128,5120]{1,0:T(8,128)(2,1)} %refs_2_.11) | copy-start | bytes 3932164
  2.7 2.1 %copy-start = (bf16[128,5120]{1,0:T(8,128)(2,1)S(1)}, bf16[128,5120]{1,0:T(8,128)(2,1)}, u32[]{:S(2)}) copy-start(bf16[128,5120]{1,0:T(8,128)(2,1)} %refs_0_.11) | copy-start | bytes 3932164
  2.8 2.1 %copy-start.3 = (f32[128,40]{0,1:T(8,128)S(1)}, f32[128,40]{0,1:T(8,128)}, u32[]{:S(2)}) copy-start(f32[128,40]{0,1:T(8,128)} %param.12) | copy-start | bytes 61444
  2.8 1.9 %collective-permute-start = (bf16[4,272,128]{2,1,0:T(8,128)(2,1)}, bf16[4,272,128]{2,1,0:T(8,128)(2,1)S(1)}, u32[]{:S(2)}, u32[]{:S(2)}) collective-permute-start(bf16[4,272,128]{2,1,0:T(8,128)(2,1)} %kv_pack.1), channel_id=1, source_target_pairs={{0,1},{1,0},{2,3},{3,2},{4,5},{5,4},{6,7},{7,6},{8,9},{9,8},{10,11... | collective-permute-start | bytes 835592 | tf_op jit(solution)/shard_map/ppermute | solution.py:355
  5.3 7.6 %collective-permute-start.5 = (bf16[2,1328,128]{2,1,0:T(8,128)(2,1)S(1)}, bf16[2,1328,128]{2,1,0:T(8,128)(2,1)S(1)}, u32[]{:S(2)}, u32[]{:S(2)}) collective-permute-start(bf16[2,1328,128]{2,1,0:T(8,128)(2,1)S(1)} %qg_pack.5), channel_id=1, source_target_pairs={{0,1},{1,0},{2,3},{3,2},{4,5},{5,4},{6,7},{7,6},{8,9},{9,8},{10,11... | collective-permute-start | bytes 2039816 | tf_op jit(solution)/shard_map/ppermute | solution.py:355
  5.7 6.8 %collective-permute-start.4 = (bf16[2,272,128]{2,1,0:T(8,128)(2,1)S(1)}, bf16[2,272,128]{2,1,0:T(8,128)(2,1)S(1)}, u32[]{:S(2)}, u32[]{:S(2)}) collective-permute-start(bf16[2,272,128]{2,1,0:T(8,128)(2,1)S(1)} %get-tuple-element.36.refs_3_), channel_id=1, source_target_pairs={{0,16},{16,0},{1,17},{17,1},{2,18},{18,2},{3,19},{19,3},{4,20},{20... | collective-permute-start | bytes 417800 | tf_op jit(solution)/shard_map/ppermute | solution.py:358
  8.3 5.7 %collective-permute-start.1 = (bf16[2,272,128]{2,1,0:T(8,128)(2,1)S(1)}, bf16[2,272,128]{2,1,0:T(8,128)(2,1)S(1)}, u32[]{:S(2)}, u32[]{:S(2)}) collective-permute-start(bf16[2,272,128]{2,1,0:T(8,128)(2,1)S(1)} %get-tuple-element.37.refs_4_), channel_id=1, source_target_pairs={{0,2},{1,3},{2,0},{3,1},{4,6},{5,7},{6,4},{7,5},{8,10},{9,11},{10,... | collective-permute-start | bytes 417800 | tf_op jit(solution)/shard_map/ppermute | solution.py:355
  9.9 6.6 %collective-permute-start.2 = (bf16[2,272,128]{2,1,0:T(8,128)(2,1)S(1)}, bf16[2,272,128]{2,1,0:T(8,128)(2,1)S(1)}, u32[]{:S(2)}, u32[]{:S(2)}) collective-permute-start(bf16[2,272,128]{2,1,0:T(8,128)(2,1)S(1)} %get-tuple-element.38), channel_id=1, source_target_pairs={{0,4},{1,5},{2,6},{3,7},{4,0},{5,1},{6,2},{7,3},{8,12},{9,13},{10,... | collective-permute-start | bytes 417800 | tf_op jit(solution)/shard_map/ppermute | solution.py:355
  11.4 6.7 %collective-permute-start.3 = (bf16[2,272,128]{2,1,0:T(8,128)(2,1)S(1)}, bf16[2,272,128]{2,1,0:T(8,128)(2,1)S(1)}, u32[]{:S(2)}, u32[]{:S(2)}) collective-permute-start(bf16[2,272,128]{2,1,0:T(8,128)(2,1)S(1)} %get-tuple-element.39), channel_id=1, source_target_pairs={{0,6},{1,7},{2,4},{3,5},{4,2},{5,3},{6,0},{7,1},{8,14},{9,15},{10,... | collective-permute-start | bytes 417800 | tf_op jit(solution)/shard_map/ppermute | solution.py:355
  18.2 19.2 %collective-permute-start.13 = (bf16[2,1328,128]{2,1,0:T(8,128)(2,1)S(1)}, bf16[2,1328,128]{2,1,0:T(8,128)(2,1)S(1)}, u32[]{:S(2)}, u32[]{:S(2)}) collective-permute-start(bf16[2,1328,128]{2,1,0:T(8,128)(2,1)S(1)} %pair_up.2), channel_id=1, source_target_pairs={{0,6},{1,7},{2,4},{3,5},{4,2},{5,3},{6,0},{7,1},{8,14},{9,15},{10,... | collective-permute-start | bytes 2039816 | tf_op jit(solution)/shard_map/ppermute | solution.py:355
  20.8 6.6 %collective-permute-start.7 = (bf16[2,272,128]{2,1,0:T(8,128)(2,1)S(1)}, bf16[2,272,128]{2,1,0:T(8,128)(2,1)S(1)}, u32[]{:S(2)}, u32[]{:S(2)}) collective-permute-start(bf16[2,272,128]{2,1,0:T(8,128)(2,1)S(1)} %collective-permute-done.2.refs_5_.refs_3_), channel_id=1, source_target_pairs={{0,16},{16,0},{1,17},{17,1},{2,18},{18,2},{3,19},{19,3},{4,20},{20... | collective-permute-start | bytes 417800 | tf_op jit(solution)/shard_map/ppermute | solution.py:358
  21.3 8.2 %collective-permute-start.8 = (bf16[2,272,128]{2,1,0:T(8,128)(2,1)S(1)}, bf16[2,272,128]{2,1,0:T(8,128)(2,1)S(1)}, u32[]{:S(2)}, u32[]{:S(2)}) collective-permute-start(bf16[2,272,128]{2,1,0:T(8,128)(2,1)S(1)} %collective-permute-done.3.refs_6_.refs_2_), channel_id=1, source_target_pairs={{0,16},{16,0},{1,17},{17,1},{2,18},{18,2},{3,19},{19,3},{4,20},{20... | collective-permute-start | bytes 417800 | tf_op jit(solution)/shard_map/ppermute | solution.py:358
  22.8 8.2 %collective-permute-start.6 = (bf16[2,272,128]{2,1,0:T(8,128)(2,1)S(1)}, bf16[2,272,128]{2,1,0:T(8,128)(2,1)S(1)}, u32[]{:S(2)}, u32[]{:S(2)}) collective-permute-start(bf16[2,272,128]{2,1,0:T(8,128)(2,1)S(1)} %collective-permute-done.1.refs_4_), channel_id=1, source_target_pairs={{0,16},{16,0},{1,17},{17,1},{2,18},{18,2},{3,19},{19,3},{4,20},{20... | collective-permute-start | bytes 417800 | tf_op jit(solution)/shard_map/ppermute | solution.py:358
  27.8 16.9 %collective-permute-start.11 = (bf16[1,1328,128]{2,1,0:T(8,128)(2,1)S(1)}, bf16[1,1328,128]{2,1,0:T(8,128)(2,1)S(1)}, u32[]{:S(2)}, u32[]{:S(2)}) collective-permute-start(bf16[1,1328,128]{2,1,0:T(8,128)(2,1)S(1)} %get-tuple-element.47), channel_id=1, source_target_pairs={{0,2},{1,3},{2,0},{3,1},{4,6},{5,7},{6,4},{7,5},{8,10},{9,11},{10,... | collective-permute-start | bytes 1019912 | tf_op jit(solution)/shard_map/ppermute | solution.py:355
  28.4 16.4 %collective-permute-start.12 = (bf16[1,1328,128]{2,1,0:T(8,128)(2,1)S(1)}, bf16[1,1328,128]{2,1,0:T(8,128)(2,1)S(1)}, u32[]{:S(2)}, u32[]{:S(2)}) collective-permute-start(bf16[1,1328,128]{2,1,0:T(8,128)(2,1)S(1)} %get-tuple-element.48), channel_id=1, source_target_pairs={{0,4},{1,5},{2,6},{3,7},{4,0},{5,1},{6,2},{7,3},{8,12},{9,13},{10,... | collective-permute-start | bytes 1019912 | tf_op jit(solution)/shard_map/ppermute | solution.py:355
  29.9 21.2 %collective-permute-start.10 = (bf16[1,1328,128]{2,1,0:T(8,128)(2,1)S(1)}, bf16[1,1328,128]{2,1,0:T(8,128)(2,1)S(1)}, u32[]{:S(2)}, u32[]{:S(2)}) collective-permute-start(bf16[1,1328,128]{2,1,0:T(8,128)(2,1)S(1)} %get-tuple-element.43), channel_id=1, source_target_pairs={{0,5},{1,4},{2,7},{3,6},{4,1},{5,0},{6,3},{7,2},{8,13},{9,12},{10,... | collective-permute-start | bytes 1019912 | tf_op jit(solution)/shard_map/ppermute | solution.py:355
  31.0 20.7 %collective-permute-start.9 = (bf16[1,1328,128]{2,1,0:T(8,128)(2,1)S(1)}, bf16[1,1328,128]{2,1,0:T(8,128)(2,1)S(1)}, u32[]{:S(2)}, u32[]{:S(2)}) collective-permute-start(bf16[1,1328,128]{2,1,0:T(8,128)(2,1)S(1)} %get-tuple-element.42), channel_id=1, source_target_pairs={{0,3},{1,2},{2,1},{3,0},{4,7},{5,6},{6,5},{7,4},{8,11},{9,10},{10,... | collective-permute-start | bytes 1019912 | tf_op jit(solution)/shard_map/ppermute | solution.py:355
  44.7 12.7 %collective-permute-start.16 = (bf16[2,640,128]{2,1,0:T(8,128)(2,1)S(1)}, bf16[2,640,128]{2,1,0:T(8,128)(2,1)S(1)}, u32[]{:S(2)}, u32[]{:S(2)}) collective-permute-start(bf16[2,640,128]{2,1,0:T(8,128)(2,1)S(1)} %get-tuple-element.56), channel_id=1, source_target_pairs={{0,6},{1,7},{2,4},{3,5},{4,2},{5,3},{6,0},{7,1},{8,14},{9,15},{10,... | collective-permute-start | bytes 983048 | tf_op jit(solution)/shard_map/ppermute | solution.py:355
  57.4 9.3 %collective-permute-start.18 = (bf16[4,256,128]{2,1,0:T(8,128)(2,1)S(1)}, bf16[4,256,128]{2,1,0:T(8,128)(2,1)S(1)}, u32[]{:S(2)}, u32[]{:S(2)}) collective-permute-start(bf16[4,256,128]{2,1,0:T(8,128)(2,1)S(1)} %pass_on.1), channel_id=1, source_target_pairs={{0,16},{16,0},{1,17},{17,1},{2,18},{18,2},{3,19},{19,3},{4,20},{20... | collective-permute-start | bytes 786440 | tf_op jit(solution)/shard_map/ppermute | solution.py:358
  57.6 12.5 %collective-permute-start.17 = (bf16[4,256,128]{2,1,0:T(8,128)(2,1)S(1)}, bf16[4,256,128]{2,1,0:T(8,128)(2,1)S(1)}, u32[]{:S(2)}, u32[]{:S(2)}) collective-permute-start(bf16[4,256,128]{2,1,0:T(8,128)(2,1)S(1)} %get-tuple-element.58), channel_id=1, source_target_pairs={{0,16},{16,0},{1,17},{17,1},{2,18},{18,2},{3,19},{19,3},{4,20},{20... | collective-permute-start | bytes 786440 | tf_op jit(solution)/shard_map/ppermute | solution.py:358
  59.5 10.7 %collective-permute-start.14 = (bf16[2,640,128]{2,1,0:T(8,128)(2,1)S(1)}, bf16[2,640,128]{2,1,0:T(8,128)(2,1)S(1)}, u32[]{:S(2)}, u32[]{:S(2)}) collective-permute-start(bf16[2,640,128]{2,1,0:T(8,128)(2,1)S(1)} %get-tuple-element.54), channel_id=1, source_target_pairs={{0,2},{1,3},{2,0},{3,1},{4,6},{5,7},{6,4},{7,5},{8,10},{9,11},{10,... | collective-permute-start | bytes 983048 | tf_op jit(solution)/shard_map/ppermute | solution.py:355
  60.5 9.7 %collective-permute-start.15 = (bf16[2,640,128]{2,1,0:T(8,128)(2,1)S(1)}, bf16[2,640,128]{2,1,0:T(8,128)(2,1)S(1)}, u32[]{:S(2)}, u32[]{:S(2)}) collective-permute-start(bf16[2,640,128]{2,1,0:T(8,128)(2,1)S(1)} %get-tuple-element.55), channel_id=1, source_target_pairs={{0,4},{1,5},{2,6},{3,7},{4,0},{5,1},{6,2},{7,3},{8,12},{9,13},{10,... | collective-permute-start | bytes 983048 | tf_op jit(solution)/shard_map/ppermute | solution.py:355
  66.8 3.4 %collective-permute-start.19 = (bf16[4,256,128]{2,1,0:T(8,128)(2,1)S(1)}, bf16[4,256,128]{2,1,0:T(8,128)(2,1)S(1)}, u32[]{:S(2)}, u32[]{:S(2)}) collective-permute-start(bf16[4,256,128]{2,1,0:T(8,128)(2,1)S(1)} %kv_sum.3), channel_id=1, source_target_pairs={{0,1},{1,0},{2,3},{3,2},{4,5},{5,4},{6,7},{7,6},{8,9},{9,8},{10,11... | collective-permute-start | bytes 786440 | tf_op jit(solution)/shard_map/ppermute | solution.py:355
  70.3 3.8 %collective-permute-start.20 = (bf16[4,640,128]{2,1,0:T(8,128)(2,1)S(1)}, bf16[4,640,128]{2,1,0:T(8,128)(2,1)S(1)}, u32[]{:S(2)}, u32[]{:S(2)}) collective-permute-start(bf16[4,640,128]{2,1,0:T(8,128)(2,1)S(1)} %query_relay.1), channel_id=1, source_target_pairs={{0,1},{1,0},{2,3},{3,2},{4,5},{5,4},{6,7},{7,6},{8,9},{9,8},{10,11... | collective-permute-start | bytes 1966088 | tf_op jit(solution)/shard_map/ppermute | solution.py:355
  70.4 7.3 %collective-permute-start.21 = (bf16[2,256,128]{2,1,0:T(8,128)(2,1)S(1)}, bf16[2,256,128]{2,1,0:T(8,128)(2,1)S(1)}, u32[]{:S(2)}, u32[]{:S(2)}) collective-permute-start(bf16[2,256,128]{2,1,0:T(8,128)(2,1)S(1)} %get-tuple-element.63), channel_id=1, source_target_pairs={{0,6},{1,7},{2,4},{3,5},{4,2},{5,3},{6,0},{7,1},{8,14},{9,15},{10,... | collective-permute-start | bytes 393224 | tf_op jit(solution)/shard_map/ppermute | solution.py:355
  72.6 7.6 %collective-permute-start.22 = (bf16[2,256,128]{2,1,0:T(8,128)(2,1)S(1)}, bf16[2,256,128]{2,1,0:T(8,128)(2,1)S(1)}, u32[]{:S(2)}, u32[]{:S(2)}) collective-permute-start(bf16[2,256,128]{2,1,0:T(8,128)(2,1)S(1)} %get-tuple-element.64), channel_id=1, source_target_pairs={{0,4},{1,5},{2,6},{3,7},{4,0},{5,1},{6,2},{7,3},{8,12},{9,13},{10,... | collective-permute-start | bytes 393224 | tf_op jit(solution)/shard_map/ppermute | solution.py:355
  73.6 6.6 %collective-permute-start.23 = (bf16[2,256,128]{2,1,0:T(8,128)(2,1)S(1)}, bf16[2,256,128]{2,1,0:T(8,128)(2,1)S(1)}, u32[]{:S(2)}, u32[]{:S(2)}) collective-permute-start(bf16[2,256,128]{2,1,0:T(8,128)(2,1)S(1)} %get-tuple-element.65), channel_id=1, source_target_pairs={{0,2},{1,3},{2,0},{3,1},{4,6},{5,7},{6,4},{7,5},{8,10},{9,11},{10,... | collective-permute-start | bytes 393224 | tf_op jit(solution)/shard_map/ppermute | solution.py:355

commit v5 on v3

--- a/solution.py
+++ b/solution.py
@@ -182,7 +182,7 @@
     return call(functools.partial(qg_pack_kernel, slots), "qg_pack", in_vmem(4), outs, scratch, 1, args, after)
 
 
-def attend_kernel(ks, kind, *refs):
+def attend_kernel(ks, kind, width, *refs):
     refs = list(refs)
     opens, joins, closes = kind == "first", kind in ("join", "last"), kind == "last"
     lists = refs.pop(0)
@@ -234,7 +234,7 @@
         scores = dot_nt(both(keys, pair, 0), messages[n][:Q_ROWS, :])
         probs = jnp.exp2(scores * (SCALING * math.log2(math.e)) - totals)
         if diagonal:
-            at_key = lax.broadcasted_iota(jnp.int32, probs.shape, 0) - BLOCK
+            at_key = lax.broadcasted_iota(jnp.int32, probs.shape, 0) - (width - 1) * BLOCK
             at_query = lax.broadcasted_iota(jnp.int32, probs.shape, 1) % BLOCK
             probs = jnp.where(at_key <= at_query, probs, 0.0)
         grad_probs = dot_nt(both(values, pair, 0), messages[n][Q_ROWS:X_AT, :])
@@ -263,22 +263,25 @@
         deltas = jnp.concatenate([rows[8 + h : 9 + h, :] for h in range(GROUP)], axis=1)
         extras = (totals, deltas)
         count = lists[k, COUNT_COL]
-        pairs = count // 2
-        left = jnp.where(count % 2 == 1, lists[k, jnp.maximum(count - 1, 0)], spare)
+        steps = count // width
+        left = count - steps * width
+        first = tuple(
+            jnp.where(i < left, lists[k, jnp.minimum(steps * width + i, TREE_B - 1)], spare) for i in range(width - 1)
+        ) + (lists[k, OWN_COL],)
         if pair is not None:
             consume(n - 1, pair)
-        produce(n, (left, lists[k, OWN_COL]), extras, True)
+        produce(n, first, extras, True)
         if pair is not None:
             finish(n - 1)
         query_sum[...] = jnp.zeros(query_sum.shape, F32)
 
         def visit(t, held):
             consume(n, held)
-            following = (lists[k, 2 * t], lists[k, 2 * t + 1])
+            following = tuple(lists[k, width * t + i] for i in range(width))
             produce(n, following, extras, False)
             return following
 
-        pair = lax.fori_loop(0, pairs, visit, (left, lists[k, OWN_COL]))
+        pair = lax.fori_loop(0, steps, visit, first)
     consume(len(ks) - 1, pair)
     finish(len(ks) - 1)
 
@@ -292,7 +295,7 @@
                 other[i, BLOCK:, :] = sums[at + 1 - parity, BLOCK:, :].astype(BF16)
 
 
-def attend(name, kind, ks, lists, messages, state, micros):
+def attend(name, kind, ks, width, lists, messages, state, micros):
     blocks = 2 * KVH + 1
     sums = ((blocks, 2 * BLOCK, HD), F32)
     scratch = []
@@ -307,9 +310,9 @@
         scratch = [pltpu.VMEM(*sums)]
     else:
         outs += [sums]
-    scratch += [pltpu.VMEM((HD, Q_ROWS), F32), pltpu.VMEM((2 * BLOCK, Q_ROWS), BF16), pltpu.VMEM((2 * BLOCK, Q_ROWS), BF16)]
+    scratch += [pltpu.VMEM((HD, Q_ROWS), F32), pltpu.VMEM((width * BLOCK, Q_ROWS), BF16), pltpu.VMEM((width * BLOCK, Q_ROWS), BF16)]
     specs = [pl.BlockSpec(memory_space=pltpu.SMEM)] + in_vmem(len(messages) + len(state))
-    kernel = functools.partial(attend_kernel, ks, kind)
+    kernel = functools.partial(attend_kernel, ks, kind, width)
     return call(kernel, name, specs, outs, scratch, micros, (lists, *messages, *state))
 
 
@@ -345,6 +348,7 @@
 CHIPS = (0, 2, 4, 6)
 VISITS = (("first", (0, 1)), ("more", (6, 7)), ("more", (2, 4)), ("last", (3, 5)))
 EXPECTED = (0.5, 0.5, 0.5, 6)
+WIDTHS = (2, 4, 2, 4)
 BACK_HALVES = ((1, 3, 5, 7), CHIPS)
 
 
@@ -376,7 +380,7 @@
     for i, (kind, ks) in enumerate(VISITS):
         if kind == "last":
             state = (*state, grads[-1])
-        results = attend(f"attend_{i}", kind, ks, lists, here[i], state, EXPECTED[i])
+        results = attend(f"attend_{i}", kind, ks, WIDTHS[i], lists, here[i], state, EXPECTED[i])
         grads.append(results[0])
         state = tuple(results[1:]) if kind == "first" else (*state[:3], results[-1])
     far_back = exchanged(grads[1], 6)

time: 82.5 us -> 82.3 us (level)
  Pallas kernels: 23.9 us -> 26.3 us
  waiting for transfers between devices: 33.9 us -> 31.6 us
    pallas_call x18, Pallas kernels: 23.9 us -> 26.3 us  [call(): pl.pallas_call(body, name=name, in_specs=[*in_specs, *[pl.BlockSpec(memor...]
    ppermute x18, waiting for transfers between devices: 18.9 us -> 17.1 us  [exchanged(): return lax.ppermute(array, 'blk', [(i, i ^ k) for i in range(size)])]
  transfers between devices with their start and end apart: 24 -> 24, of which waited for: 19 -> 17; matrix products, arithmetic and copies ran while one was open for 0% -> 0% of each run, Pallas kernels for 25% -> 28%
where the time goes in v5:
time: 82.3 us; the launch traced here: 82.2 us
  waiting for transfers between devices  31.6 us (38%)
  Pallas kernels  26.3 us (32%)
  starting transfers between devices  23.2 us (28%)
  between operations  0.93 us (1%)
    pallas_call x18, Pallas kernels, call(): pl.pallas_call(body, name=name, in_specs=[*in_specs, *[pl.BlockSpec(memor...  26.3 us
    ppermute x18, waiting for transfers between devices, exchanged(): return lax.ppermute(array, 'blk', [(i, i ^ k) for i in range(size)])  17.1 us
    ppermute x18, starting transfers between devices, exchanged(): return lax.ppermute(array, 'blk', [(i, i ^ k) for i in range(size)])  15.9 us
    ppermute x6, waiting for transfers between devices, swapped(): return lax.ppermute(array, 'head', [(0, 1), (1, 0)])  14.6 us
    ppermute x6, starting transfers between devices, swapped(): return lax.ppermute(array, 'head', [(0, 1), (1, 0)])  7.29 us
  transfers between devices with their start and end apart: 24, of which 17 were waited for; matrix products, arithmetic and copies ran while one was open for 0% of the time, Pallas kernels for 28%

profile of v5, /device:TPU:0, one launch (start us, length us, event | category | flops | bytes accessed | tf_op | source)
XLA Modules:
  0.0 82.2 jit_solution(7713219873480693176)
XLA Ops:
  0.7 2.1 %kv_pack.1 = bf16[4,272,128]{2,1,0:T(8,128)(2,1)} custom-call(bf16[128,1024]{1,0:T(8,128)(2,1)} %refs_0_.7, bf16[128,1024]{1,0:T(8,128)(2,1)} %refs_1_.7, s32[2,32]{1,0:T(2,128)} %refs_2_.7), custom_call_target="tpu_custom_call" | custom-call | flops 1000000000 | bytes 3000000 | tf_op jit(solution)/shard_map/kv_pack/pallas_call | solution.py:56
  2.8 0.5 collective-permute-start
  3.3 1.4 %collective-permute-done.refs_3_ = bf16[4,272,128]{2,1,0:T(8,128)(2,1)S(1)} collective-permute-done((bf16[4,272,128]{2,1,0:T(8,128)(2,1)}, bf16[4,272,128]{2,1,0:T(8,128)(2,1)S(1)}, u32[]{:S(2)}, u32[]{:S(2)}) %collective-permute-start) | collective-permute-done | bytes 278560 | tf_op jit(solution)/shard_map/ppermute | solution.py:359
  4.9 0.4 qg_pack.5
  5.3 0.4 collective-permute-start.5
  5.7 2.6 %collective-permute-start.4 = (bf16[2,272,128]{2,1,0:T(8,128)(2,1)S(1)}, bf16[2,272,128]{2,1,0:T(8,128)(2,1)S(1)}, u32[]{:S(2)}, u32[]{:S(2)}) collective-permute-start(bf16[2,272,128]{2,1,0:T(8,128)(2,1)S(1)} %get-tuple-element.36.refs_3_), channel_id=1, source_target_pairs={{0,16},{16,0},{1,17},{17,1},{2,18},{18,2},{3,19},{19,3},{4,20},{20... | collective-permute-start | bytes 417800 | tf_op jit(solution)/shard_map/ppermute | solution.py:362
  8.3 1.5 %collective-permute-start.1 = (bf16[2,272,128]{2,1,0:T(8,128)(2,1)S(1)}, bf16[2,272,128]{2,1,0:T(8,128)(2,1)S(1)}, u32[]{:S(2)}, u32[]{:S(2)}) collective-permute-start(bf16[2,272,128]{2,1,0:T(8,128)(2,1)S(1)} %get-tuple-element.37.refs_4_), channel_id=1, source_target_pairs={{0,2},{1,3},{2,0},{3,1},{4,6},{5,7},{6,4},{7,5},{8,10},{9,11},{10,... | collective-permute-start | bytes 417800 | tf_op jit(solution)/shard_map/ppermute | solution.py:359
  9.9 1.6 %collective-permute-start.2 = (bf16[2,272,128]{2,1,0:T(8,128)(2,1)S(1)}, bf16[2,272,128]{2,1,0:T(8,128)(2,1)S(1)}, u32[]{:S(2)}, u32[]{:S(2)}) collective-permute-start(bf16[2,272,128]{2,1,0:T(8,128)(2,1)S(1)} %get-tuple-element.38), channel_id=1, source_target_pairs={{0,4},{1,5},{2,6},{3,7},{4,0},{5,1},{6,2},{7,3},{8,12},{9,13},{10,... | collective-permute-start | bytes 417800 | tf_op jit(solution)/shard_map/ppermute | solution.py:359
  11.4 0.4 collective-permute-start.3
  11.8 0.7 collective-permute-done.4.refs_4_.refs_7_.refs_5_
  12.5 0.4 qg_pack.4
  13.0 1.0 %collective-permute-done.1.refs_4_.refs_2_ = bf16[2,272,128]{2,1,0:T(8,128)(2,1)S(1)} collective-permute-done((bf16[2,272,128]{2,1,0:T(8,128)(2,1)S(1)}, bf16[2,272,128]{2,1,0:T(8,128)(2,1)S(1)}, u32[]{:S(2)}, u32[]{:S(2)}) %collective-permute-start.1) | collective-permute-done | bytes 139296 | tf_op jit(solution)/shard_map/ppermute | solution.py:359
  14.0 2.4 %collective-permute-done.2.refs_5_.refs_3_ = bf16[2,272,128]{2,1,0:T(8,128)(2,1)S(1)} collective-permute-done((bf16[2,272,128]{2,1,0:T(8,128)(2,1)S(1)}, bf16[2,272,128]{2,1,0:T(8,128)(2,1)S(1)}, u32[]{:S(2)}, u32[]{:S(2)}) %collective-permute-start.2) | collective-permute-done | bytes 139296 | tf_op jit(solution)/shard_map/ppermute | solution.py:359
  16.4 1.7 %collective-permute-done.3.refs_6_.refs_4_ = bf16[2,272,128]{2,1,0:T(8,128)(2,1)S(1)} collective-permute-done((bf16[2,272,128]{2,1,0:T(8,128)(2,1)S(1)}, bf16[2,272,128]{2,1,0:T(8,128)(2,1)S(1)}, u32[]{:S(2)}, u32[]{:S(2)}) %collective-permute-start.3) | collective-permute-done | bytes 139296 | tf_op jit(solution)/shard_map/ppermute | solution.py:359
  18.2 2.6 %collective-permute-start.13 = (bf16[2,1328,128]{2,1,0:T(8,128)(2,1)S(1)}, bf16[2,1328,128]{2,1,0:T(8,128)(2,1)S(1)}, u32[]{:S(2)}, u32[]{:S(2)}) collective-permute-start(bf16[2,1328,128]{2,1,0:T(8,128)(2,1)S(1)} %pair_up.2), channel_id=1, source_target_pairs={{0,6},{1,7},{2,4},{3,5},{4,2},{5,3},{6,0},{7,1},{8,14},{9,15},{10,... | collective-permute-start | bytes 2039816 | tf_op jit(solution)/shard_map/ppermute | solution.py:359
  20.8 0.5 collective-permute-start.7
  21.3 1.5 %collective-permute-start.8 = (bf16[2,272,128]{2,1,0:T(8,128)(2,1)S(1)}, bf16[2,272,128]{2,1,0:T(8,128)(2,1)S(1)}, u32[]{:S(2)}, u32[]{:S(2)}) collective-permute-start(bf16[2,272,128]{2,1,0:T(8,128)(2,1)S(1)} %collective-permute-done.3.refs_6_.refs_4_), channel_id=1, source_target_pairs={{0,16},{16,0},{1,17},{17,1},{2,18},{18,2},{3,19},{19,3},{4,20},{20... | collective-permute-start | bytes 417800 | tf_op jit(solution)/shard_map/ppermute | solution.py:362
  22.8 0.5 collective-permute-start.6
  23.4 4.0 %collective-permute-done.7.refs_9_.refs_4_ = bf16[2,272,128]{2,1,0:T(8,128)(2,1)S(1)} collective-permute-done((bf16[2,272,128]{2,1,0:T(8,128)(2,1)S(1)}, bf16[2,272,128]{2,1,0:T(8,128)(2,1)S(1)}, u32[]{:S(2)}, u32[]{:S(2)}) %collective-permute-start.7) | collective-permute-done | bytes 139296 | tf_op jit(solution)/shard_map/ppermute | solution.py:362
  27.4 0.4 qg_pack.7
  27.8 0.5 collective-permute-start.11
  28.4 0.5 collective-permute-start.12
  28.8 0.7 collective-permute-done.8.refs_10_.refs_4_
  29.5 0.4 qg_pack.6
  29.9 1.1 %collective-permute-done.6.refs_8_ = bf16[2,272,128]{2,1,0:T(8,128)(2,1)S(1)} collective-permute-done((bf16[2,272,128]{2,1,0:T(8,128)(2,1)S(1)}, bf16[2,272,128]{2,1,0:T(8,128)(2,1)S(1)}, u32[]{:S(2)}, u32[]{:S(2)}) %collective-permute-start.6) | collective-permute-done | bytes 139296 | tf_op jit(solution)/shard_map/ppermute | solution.py:362
  31.0 1.1 %collective-permute-start.9 = (bf16[1,1328,128]{2,1,0:T(8,128)(2,1)S(1)}, bf16[1,1328,128]{2,1,0:T(8,128)(2,1)S(1)}, u32[]{:S(2)}, u32[]{:S(2)}) collective-permute-start(bf16[1,1328,128]{2,1,0:T(8,128)(2,1)S(1)} %get-tuple-element.42), channel_id=1, source_target_pairs={{0,3},{1,2},{2,1},{3,0},{4,7},{5,6},{6,5},{7,4},{8,11},{9,10},{10,... | collective-permute-start | bytes 1019912 | tf_op jit(solution)/shard_map/ppermute | solution.py:359
  32.1 2.8 %attend_0.1 = (bf16[2,640,128]{2,1,0:T(8,128)(2,1)S(1)}, bf16[17,128,128]{2,1,0:T(8,128)(2,1)S(1)}, bf16[17,128,128]{2,1,0:T(8,128)(2,1)S(1)}, bf16[17,128,128]{2,1,0:T(8,128)(2,1)S(1)}, f32[17,256,128]{2,1,0:T(8,128)S(1)}) custom-call(s32[8,34]{1,0:T(8,128)S(1)} %maximum_convert_fusion.refs_0_, bf16[1,1328,128]{2,1,0:T(8,128)(2,1)S(1)} %get-tuple-element.40.refs_1_, ...), custom_call_target="tpu_custom_call" | custom-call | flops 500000000 | bytes 1500000 | tf_op jit(solution)/shard_map/attend_0/pallas_call | solution.py:56
  35.0 2.4 %collective-permute-done.13.refs_1_ = bf16[2,1328,128]{2,1,0:T(8,128)(2,1)S(1)} collective-permute-done((bf16[2,1328,128]{2,1,0:T(8,128)(2,1)S(1)}, bf16[2,1328,128]{2,1,0:T(8,128)(2,1)S(1)}, u32[]{:S(2)}, u32[]{:S(2)}) %collective-permute-start.13) | collective-permute-done | bytes 679968 | tf_op jit(solution)/shard_map/ppermute | solution.py:359
  37.4 5.8 %attend_1.1 = (bf16[2,640,128]{2,1,0:T(8,128)(2,1)S(1)}, f32[17,256,128]{2,1,0:T(8,128)S(1)}) custom-call(s32[8,34]{1,0:T(8,128)S(1)} %maximum_convert_fusion.refs_0_, bf16[2,1328,128]{2,1,0:T(8,128)(2,1)S(1)} %collective-permute-done.13.refs_1_, bf16[17,128,128]{2,1,0:T(8,128)(2,1)S(1)} %get-tuple-element.44.refs_2_.refs_3_, ...), custom_call_target="tpu_custom_call" | custom-call | flops 500000000 | bytes 1500000 | tf_op jit(solution)/shard_map/attend_1/pallas_call | solution.py:56
  43.4 1.4 %collective-permute-done.12.refs_2_ = bf16[1,1328,128]{2,1,0:T(8,128)(2,1)S(1)} collective-permute-done((bf16[1,1328,128]{2,1,0:T(8,128)(2,1)S(1)}, bf16[1,1328,128]{2,1,0:T(8,128)(2,1)S(1)}, u32[]{:S(2)}, u32[]{:S(2)}) %collective-permute-start.12) | collective-permute-done | bytes 340000 | tf_op jit(solution)/shard_map/ppermute | solution.py:359
  44.8 5.2 %attend_2.1 = (bf16[2,640,128]{2,1,0:T(8,128)(2,1)S(1)}, f32[17,256,128]{2,1,0:T(8,128)S(1)}) custom-call(s32[8,34]{1,0:T(8,128)S(1)} %maximum_convert_fusion.refs_0_, bf16[1,1328,128]{2,1,0:T(8,128)(2,1)S(1)} %collective-permute-done.11.refs_1_, bf16[1,1328,128]{2,1,0:T(8,128)(2,1)S(1)} %collective-permute-done.12.refs_2_, ...), custom_call_target="tpu_custom_call" | custom-call | flops 500000000 | bytes 1500000 | tf_op jit(solution)/shard_map/attend_2/pallas_call | solution.py:56
  50.0 1.2 %collective-permute-done.10.refs_2_ = bf16[1,1328,128]{2,1,0:T(8,128)(2,1)S(1)} collective-permute-done((bf16[1,1328,128]{2,1,0:T(8,128)(2,1)S(1)}, bf16[1,1328,128]{2,1,0:T(8,128)(2,1)S(1)}, u32[]{:S(2)}, u32[]{:S(2)}) %collective-permute-start.10) | collective-permute-done | bytes 340000 | tf_op jit(solution)/shard_map/ppermute | solution.py:359
  51.1 0.6 collective-permute-done.9.refs_1_
  51.7 5.9 %attend_3.1 = (bf16[2,640,128]{2,1,0:T(8,128)(2,1)S(1)}, bf16[2,640,128]{2,1,0:T(8,128)(2,1)S(1)}, f32[4,256,128]{2,1,0:T(8,128)S(1)}, f32[4,256,128]{2,1,0:T(8,...) custom-call(s32[8,34]{1,0:T(8,128)S(1)} %maximum_convert_fusion.refs_0_, ...), custom_call_target="tpu_custom_call" | custom-call | flops 6000000000 | bytes 18000000 | tf_op jit(solution)/shard_map/attend_3/pallas_call | solution.py:56
  57.7 0.4 collective-permute-start.18
  58.1 1.7 %collective-permute-start.17 = (bf16[4,256,128]{2,1,0:T(8,128)(2,1)S(1)}, bf16[4,256,128]{2,1,0:T(8,128)(2,1)S(1)}, u32[]{:S(2)}, u32[]{:S(2)}) collective-permute-start(bf16[4,256,128]{2,1,0:T(8,128)(2,1)S(1)} %get-tuple-element.58), channel_id=1, source_target_pairs={{0,16},{16,0},{1,17},{17,1},{2,18},{18,2},{3,19},{19,3},{4,20},{20... | collective-permute-start | bytes 786440 | tf_op jit(solution)/shard_map/ppermute | solution.py:362
  59.8 0.8 collective-permute-start.14
  60.5 2.4 %collective-permute-start.15 = (bf16[2,640,128]{2,1,0:T(8,128)(2,1)S(1)}, bf16[2,640,128]{2,1,0:T(8,128)(2,1)S(1)}, u32[]{:S(2)}, u32[]{:S(2)}) collective-permute-start(bf16[2,640,128]{2,1,0:T(8,128)(2,1)S(1)} %get-tuple-element.55), channel_id=1, source_target_pairs={{0,4},{1,5},{2,6},{3,7},{4,0},{5,1},{6,2},{7,3},{8,12},{9,13},{10,... | collective-permute-start | bytes 983048 | tf_op jit(solution)/shard_map/ppermute | solution.py:359
  62.9 4.1 %collective-permute-done.18.refs_1_ = bf16[4,256,128]{2,1,0:T(8,128)(2,1)S(1)} collective-permute-done((bf16[4,256,128]{2,1,0:T(8,128)(2,1)S(1)}, bf16[4,256,128]{2,1,0:T(8,128)(2,1)S(1)}, u32[]{:S(2)}, u32[]{:S(2)}) %collective-permute-start.18) | collective-permute-done | bytes 262176 | tf_op jit(solution)/shard_map/ppermute | solution.py:362
  67.1 4.0 %collective-permute-done.17.refs_1_ = bf16[4,256,128]{2,1,0:T(8,128)(2,1)S(1)} collective-permute-done((bf16[4,256,128]{2,1,0:T(8,128)(2,1)S(1)}, bf16[4,256,128]{2,1,0:T(8,128)(2,1)S(1)}, u32[]{:S(2)}, u32[]{:S(2)}) %collective-permute-start.17) | collective-permute-done | bytes 262176 | tf_op jit(solution)/shard_map/ppermute | solution.py:362
  71.4 1.2 %collective-permute-start.21 = (bf16[2,256,128]{2,1,0:T(8,128)(2,1)S(1)}, bf16[2,256,128]{2,1,0:T(8,128)(2,1)S(1)}, u32[]{:S(2)}, u32[]{:S(2)}) collective-permute-start(bf16[2,256,128]{2,1,0:T(8,128)(2,1)S(1)} %get-tuple-element.63), channel_id=1, source_target_pairs={{0,2},{1,3},{2,0},{3,1},{4,6},{5,7},{6,4},{7,5},{8,10},{9,11},{10,... | collective-permute-start | bytes 393224 | tf_op jit(solution)/shard_map/ppermute | solution.py:359
  72.6 1.6 %collective-permute-start.22 = (bf16[2,256,128]{2,1,0:T(8,128)(2,1)S(1)}, bf16[2,256,128]{2,1,0:T(8,128)(2,1)S(1)}, u32[]{:S(2)}, u32[]{:S(2)}) collective-permute-start(bf16[2,256,128]{2,1,0:T(8,128)(2,1)S(1)} %get-tuple-element.64), channel_id=1, source_target_pairs={{0,4},{1,5},{2,6},{3,7},{4,0},{5,1},{6,2},{7,3},{8,12},{9,13},{10,... | collective-permute-start | bytes 393224 | tf_op jit(solution)/shard_map/ppermute | solution.py:359
  74.2 0.7 collective-permute-start.23
  74.9 1.4 %query_unpack.1 = (bf16[128,5120]{1,0:T(8,128)(2,1)}, f32[8,128]{1,0:T(8,128)S(1)}) custom-call(bf16[2,640,128]{2,1,0:T(8,128)(2,1)S(1)} %get-tuple-element.41.refs_0_, bf16[2,640,128]{2,1,0:T(8,128)(2,1)S(1)} %collective-permute-done.14.refs_1_, bf16[2,640,128]{2,1,0:T(8,128)(2,1)S(1)} %collective-permute-done.15.refs_2_, ...), custom_call_target="tpu_custom_call" | custom-call | flops 1000000000 | bytes 3000000 | tf_op jit(solution)/shard_map/query_unpack/pallas_call | solution.py:56
  76.3 0.9 %collective-permute-done.21.refs_1_ = bf16[2,256,128]{2,1,0:T(8,128)(2,1)S(1)} collective-permute-done((bf16[2,256,128]{2,1,0:T(8,128)(2,1)S(1)}, bf16[2,256,128]{2,1,0:T(8,128)(2,1)S(1)}, u32[]{:S(2)}, u32[]{:S(2)}) %collective-permute-start.21) | collective-permute-done | bytes 131104 | tf_op jit(solution)/shard_map/ppermute | solution.py:359
  77.3 1.7 %collective-permute-done.22.refs_2_ = bf16[2,256,128]{2,1,0:T(8,128)(2,1)S(1)} collective-permute-done((bf16[2,256,128]{2,1,0:T(8,128)(2,1)S(1)}, bf16[2,256,128]{2,1,0:T(8,128)(2,1)S(1)}, u32[]{:S(2)}, u32[]{:S(2)}) %collective-permute-start.22) | collective-permute-done | bytes 131104 | tf_op jit(solution)/shard_map/ppermute | solution.py:359
  78.9 2.3 %collective-permute-done.23.refs_3_ = bf16[2,256,128]{2,1,0:T(8,128)(2,1)S(1)} collective-permute-done((bf16[2,256,128]{2,1,0:T(8,128)(2,1)S(1)}, bf16[2,256,128]{2,1,0:T(8,128)(2,1)S(1)}, u32[]{:S(2)}, u32[]{:S(2)}) %collective-permute-start.23) | collective-permute-done | bytes 131104 | tf_op jit(solution)/shard_map/ppermute | solution.py:359
  81.3 0.9 %kv_unpack.1 = (bf16[128,1024]{1,0:T(8,128)(2,1)}, bf16[128,1024]{1,0:T(8,128)(2,1)}) custom-call(bf16[2,256,128]{2,1,0:T(8,128)(2,1)S(1)} %get-tuple-element.61.refs_4_.refs_0_, bf16[2,256,128]{2,1,0:T(8,128)(2,1)S(1)} %collective-permute-done.21.refs_1_, bf16[2,256,128]{2,1,0:T(8,128)(2,1)S(1)} %collective-permute-done.22.refs_2_, ...), custom_call_target="tpu_custom_call" | custom-call | flops 1000000000 | bytes 3000000 | tf_op jit(solution)/shard_map/kv_unpack/pallas_call | solution.py:56
  (42 shorter events, 0.7 us)
Async XLA Ops:
  0.6 4.1 %copy-start.6 = (s32[2,32]{1,0:T(2,128)S(1)}, s32[2,32]{1,0:T(2,128)}, u32[]{:S(2)}) copy-start(s32[2,32]{1,0:T(2,128)} %refs_2_.7) | copy-start | bytes 772
  0.6 4.1 %copy-start.4 = (bf16[128,1024]{1,0:T(8,128)(2,1)S(1)}, bf16[128,1024]{1,0:T(8,128)(2,1)}, u32[]{:S(2)}) copy-start(bf16[128,1024]{1,0:T(8,128)(2,1)} %refs_0_.7) | copy-start | bytes 786436
  0.7 4.0 %copy-start.5 = (bf16[128,1024]{1,0:T(8,128)(2,1)S(1)}, bf16[128,1024]{1,0:T(8,128)(2,1)}, u32[]{:S(2)}) copy-start(bf16[128,1024]{1,0:T(8,128)(2,1)} %refs_1_.7) | copy-start | bytes 786436
  0.7 4.2 %copy-start.1 = (bf16[128,5120]{1,0:T(8,128)(2,1)S(1)}, bf16[128,5120]{1,0:T(8,128)(2,1)}, u32[]{:S(2)}) copy-start(bf16[128,5120]{1,0:T(8,128)(2,1)} %refs_1_.11) | copy-start | bytes 3932164
  0.7 4.2 %copy-start.2 = (bf16[128,5120]{1,0:T(8,128)(2,1)S(1)}, bf16[128,5120]{1,0:T(8,128)(2,1)}, u32[]{:S(2)}) copy-start(bf16[128,5120]{1,0:T(8,128)(2,1)} %refs_2_.11) | copy-start | bytes 3932164
  2.7 2.1 %copy-start = (bf16[128,5120]{1,0:T(8,128)(2,1)S(1)}, bf16[128,5120]{1,0:T(8,128)(2,1)}, u32[]{:S(2)}) copy-start(bf16[128,5120]{1,0:T(8,128)(2,1)} %refs_0_.11) | copy-start | bytes 3932164
  2.8 2.1 %copy-start.3 = (f32[128,40]{0,1:T(8,128)S(1)}, f32[128,40]{0,1:T(8,128)}, u32[]{:S(2)}) copy-start(f32[128,40]{0,1:T(8,128)} %param.12) | copy-start | bytes 61444
  2.8 1.9 %collective-permute-start = (bf16[4,272,128]{2,1,0:T(8,128)(2,1)}, bf16[4,272,128]{2,1,0:T(8,128)(2,1)S(1)}, u32[]{:S(2)}, u32[]{:S(2)}) collective-permute-start(bf16[4,272,128]{2,1,0:T(8,128)(2,1)} %kv_pack.1), channel_id=1, source_target_pairs={{0,1},{1,0},{2,3},{3,2},{4,5},{5,4},{6,7},{7,6},{8,9},{9,8},{10,11... | collective-permute-start | bytes 835592 | tf_op jit(solution)/shard_map/ppermute | solution.py:359
  5.3 7.6 %collective-permute-start.5 = (bf16[2,1328,128]{2,1,0:T(8,128)(2,1)S(1)}, bf16[2,1328,128]{2,1,0:T(8,128)(2,1)S(1)}, u32[]{:S(2)}, u32[]{:S(2)}) collective-permute-start(bf16[2,1328,128]{2,1,0:T(8,128)(2,1)S(1)} %qg_pack.5), channel_id=1, source_target_pairs={{0,1},{1,0},{2,3},{3,2},{4,5},{5,4},{6,7},{7,6},{8,9},{9,8},{10,11... | collective-permute-start | bytes 2039816 | tf_op jit(solution)/shard_map/ppermute | solution.py:359
  5.7 6.8 %collective-permute-start.4 = (bf16[2,272,128]{2,1,0:T(8,128)(2,1)S(1)}, bf16[2,272,128]{2,1,0:T(8,128)(2,1)S(1)}, u32[]{:S(2)}, u32[]{:S(2)}) collective-permute-start(bf16[2,272,128]{2,1,0:T(8,128)(2,1)S(1)} %get-tuple-element.36.refs_3_), channel_id=1, source_target_pairs={{0,16},{16,0},{1,17},{17,1},{2,18},{18,2},{3,19},{19,3},{4,20},{20... | collective-permute-start | bytes 417800 | tf_op jit(solution)/shard_map/ppermute | solution.py:362
  8.3 5.7 %collective-permute-start.1 = (bf16[2,272,128]{2,1,0:T(8,128)(2,1)S(1)}, bf16[2,272,128]{2,1,0:T(8,128)(2,1)S(1)}, u32[]{:S(2)}, u32[]{:S(2)}) collective-permute-start(bf16[2,272,128]{2,1,0:T(8,128)(2,1)S(1)} %get-tuple-element.37.refs_4_), channel_id=1, source_target_pairs={{0,2},{1,3},{2,0},{3,1},{4,6},{5,7},{6,4},{7,5},{8,10},{9,11},{10,... | collective-permute-start | bytes 417800 | tf_op jit(solution)/shard_map/ppermute | solution.py:359
  9.9 6.6 %collective-permute-start.2 = (bf16[2,272,128]{2,1,0:T(8,128)(2,1)S(1)}, bf16[2,272,128]{2,1,0:T(8,128)(2,1)S(1)}, u32[]{:S(2)}, u32[]{:S(2)}) collective-permute-start(bf16[2,272,128]{2,1,0:T(8,128)(2,1)S(1)} %get-tuple-element.38), channel_id=1, source_target_pairs={{0,4},{1,5},{2,6},{3,7},{4,0},{5,1},{6,2},{7,3},{8,12},{9,13},{10,... | collective-permute-start | bytes 417800 | tf_op jit(solution)/shard_map/ppermute | solution.py:359
  11.4 6.7 %collective-permute-start.3 = (bf16[2,272,128]{2,1,0:T(8,128)(2,1)S(1)}, bf16[2,272,128]{2,1,0:T(8,128)(2,1)S(1)}, u32[]{:S(2)}, u32[]{:S(2)}) collective-permute-start(bf16[2,272,128]{2,1,0:T(8,128)(2,1)S(1)} %get-tuple-element.39), channel_id=1, source_target_pairs={{0,6},{1,7},{2,4},{3,5},{4,2},{5,3},{6,0},{7,1},{8,14},{9,15},{10,... | collective-permute-start | bytes 417800 | tf_op jit(solution)/shard_map/ppermute | solution.py:359
  18.2 19.2 %collective-permute-start.13 = (bf16[2,1328,128]{2,1,0:T(8,128)(2,1)S(1)}, bf16[2,1328,128]{2,1,0:T(8,128)(2,1)S(1)}, u32[]{:S(2)}, u32[]{:S(2)}) collective-permute-start(bf16[2,1328,128]{2,1,0:T(8,128)(2,1)S(1)} %pair_up.2), channel_id=1, source_target_pairs={{0,6},{1,7},{2,4},{3,5},{4,2},{5,3},{6,0},{7,1},{8,14},{9,15},{10,... | collective-permute-start | bytes 2039816 | tf_op jit(solution)/shard_map/ppermute | solution.py:359
  20.8 6.6 %collective-permute-start.7 = (bf16[2,272,128]{2,1,0:T(8,128)(2,1)S(1)}, bf16[2,272,128]{2,1,0:T(8,128)(2,1)S(1)}, u32[]{:S(2)}, u32[]{:S(2)}) collective-permute-start(bf16[2,272,128]{2,1,0:T(8,128)(2,1)S(1)} %collective-permute-done.2.refs_5_.refs_3_), channel_id=1, source_target_pairs={{0,16},{16,0},{1,17},{17,1},{2,18},{18,2},{3,19},{19,3},{4,20},{20... | collective-permute-start | bytes 417800 | tf_op jit(solution)/shard_map/ppermute | solution.py:362
  21.3 8.2 %collective-permute-start.8 = (bf16[2,272,128]{2,1,0:T(8,128)(2,1)S(1)}, bf16[2,272,128]{2,1,0:T(8,128)(2,1)S(1)}, u32[]{:S(2)}, u32[]{:S(2)}) collective-permute-start(bf16[2,272,128]{2,1,0:T(8,128)(2,1)S(1)} %collective-permute-done.3.refs_6_.refs_4_), channel_id=1, source_target_pairs={{0,16},{16,0},{1,17},{17,1},{2,18},{18,2},{3,19},{19,3},{4,20},{20... | collective-permute-start | bytes 417800 | tf_op jit(solution)/shard_map/ppermute | solution.py:362
  22.8 8.2 %collective-permute-start.6 = (bf16[2,272,128]{2,1,0:T(8,128)(2,1)S(1)}, bf16[2,272,128]{2,1,0:T(8,128)(2,1)S(1)}, u32[]{:S(2)}, u32[]{:S(2)}) collective-permute-start(bf16[2,272,128]{2,1,0:T(8,128)(2,1)S(1)} %collective-permute-done.1.refs_4_.refs_2_), channel_id=1, source_target_pairs={{0,16},{16,0},{1,17},{17,1},{2,18},{18,2},{3,19},{19,3},{4,20},{20... | collective-permute-start | bytes 417800 | tf_op jit(solution)/shard_map/ppermute | solution.py:362
  27.8 15.5 %collective-permute-start.11 = (bf16[1,1328,128]{2,1,0:T(8,128)(2,1)S(1)}, bf16[1,1328,128]{2,1,0:T(8,128)(2,1)S(1)}, u32[]{:S(2)}, u32[]{:S(2)}) collective-permute-start(bf16[1,1328,128]{2,1,0:T(8,128)(2,1)S(1)} %get-tuple-element.47), channel_id=1, source_target_pairs={{0,2},{1,3},{2,0},{3,1},{4,6},{5,7},{6,4},{7,5},{8,10},{9,11},{10,... | collective-permute-start | bytes 1019912 | tf_op jit(solution)/shard_map/ppermute | solution.py:359
  28.4 16.4 %collective-permute-start.12 = (bf16[1,1328,128]{2,1,0:T(8,128)(2,1)S(1)}, bf16[1,1328,128]{2,1,0:T(8,128)(2,1)S(1)}, u32[]{:S(2)}, u32[]{:S(2)}) collective-permute-start(bf16[1,1328,128]{2,1,0:T(8,128)(2,1)S(1)} %get-tuple-element.48), channel_id=1, source_target_pairs={{0,4},{1,5},{2,6},{3,7},{4,0},{5,1},{6,2},{7,3},{8,12},{9,13},{10,... | collective-permute-start | bytes 1019912 | tf_op jit(solution)/shard_map/ppermute | solution.py:359
  29.9 21.2 %collective-permute-start.10 = (bf16[1,1328,128]{2,1,0:T(8,128)(2,1)S(1)}, bf16[1,1328,128]{2,1,0:T(8,128)(2,1)S(1)}, u32[]{:S(2)}, u32[]{:S(2)}) collective-permute-start(bf16[1,1328,128]{2,1,0:T(8,128)(2,1)S(1)} %get-tuple-element.43), channel_id=1, source_target_pairs={{0,5},{1,4},{2,7},{3,6},{4,1},{5,0},{6,3},{7,2},{8,13},{9,12},{10,... | collective-permute-start | bytes 1019912 | tf_op jit(solution)/shard_map/ppermute | solution.py:359
  31.0 20.7 %collective-permute-start.9 = (bf16[1,1328,128]{2,1,0:T(8,128)(2,1)S(1)}, bf16[1,1328,128]{2,1,0:T(8,128)(2,1)S(1)}, u32[]{:S(2)}, u32[]{:S(2)}) collective-permute-start(bf16[1,1328,128]{2,1,0:T(8,128)(2,1)S(1)} %get-tuple-element.42), channel_id=1, source_target_pairs={{0,3},{1,2},{2,1},{3,0},{4,7},{5,6},{6,5},{7,4},{8,11},{9,10},{10,... | collective-permute-start | bytes 1019912 | tf_op jit(solution)/shard_map/ppermute | solution.py:359
  43.3 14.4 %collective-permute-start.16 = (bf16[2,640,128]{2,1,0:T(8,128)(2,1)S(1)}, bf16[2,640,128]{2,1,0:T(8,128)(2,1)S(1)}, u32[]{:S(2)}, u32[]{:S(2)}) collective-permute-start(bf16[2,640,128]{2,1,0:T(8,128)(2,1)S(1)} %get-tuple-element.56), channel_id=1, source_target_pairs={{0,6},{1,7},{2,4},{3,5},{4,2},{5,3},{6,0},{7,1},{8,14},{9,15},{10,... | collective-permute-start | bytes 983048 | tf_op jit(solution)/shard_map/ppermute | solution.py:359
  57.7 9.3 %collective-permute-start.18 = (bf16[4,256,128]{2,1,0:T(8,128)(2,1)S(1)}, bf16[4,256,128]{2,1,0:T(8,128)(2,1)S(1)}, u32[]{:S(2)}, u32[]{:S(2)}) collective-permute-start(bf16[4,256,128]{2,1,0:T(8,128)(2,1)S(1)} %pass_on.1), channel_id=1, source_target_pairs={{0,16},{16,0},{1,17},{17,1},{2,18},{18,2},{3,19},{19,3},{4,20},{20... | collective-permute-start | bytes 786440 | tf_op jit(solution)/shard_map/ppermute | solution.py:362
  58.1 13.0 %collective-permute-start.17 = (bf16[4,256,128]{2,1,0:T(8,128)(2,1)S(1)}, bf16[4,256,128]{2,1,0:T(8,128)(2,1)S(1)}, u32[]{:S(2)}, u32[]{:S(2)}) collective-permute-start(bf16[4,256,128]{2,1,0:T(8,128)(2,1)S(1)} %get-tuple-element.58), channel_id=1, source_target_pairs={{0,16},{16,0},{1,17},{17,1},{2,18},{18,2},{3,19},{19,3},{4,20},{20... | collective-permute-start | bytes 786440 | tf_op jit(solution)/shard_map/ppermute | solution.py:362
  59.8 11.4 %collective-permute-start.14 = (bf16[2,640,128]{2,1,0:T(8,128)(2,1)S(1)}, bf16[2,640,128]{2,1,0:T(8,128)(2,1)S(1)}, u32[]{:S(2)}, u32[]{:S(2)}) collective-permute-start(bf16[2,640,128]{2,1,0:T(8,128)(2,1)S(1)} %get-tuple-element.54), channel_id=1, source_target_pairs={{0,2},{1,3},{2,0},{3,1},{4,6},{5,7},{6,4},{7,5},{8,10},{9,11},{10,... | collective-permute-start | bytes 983048 | tf_op jit(solution)/shard_map/ppermute | solution.py:359
  60.5 10.7 %collective-permute-start.15 = (bf16[2,640,128]{2,1,0:T(8,128)(2,1)S(1)}, bf16[2,640,128]{2,1,0:T(8,128)(2,1)S(1)}, u32[]{:S(2)}, u32[]{:S(2)}) collective-permute-start(bf16[2,640,128]{2,1,0:T(8,128)(2,1)S(1)} %get-tuple-element.55), channel_id=1, source_target_pairs={{0,4},{1,5},{2,6},{3,7},{4,0},{5,1},{6,2},{7,3},{8,12},{9,13},{10,... | collective-permute-start | bytes 983048 | tf_op jit(solution)/shard_map/ppermute | solution.py:359
  67.0 4.1 %collective-permute-start.19 = (bf16[4,256,128]{2,1,0:T(8,128)(2,1)S(1)}, bf16[4,256,128]{2,1,0:T(8,128)(2,1)S(1)}, u32[]{:S(2)}, u32[]{:S(2)}) collective-permute-start(bf16[4,256,128]{2,1,0:T(8,128)(2,1)S(1)} %kv_sum.3), channel_id=1, source_target_pairs={{0,1},{1,0},{2,3},{3,2},{4,5},{5,4},{6,7},{7,6},{8,9},{9,8},{10,11... | collective-permute-start | bytes 786440 | tf_op jit(solution)/shard_map/ppermute | solution.py:359
  71.3 3.6 %collective-permute-start.20 = (bf16[4,640,128]{2,1,0:T(8,128)(2,1)S(1)}, bf16[4,640,128]{2,1,0:T(8,128)(2,1)S(1)}, u32[]{:S(2)}, u32[]{:S(2)}) collective-permute-start(bf16[4,640,128]{2,1,0:T(8,128)(2,1)S(1)} %query_relay.1), channel_id=1, source_target_pairs={{0,1},{1,0},{2,3},{3,2},{4,5},{5,4},{6,7},{7,6},{8,9},{9,8},{10,11... | collective-permute-start | bytes 1966088 | tf_op jit(solution)/shard_map/ppermute | solution.py:359
  71.4 5.9 %collective-permute-start.21 = (bf16[2,256,128]{2,1,0:T(8,128)(2,1)S(1)}, bf16[2,256,128]{2,1,0:T(8,128)(2,1)S(1)}, u32[]{:S(2)}, u32[]{:S(2)}) collective-permute-start(bf16[2,256,128]{2,1,0:T(8,128)(2,1)S(1)} %get-tuple-element.63), channel_id=1, source_target_pairs={{0,2},{1,3},{2,0},{3,1},{4,6},{5,7},{6,4},{7,5},{8,10},{9,11},{10,... | collective-permute-start | bytes 393224 | tf_op jit(solution)/shard_map/ppermute | solution.py:359
  72.6 6.3 %collective-permute-start.22 = (bf16[2,256,128]{2,1,0:T(8,128)(2,1)S(1)}, bf16[2,256,128]{2,1,0:T(8,128)(2,1)S(1)}, u32[]{:S(2)}, u32[]{:S(2)}) collective-permute-start(bf16[2,256,128]{2,1,0:T(8,128)(2,1)S(1)} %get-tuple-element.64), channel_id=1, source_target_pairs={{0,4},{1,5},{2,6},{3,7},{4,0},{5,1},{6,2},{7,3},{8,12},{9,13},{10,... | collective-permute-start | bytes 393224 | tf_op jit(solution)/shard_map/ppermute | solution.py:359
  74.2 7.1 %collective-permute-start.23 = (bf16[2,256,128]{2,1,0:T(8,128)(2,1)S(1)}, bf16[2,256,128]{2,1,0:T(8,128)(2,1)S(1)}, u32[]{:S(2)}, u32[]{:S(2)}) collective-permute-start(bf16[2,256,128]{2,1,0:T(8,128)(2,1)S(1)} %get-tuple-element.65), channel_id=1, source_target_pairs={{0,6},{1,7},{2,4},{3,5},{4,2},{5,3},{6,0},{7,1},{8,14},{9,15},{10,... | collective-permute-start | bytes 393224 | tf_op jit(solution)/shard_map/ppermute | solution.py:359

commit v6 on v5

--- a/solution.py
+++ b/solution.py
@@ -348,7 +348,7 @@
 CHIPS = (0, 2, 4, 6)
 VISITS = (("first", (0, 1)), ("more", (6, 7)), ("more", (2, 4)), ("last", (3, 5)))
 EXPECTED = (0.5, 0.5, 0.5, 6)
-WIDTHS = (2, 4, 2, 4)
+WIDTHS = (2, 2, 2, 4)
 BACK_HALVES = ((1, 3, 5, 7), CHIPS)
 
 

time: 82.3 us -> 83 us (level)
  Pallas kernels: 26.3 us -> 28.8 us
  waiting for transfers between devices: 31.6 us -> 29.3 us
    pallas_call x18, Pallas kernels: 26.3 us -> 28.8 us  [call(): pl.pallas_call(body, name=name, in_specs=[*in_specs, *[pl.BlockSpec(memor...]
    ppermute x18, waiting for transfers between devices: 17.1 us -> 14.7 us  [exchanged(): return lax.ppermute(array, 'blk', [(i, i ^ k) for i in range(size)])]
  transfers between devices with their start and end apart: 24 -> 24, of which waited for: 17 -> 16; matrix products, arithmetic and copies ran while one was open for 0% -> 0% of each run, Pallas kernels for 28% -> 31%
where the time goes in v6:
time: 83 us; the launch traced here: 82.4 us
  waiting for transfers between devices  29.3 us (35%)
  Pallas kernels  28.8 us (35%)
  starting transfers between devices  23.2 us (28%)
  between operations  0.93 us (1%)
    pallas_call x18, Pallas kernels, call(): pl.pallas_call(body, name=name, in_specs=[*in_specs, *[pl.BlockSpec(memor...  28.8 us
    ppermute x18, starting transfers between devices, exchanged(): return lax.ppermute(array, 'blk', [(i, i ^ k) for i in range(size)])  15.9 us
    ppermute x18, waiting for transfers between devices, exchanged(): return lax.ppermute(array, 'blk', [(i, i ^ k) for i in range(size)])  14.7 us
    ppermute x6, waiting for transfers between devices, swapped(): return lax.ppermute(array, 'head', [(0, 1), (1, 0)])  14.6 us
    ppermute x6, starting transfers between devices, swapped(): return lax.ppermute(array, 'head', [(0, 1), (1, 0)])  7.29 us
  transfers between devices with their start and end apart: 24, of which 16 were waited for; matrix products, arithmetic and copies ran while one was open for 0% of the time, Pallas kernels for 31%

profile of v6, /device:TPU:0, one launch (start us, length us, event | category | flops | bytes accessed | tf_op | source)
XLA Modules:
  0.0 82.4 jit_solution(10533547605913024386)
XLA Ops:
  0.7 2.1 %kv_pack.1 = bf16[4,272,128]{2,1,0:T(8,128)(2,1)} custom-call(bf16[128,1024]{1,0:T(8,128)(2,1)} %refs_0_.7, bf16[128,1024]{1,0:T(8,128)(2,1)} %refs_1_.7, s32[2,32]{1,0:T(2,128)} %refs_2_.7), custom_call_target="tpu_custom_call" | custom-call | flops 1000000000 | bytes 3000000 | tf_op jit(solution)/shard_map/kv_pack/pallas_call | solution.py:56
  2.8 0.5 collective-permute-start
  3.3 1.4 %collective-permute-done.refs_3_ = bf16[4,272,128]{2,1,0:T(8,128)(2,1)S(1)} collective-permute-done((bf16[4,272,128]{2,1,0:T(8,128)(2,1)}, bf16[4,272,128]{2,1,0:T(8,128)(2,1)S(1)}, u32[]{:S(2)}, u32[]{:S(2)}) %collective-permute-start) | collective-permute-done | bytes 278560 | tf_op jit(solution)/shard_map/ppermute | solution.py:359
  4.7 0.1 kv_pair.1
  4.9 0.4 qg_pack.5
  5.3 0.4 collective-permute-start.5
  5.7 2.6 %collective-permute-start.4 = (bf16[2,272,128]{2,1,0:T(8,128)(2,1)S(1)}, bf16[2,272,128]{2,1,0:T(8,128)(2,1)S(1)}, u32[]{:S(2)}, u32[]{:S(2)}) collective-permute-start(bf16[2,272,128]{2,1,0:T(8,128)(2,1)S(1)} %get-tuple-element.36.refs_3_), channel_id=1, source_target_pairs={{0,16},{16,0},{1,17},{17,1},{2,18},{18,2},{3,19},{19,3},{4,20},{20... | collective-permute-start | bytes 417800 | tf_op jit(solution)/shard_map/ppermute | solution.py:362
  8.3 1.5 %collective-permute-start.1 = (bf16[2,272,128]{2,1,0:T(8,128)(2,1)S(1)}, bf16[2,272,128]{2,1,0:T(8,128)(2,1)S(1)}, u32[]{:S(2)}, u32[]{:S(2)}) collective-permute-start(bf16[2,272,128]{2,1,0:T(8,128)(2,1)S(1)} %get-tuple-element.37.refs_4_), channel_id=1, source_target_pairs={{0,2},{1,3},{2,0},{3,1},{4,6},{5,7},{6,4},{7,5},{8,10},{9,11},{10,... | collective-permute-start | bytes 417800 | tf_op jit(solution)/shard_map/ppermute | solution.py:359
  9.9 1.6 %collective-permute-start.2 = (bf16[2,272,128]{2,1,0:T(8,128)(2,1)S(1)}, bf16[2,272,128]{2,1,0:T(8,128)(2,1)S(1)}, u32[]{:S(2)}, u32[]{:S(2)}) collective-permute-start(bf16[2,272,128]{2,1,0:T(8,128)(2,1)S(1)} %get-tuple-element.38), channel_id=1, source_target_pairs={{0,4},{1,5},{2,6},{3,7},{4,0},{5,1},{6,2},{7,3},{8,12},{9,13},{10,... | collective-permute-start | bytes 417800 | tf_op jit(solution)/shard_map/ppermute | solution.py:359
  11.4 0.4 collective-permute-start.3
  11.8 0.7 collective-permute-done.4.refs_4_.refs_7_.refs_5_
  12.5 0.4 qg_pack.4
  13.0 1.0 %collective-permute-done.1.refs_4_.refs_2_ = bf16[2,272,128]{2,1,0:T(8,128)(2,1)S(1)} collective-permute-done((bf16[2,272,128]{2,1,0:T(8,128)(2,1)S(1)}, bf16[2,272,128]{2,1,0:T(8,128)(2,1)S(1)}, u32[]{:S(2)}, u32[]{:S(2)}) %collective-permute-start.1) | collective-permute-done | bytes 139296 | tf_op jit(solution)/shard_map/ppermute | solution.py:359
  14.0 2.4 %collective-permute-done.2.refs_5_.refs_3_ = bf16[2,272,128]{2,1,0:T(8,128)(2,1)S(1)} collective-permute-done((bf16[2,272,128]{2,1,0:T(8,128)(2,1)S(1)}, bf16[2,272,128]{2,1,0:T(8,128)(2,1)S(1)}, u32[]{:S(2)}, u32[]{:S(2)}) %collective-permute-start.2) | collective-permute-done | bytes 139296 | tf_op jit(solution)/shard_map/ppermute | solution.py:359
  16.4 1.7 %collective-permute-done.3.refs_6_.refs_4_ = bf16[2,272,128]{2,1,0:T(8,128)(2,1)S(1)} collective-permute-done((bf16[2,272,128]{2,1,0:T(8,128)(2,1)S(1)}, bf16[2,272,128]{2,1,0:T(8,128)(2,1)S(1)}, u32[]{:S(2)}, u32[]{:S(2)}) %collective-permute-start.3) | collective-permute-done | bytes 139296 | tf_op jit(solution)/shard_map/ppermute | solution.py:359
  18.2 2.6 %collective-permute-start.13 = (bf16[2,1328,128]{2,1,0:T(8,128)(2,1)S(1)}, bf16[2,1328,128]{2,1,0:T(8,128)(2,1)S(1)}, u32[]{:S(2)}, u32[]{:S(2)}) collective-permute-start(bf16[2,1328,128]{2,1,0:T(8,128)(2,1)S(1)} %pair_up.2), channel_id=1, source_target_pairs={{0,6},{1,7},{2,4},{3,5},{4,2},{5,3},{6,0},{7,1},{8,14},{9,15},{10,... | collective-permute-start | bytes 2039816 | tf_op jit(solution)/shard_map/ppermute | solution.py:359
  20.8 0.5 collective-permute-start.7
  21.3 1.5 %collective-permute-start.8 = (bf16[2,272,128]{2,1,0:T(8,128)(2,1)S(1)}, bf16[2,272,128]{2,1,0:T(8,128)(2,1)S(1)}, u32[]{:S(2)}, u32[]{:S(2)}) collective-permute-start(bf16[2,272,128]{2,1,0:T(8,128)(2,1)S(1)} %collective-permute-done.3.refs_6_.refs_4_), channel_id=1, source_target_pairs={{0,16},{16,0},{1,17},{17,1},{2,18},{18,2},{3,19},{19,3},{4,20},{20... | collective-permute-start | bytes 417800 | tf_op jit(solution)/shard_map/ppermute | solution.py:362
  22.8 0.5 collective-permute-start.6
  23.4 4.0 %collective-permute-done.7.refs_9_.refs_4_ = bf16[2,272,128]{2,1,0:T(8,128)(2,1)S(1)} collective-permute-done((bf16[2,272,128]{2,1,0:T(8,128)(2,1)S(1)}, bf16[2,272,128]{2,1,0:T(8,128)(2,1)S(1)}, u32[]{:S(2)}, u32[]{:S(2)}) %collective-permute-start.7) | collective-permute-done | bytes 139296 | tf_op jit(solution)/shard_map/ppermute | solution.py:362
  27.4 0.4 qg_pack.7
  27.8 0.5 collective-permute-start.11
  28.4 0.5 collective-permute-start.12
  28.8 0.7 collective-permute-done.8.refs_10_.refs_4_
  29.5 0.4 qg_pack.6
  29.9 1.1 %collective-permute-done.6.refs_8_ = bf16[2,272,128]{2,1,0:T(8,128)(2,1)S(1)} collective-permute-done((bf16[2,272,128]{2,1,0:T(8,128)(2,1)S(1)}, bf16[2,272,128]{2,1,0:T(8,128)(2,1)S(1)}, u32[]{:S(2)}, u32[]{:S(2)}) %collective-permute-start.6) | collective-permute-done | bytes 139296 | tf_op jit(solution)/shard_map/ppermute | solution.py:362
  31.0 1.1 %collective-permute-start.9 = (bf16[1,1328,128]{2,1,0:T(8,128)(2,1)S(1)}, bf16[1,1328,128]{2,1,0:T(8,128)(2,1)S(1)}, u32[]{:S(2)}, u32[]{:S(2)}) collective-permute-start(bf16[1,1328,128]{2,1,0:T(8,128)(2,1)S(1)} %get-tuple-element.42), channel_id=1, source_target_pairs={{0,3},{1,2},{2,1},{3,0},{4,7},{5,6},{6,5},{7,4},{8,11},{9,10},{10,... | collective-permute-start | bytes 1019912 | tf_op jit(solution)/shard_map/ppermute | solution.py:359
  32.1 2.8 %attend_0.1 = (bf16[2,640,128]{2,1,0:T(8,128)(2,1)S(1)}, bf16[17,128,128]{2,1,0:T(8,128)(2,1)S(1)}, bf16[17,128,128]{2,1,0:T(8,128)(2,1)S(1)}, bf16[17,128,128]{2,1,0:T(8,128)(2,1)S(1)}, f32[17,256,128]{2,1,0:T(8,128)S(1)}) custom-call(s32[8,34]{1,0:T(8,128)S(1)} %maximum_convert_fusion.refs_0_, bf16[1,1328,128]{2,1,0:T(8,128)(2,1)S(1)} %get-tuple-element.40.refs_1_, ...), custom_call_target="tpu_custom_call" | custom-call | flops 500000000 | bytes 1500000 | tf_op jit(solution)/shard_map/attend_0/pallas_call | solution.py:56
  35.0 2.4 %collective-permute-done.13.refs_1_ = bf16[2,1328,128]{2,1,0:T(8,128)(2,1)S(1)} collective-permute-done((bf16[2,1328,128]{2,1,0:T(8,128)(2,1)S(1)}, bf16[2,1328,128]{2,1,0:T(8,128)(2,1)S(1)}, u32[]{:S(2)}, u32[]{:S(2)}) %collective-permute-start.13) | collective-permute-done | bytes 679968 | tf_op jit(solution)/shard_map/ppermute | solution.py:359
  37.4 8.4 %attend_1.1 = (bf16[2,640,128]{2,1,0:T(8,128)(2,1)S(1)}, f32[17,256,128]{2,1,0:T(8,128)S(1)}) custom-call(s32[8,34]{1,0:T(8,128)S(1)} %maximum_convert_fusion.refs_0_, bf16[2,1328,128]{2,1,0:T(8,128)(2,1)S(1)} %collective-permute-done.13.refs_1_, bf16[17,128,128]{2,1,0:T(8,128)(2,1)S(1)} %get-tuple-element.44.refs_2_.refs_3_, ...), custom_call_target="tpu_custom_call" | custom-call | flops 500000000 | bytes 1500000 | tf_op jit(solution)/shard_map/attend_1/pallas_call | solution.py:56
  45.9 5.0 %attend_2.1 = (bf16[2,640,128]{2,1,0:T(8,128)(2,1)S(1)}, f32[17,256,128]{2,1,0:T(8,128)S(1)}) custom-call(s32[8,34]{1,0:T(8,128)S(1)} %maximum_convert_fusion.refs_0_, bf16[1,1328,128]{2,1,0:T(8,128)(2,1)S(1)} %collective-permute-done.11.refs_1_, bf16[1,1328,128]{2,1,0:T(8,128)(2,1)S(1)} %collective-permute-done.12.refs_2_, ...), custom_call_target="tpu_custom_call" | custom-call | flops 500000000 | bytes 1500000 | tf_op jit(solution)/shard_map/attend_2/pallas_call | solution.py:56
  50.9 0.2 collective-permute-done.10.refs_2_
  51.1 0.6 collective-permute-done.9.refs_1_
  51.7 6.1 %attend_3.1 = (bf16[2,640,128]{2,1,0:T(8,128)(2,1)S(1)}, bf16[2,640,128]{2,1,0:T(8,128)(2,1)S(1)}, f32[4,256,128]{2,1,0:T(8,128)S(1)}, f32[4,256,128]{2,1,0:T(8,...) custom-call(s32[8,34]{1,0:T(8,128)S(1)} %maximum_convert_fusion.refs_0_, ...), custom_call_target="tpu_custom_call" | custom-call | flops 6000000000 | bytes 18000000 | tf_op jit(solution)/shard_map/attend_3/pallas_call | solution.py:56
  57.9 0.4 collective-permute-start.18
  58.3 1.7 %collective-permute-start.17 = (bf16[4,256,128]{2,1,0:T(8,128)(2,1)S(1)}, bf16[4,256,128]{2,1,0:T(8,128)(2,1)S(1)}, u32[]{:S(2)}, u32[]{:S(2)}) collective-permute-start(bf16[4,256,128]{2,1,0:T(8,128)(2,1)S(1)} %get-tuple-element.58), channel_id=1, source_target_pairs={{0,16},{16,0},{1,17},{17,1},{2,18},{18,2},{3,19},{19,3},{4,20},{20... | collective-permute-start | bytes 786440 | tf_op jit(solution)/shard_map/ppermute | solution.py:362
  60.0 1.5 %collective-permute-start.14 = (bf16[2,640,128]{2,1,0:T(8,128)(2,1)S(1)}, bf16[2,640,128]{2,1,0:T(8,128)(2,1)S(1)}, u32[]{:S(2)}, u32[]{:S(2)}) collective-permute-start(bf16[2,640,128]{2,1,0:T(8,128)(2,1)S(1)} %get-tuple-element.54), channel_id=1, source_target_pairs={{0,2},{1,3},{2,0},{3,1},{4,6},{5,7},{6,4},{7,5},{8,10},{9,11},{10,... | collective-permute-start | bytes 983048 | tf_op jit(solution)/shard_map/ppermute | solution.py:359
  61.5 1.6 %collective-permute-start.15 = (bf16[2,640,128]{2,1,0:T(8,128)(2,1)S(1)}, bf16[2,640,128]{2,1,0:T(8,128)(2,1)S(1)}, u32[]{:S(2)}, u32[]{:S(2)}) collective-permute-start(bf16[2,640,128]{2,1,0:T(8,128)(2,1)S(1)} %get-tuple-element.55), channel_id=1, source_target_pairs={{0,4},{1,5},{2,6},{3,7},{4,0},{5,1},{6,2},{7,3},{8,12},{9,13},{10,... | collective-permute-start | bytes 983048 | tf_op jit(solution)/shard_map/ppermute | solution.py:359
  63.1 4.1 %collective-permute-done.18.refs_1_ = bf16[4,256,128]{2,1,0:T(8,128)(2,1)S(1)} collective-permute-done((bf16[4,256,128]{2,1,0:T(8,128)(2,1)S(1)}, bf16[4,256,128]{2,1,0:T(8,128)(2,1)S(1)}, u32[]{:S(2)}, u32[]{:S(2)}) %collective-permute-start.18) | collective-permute-done | bytes 262176 | tf_op jit(solution)/shard_map/ppermute | solution.py:362
  67.3 4.0 %collective-permute-done.17.refs_1_ = bf16[4,256,128]{2,1,0:T(8,128)(2,1)S(1)} collective-permute-done((bf16[4,256,128]{2,1,0:T(8,128)(2,1)S(1)}, bf16[4,256,128]{2,1,0:T(8,128)(2,1)S(1)}, u32[]{:S(2)}, u32[]{:S(2)}) %collective-permute-start.17) | collective-permute-done | bytes 262176 | tf_op jit(solution)/shard_map/ppermute | solution.py:362
  71.5 1.2 %collective-permute-start.21 = (bf16[2,256,128]{2,1,0:T(8,128)(2,1)S(1)}, bf16[2,256,128]{2,1,0:T(8,128)(2,1)S(1)}, u32[]{:S(2)}, u32[]{:S(2)}) collective-permute-start(bf16[2,256,128]{2,1,0:T(8,128)(2,1)S(1)} %get-tuple-element.63), channel_id=1, source_target_pairs={{0,2},{1,3},{2,0},{3,1},{4,6},{5,7},{6,4},{7,5},{8,10},{9,11},{10,... | collective-permute-start | bytes 393224 | tf_op jit(solution)/shard_map/ppermute | solution.py:359
  72.8 1.6 %collective-permute-start.22 = (bf16[2,256,128]{2,1,0:T(8,128)(2,1)S(1)}, bf16[2,256,128]{2,1,0:T(8,128)(2,1)S(1)}, u32[]{:S(2)}, u32[]{:S(2)}) collective-permute-start(bf16[2,256,128]{2,1,0:T(8,128)(2,1)S(1)} %get-tuple-element.64), channel_id=1, source_target_pairs={{0,4},{1,5},{2,6},{3,7},{4,0},{5,1},{6,2},{7,3},{8,12},{9,13},{10,... | collective-permute-start | bytes 393224 | tf_op jit(solution)/shard_map/ppermute | solution.py:359
  74.3 0.7 collective-permute-start.23
  75.1 1.4 %query_unpack.1 = (bf16[128,5120]{1,0:T(8,128)(2,1)}, f32[8,128]{1,0:T(8,128)S(1)}) custom-call(bf16[2,640,128]{2,1,0:T(8,128)(2,1)S(1)} %get-tuple-element.41.refs_0_, bf16[2,640,128]{2,1,0:T(8,128)(2,1)S(1)} %collective-permute-done.14.refs_1_, bf16[2,640,128]{2,1,0:T(8,128)(2,1)S(1)} %collective-permute-done.15.refs_2_, ...), custom_call_target="tpu_custom_call" | custom-call | flops 1000000000 | bytes 3000000 | tf_op jit(solution)/shard_map/query_unpack/pallas_call | solution.py:56
  76.5 0.9 %collective-permute-done.21.refs_1_ = bf16[2,256,128]{2,1,0:T(8,128)(2,1)S(1)} collective-permute-done((bf16[2,256,128]{2,1,0:T(8,128)(2,1)S(1)}, bf16[2,256,128]{2,1,0:T(8,128)(2,1)S(1)}, u32[]{:S(2)}, u32[]{:S(2)}) %collective-permute-start.21) | collective-permute-done | bytes 131104 | tf_op jit(solution)/shard_map/ppermute | solution.py:359
  77.4 1.7 %collective-permute-done.22.refs_2_ = bf16[2,256,128]{2,1,0:T(8,128)(2,1)S(1)} collective-permute-done((bf16[2,256,128]{2,1,0:T(8,128)(2,1)S(1)}, bf16[2,256,128]{2,1,0:T(8,128)(2,1)S(1)}, u32[]{:S(2)}, u32[]{:S(2)}) %collective-permute-start.22) | collective-permute-done | bytes 131104 | tf_op jit(solution)/shard_map/ppermute | solution.py:359
  79.1 2.3 %collective-permute-done.23.refs_3_ = bf16[2,256,128]{2,1,0:T(8,128)(2,1)S(1)} collective-permute-done((bf16[2,256,128]{2,1,0:T(8,128)(2,1)S(1)}, bf16[2,256,128]{2,1,0:T(8,128)(2,1)S(1)}, u32[]{:S(2)}, u32[]{:S(2)}) %collective-permute-start.23) | collective-permute-done | bytes 131104 | tf_op jit(solution)/shard_map/ppermute | solution.py:359
  81.4 0.9 %kv_unpack.1 = (bf16[128,1024]{1,0:T(8,128)(2,1)}, bf16[128,1024]{1,0:T(8,128)(2,1)}) custom-call(bf16[2,256,128]{2,1,0:T(8,128)(2,1)S(1)} %get-tuple-element.61.refs_4_.refs_0_, bf16[2,256,128]{2,1,0:T(8,128)(2,1)S(1)} %collective-permute-done.21.refs_1_, bf16[2,256,128]{2,1,0:T(8,128)(2,1)S(1)} %collective-permute-done.22.refs_2_, ...), custom_call_target="tpu_custom_call" | custom-call | flops 1000000000 | bytes 3000000 | tf_op jit(solution)/shard_map/kv_unpack/pallas_call | solution.py:56
  (42 shorter events, 0.6 us)
Async XLA Ops:
  0.6 4.1 %copy-start.6 = (s32[2,32]{1,0:T(2,128)S(1)}, s32[2,32]{1,0:T(2,128)}, u32[]{:S(2)}) copy-start(s32[2,32]{1,0:T(2,128)} %refs_2_.7) | copy-start | bytes 772
  0.6 4.1 %copy-start.4 = (bf16[128,1024]{1,0:T(8,128)(2,1)S(1)}, bf16[128,1024]{1,0:T(8,128)(2,1)}, u32[]{:S(2)}) copy-start(bf16[128,1024]{1,0:T(8,128)(2,1)} %refs_0_.7) | copy-start | bytes 786436
  0.7 4.0 %copy-start.5 = (bf16[128,1024]{1,0:T(8,128)(2,1)S(1)}, bf16[128,1024]{1,0:T(8,128)(2,1)}, u32[]{:S(2)}) copy-start(bf16[128,1024]{1,0:T(8,128)(2,1)} %refs_1_.7) | copy-start | bytes 786436
  0.7 4.2 %copy-start.1 = (bf16[128,5120]{1,0:T(8,128)(2,1)S(1)}, bf16[128,5120]{1,0:T(8,128)(2,1)}, u32[]{:S(2)}) copy-start(bf16[128,5120]{1,0:T(8,128)(2,1)} %refs_1_.11) | copy-start | bytes 3932164
  0.7 4.2 %copy-start.2 = (bf16[128,5120]{1,0:T(8,128)(2,1)S(1)}, bf16[128,5120]{1,0:T(8,128)(2,1)}, u32[]{:S(2)}) copy-start(bf16[128,5120]{1,0:T(8,128)(2,1)} %refs_2_.11) | copy-start | bytes 3932164
  2.7 2.1 %copy-start = (bf16[128,5120]{1,0:T(8,128)(2,1)S(1)}, bf16[128,5120]{1,0:T(8,128)(2,1)}, u32[]{:S(2)}) copy-start(bf16[128,5120]{1,0:T(8,128)(2,1)} %refs_0_.11) | copy-start | bytes 3932164
  2.8 2.1 %copy-start.3 = (f32[128,40]{0,1:T(8,128)S(1)}, f32[128,40]{0,1:T(8,128)}, u32[]{:S(2)}) copy-start(f32[128,40]{0,1:T(8,128)} %param.12) | copy-start | bytes 61444
  2.8 1.9 %collective-permute-start = (bf16[4,272,128]{2,1,0:T(8,128)(2,1)}, bf16[4,272,128]{2,1,0:T(8,128)(2,1)S(1)}, u32[]{:S(2)}, u32[]{:S(2)}) collective-permute-start(bf16[4,272,128]{2,1,0:T(8,128)(2,1)} %kv_pack.1), channel_id=1, source_target_pairs={{0,1},{1,0},{2,3},{3,2},{4,5},{5,4},{6,7},{7,6},{8,9},{9,8},{10,11... | collective-permute-start | bytes 835592 | tf_op jit(solution)/shard_map/ppermute | solution.py:359
  5.3 7.6 %collective-permute-start.5 = (bf16[2,1328,128]{2,1,0:T(8,128)(2,1)S(1)}, bf16[2,1328,128]{2,1,0:T(8,128)(2,1)S(1)}, u32[]{:S(2)}, u32[]{:S(2)}) collective-permute-start(bf16[2,1328,128]{2,1,0:T(8,128)(2,1)S(1)} %qg_pack.5), channel_id=1, source_target_pairs={{0,1},{1,0},{2,3},{3,2},{4,5},{5,4},{6,7},{7,6},{8,9},{9,8},{10,11... | collective-permute-start | bytes 2039816 | tf_op jit(solution)/shard_map/ppermute | solution.py:359
  5.7 6.8 %collective-permute-start.4 = (bf16[2,272,128]{2,1,0:T(8,128)(2,1)S(1)}, bf16[2,272,128]{2,1,0:T(8,128)(2,1)S(1)}, u32[]{:S(2)}, u32[]{:S(2)}) collective-permute-start(bf16[2,272,128]{2,1,0:T(8,128)(2,1)S(1)} %get-tuple-element.36.refs_3_), channel_id=1, source_target_pairs={{0,16},{16,0},{1,17},{17,1},{2,18},{18,2},{3,19},{19,3},{4,20},{20... | collective-permute-start | bytes 417800 | tf_op jit(solution)/shard_map/ppermute | solution.py:362
  8.3 5.7 %collective-permute-start.1 = (bf16[2,272,128]{2,1,0:T(8,128)(2,1)S(1)}, bf16[2,272,128]{2,1,0:T(8,128)(2,1)S(1)}, u32[]{:S(2)}, u32[]{:S(2)}) collective-permute-start(bf16[2,272,128]{2,1,0:T(8,128)(2,1)S(1)} %get-tuple-element.37.refs_4_), channel_id=1, source_target_pairs={{0,2},{1,3},{2,0},{3,1},{4,6},{5,7},{6,4},{7,5},{8,10},{9,11},{10,... | collective-permute-start | bytes 417800 | tf_op jit(solution)/shard_map/ppermute | solution.py:359
  9.9 6.6 %collective-permute-start.2 = (bf16[2,272,128]{2,1,0:T(8,128)(2,1)S(1)}, bf16[2,272,128]{2,1,0:T(8,128)(2,1)S(1)}, u32[]{:S(2)}, u32[]{:S(2)}) collective-permute-start(bf16[2,272,128]{2,1,0:T(8,128)(2,1)S(1)} %get-tuple-element.38), channel_id=1, source_target_pairs={{0,4},{1,5},{2,6},{3,7},{4,0},{5,1},{6,2},{7,3},{8,12},{9,13},{10,... | collective-permute-start | bytes 417800 | tf_op jit(solution)/shard_map/ppermute | solution.py:359
  11.4 6.7 %collective-permute-start.3 = (bf16[2,272,128]{2,1,0:T(8,128)(2,1)S(1)}, bf16[2,272,128]{2,1,0:T(8,128)(2,1)S(1)}, u32[]{:S(2)}, u32[]{:S(2)}) collective-permute-start(bf16[2,272,128]{2,1,0:T(8,128)(2,1)S(1)} %get-tuple-element.39), channel_id=1, source_target_pairs={{0,6},{1,7},{2,4},{3,5},{4,2},{5,3},{6,0},{7,1},{8,14},{9,15},{10,... | collective-permute-start | bytes 417800 | tf_op jit(solution)/shard_map/ppermute | solution.py:359
  18.2 19.2 %collective-permute-start.13 = (bf16[2,1328,128]{2,1,0:T(8,128)(2,1)S(1)}, bf16[2,1328,128]{2,1,0:T(8,128)(2,1)S(1)}, u32[]{:S(2)}, u32[]{:S(2)}) collective-permute-start(bf16[2,1328,128]{2,1,0:T(8,128)(2,1)S(1)} %pair_up.2), channel_id=1, source_target_pairs={{0,6},{1,7},{2,4},{3,5},{4,2},{5,3},{6,0},{7,1},{8,14},{9,15},{10,... | collective-permute-start | bytes 2039816 | tf_op jit(solution)/shard_map/ppermute | solution.py:359
  20.8 6.6 %collective-permute-start.7 = (bf16[2,272,128]{2,1,0:T(8,128)(2,1)S(1)}, bf16[2,272,128]{2,1,0:T(8,128)(2,1)S(1)}, u32[]{:S(2)}, u32[]{:S(2)}) collective-permute-start(bf16[2,272,128]{2,1,0:T(8,128)(2,1)S(1)} %collective-permute-done.2.refs_5_.refs_3_), channel_id=1, source_target_pairs={{0,16},{16,0},{1,17},{17,1},{2,18},{18,2},{3,19},{19,3},{4,20},{20... | collective-permute-start | bytes 417800 | tf_op jit(solution)/shard_map/ppermute | solution.py:362
  21.3 8.2 %collective-permute-start.8 = (bf16[2,272,128]{2,1,0:T(8,128)(2,1)S(1)}, bf16[2,272,128]{2,1,0:T(8,128)(2,1)S(1)}, u32[]{:S(2)}, u32[]{:S(2)}) collective-permute-start(bf16[2,272,128]{2,1,0:T(8,128)(2,1)S(1)} %collective-permute-done.3.refs_6_.refs_4_), channel_id=1, source_target_pairs={{0,16},{16,0},{1,17},{17,1},{2,18},{18,2},{3,19},{19,3},{4,20},{20... | collective-permute-start | bytes 417800 | tf_op jit(solution)/shard_map/ppermute | solution.py:362
  22.8 8.2 %collective-permute-start.6 = (bf16[2,272,128]{2,1,0:T(8,128)(2,1)S(1)}, bf16[2,272,128]{2,1,0:T(8,128)(2,1)S(1)}, u32[]{:S(2)}, u32[]{:S(2)}) collective-permute-start(bf16[2,272,128]{2,1,0:T(8,128)(2,1)S(1)} %collective-permute-done.1.refs_4_.refs_2_), channel_id=1, source_target_pairs={{0,16},{16,0},{1,17},{17,1},{2,18},{18,2},{3,19},{19,3},{4,20},{20... | collective-permute-start | bytes 417800 | tf_op jit(solution)/shard_map/ppermute | solution.py:362
  27.8 18.0 %collective-permute-start.11 = (bf16[1,1328,128]{2,1,0:T(8,128)(2,1)S(1)}, bf16[1,1328,128]{2,1,0:T(8,128)(2,1)S(1)}, u32[]{:S(2)}, u32[]{:S(2)}) collective-permute-start(bf16[1,1328,128]{2,1,0:T(8,128)(2,1)S(1)} %get-tuple-element.47), channel_id=1, source_target_pairs={{0,2},{1,3},{2,0},{3,1},{4,6},{5,7},{6,4},{7,5},{8,10},{9,11},{10,... | collective-permute-start | bytes 1019912 | tf_op jit(solution)/shard_map/ppermute | solution.py:359
  28.4 17.5 %collective-permute-start.12 = (bf16[1,1328,128]{2,1,0:T(8,128)(2,1)S(1)}, bf16[1,1328,128]{2,1,0:T(8,128)(2,1)S(1)}, u32[]{:S(2)}, u32[]{:S(2)}) collective-permute-start(bf16[1,1328,128]{2,1,0:T(8,128)(2,1)S(1)} %get-tuple-element.48), channel_id=1, source_target_pairs={{0,4},{1,5},{2,6},{3,7},{4,0},{5,1},{6,2},{7,3},{8,12},{9,13},{10,... | collective-permute-start | bytes 1019912 | tf_op jit(solution)/shard_map/ppermute | solution.py:359
  29.9 21.2 %collective-permute-start.10 = (bf16[1,1328,128]{2,1,0:T(8,128)(2,1)S(1)}, bf16[1,1328,128]{2,1,0:T(8,128)(2,1)S(1)}, u32[]{:S(2)}, u32[]{:S(2)}) collective-permute-start(bf16[1,1328,128]{2,1,0:T(8,128)(2,1)S(1)} %get-tuple-element.43), channel_id=1, source_target_pairs={{0,5},{1,4},{2,7},{3,6},{4,1},{5,0},{6,3},{7,2},{8,13},{9,12},{10,... | collective-permute-start | bytes 1019912 | tf_op jit(solution)/shard_map/ppermute | solution.py:359
  31.0 20.7 %collective-permute-start.9 = (bf16[1,1328,128]{2,1,0:T(8,128)(2,1)S(1)}, bf16[1,1328,128]{2,1,0:T(8,128)(2,1)S(1)}, u32[]{:S(2)}, u32[]{:S(2)}) collective-permute-start(bf16[1,1328,128]{2,1,0:T(8,128)(2,1)S(1)} %get-tuple-element.42), channel_id=1, source_target_pairs={{0,3},{1,2},{2,1},{3,0},{4,7},{5,6},{6,5},{7,4},{8,11},{9,10},{10,... | collective-permute-start | bytes 1019912 | tf_op jit(solution)/shard_map/ppermute | solution.py:359
  45.8 12.1 %collective-permute-start.16 = (bf16[2,640,128]{2,1,0:T(8,128)(2,1)S(1)}, bf16[2,640,128]{2,1,0:T(8,128)(2,1)S(1)}, u32[]{:S(2)}, u32[]{:S(2)}) collective-permute-start(bf16[2,640,128]{2,1,0:T(8,128)(2,1)S(1)} %get-tuple-element.56), channel_id=1, source_target_pairs={{0,6},{1,7},{2,4},{3,5},{4,2},{5,3},{6,0},{7,1},{8,14},{9,15},{10,... | collective-permute-start | bytes 983048 | tf_op jit(solution)/shard_map/ppermute | solution.py:359
  57.9 9.3 %collective-permute-start.18 = (bf16[4,256,128]{2,1,0:T(8,128)(2,1)S(1)}, bf16[4,256,128]{2,1,0:T(8,128)(2,1)S(1)}, u32[]{:S(2)}, u32[]{:S(2)}) collective-permute-start(bf16[4,256,128]{2,1,0:T(8,128)(2,1)S(1)} %pass_on.1), channel_id=1, source_target_pairs={{0,16},{16,0},{1,17},{17,1},{2,18},{18,2},{3,19},{19,3},{4,20},{20... | collective-permute-start | bytes 786440 | tf_op jit(solution)/shard_map/ppermute | solution.py:362
  58.3 13.0 %collective-permute-start.17 = (bf16[4,256,128]{2,1,0:T(8,128)(2,1)S(1)}, bf16[4,256,128]{2,1,0:T(8,128)(2,1)S(1)}, u32[]{:S(2)}, u32[]{:S(2)}) collective-permute-start(bf16[4,256,128]{2,1,0:T(8,128)(2,1)S(1)} %get-tuple-element.58), channel_id=1, source_target_pairs={{0,16},{16,0},{1,17},{17,1},{2,18},{18,2},{3,19},{19,3},{4,20},{20... | collective-permute-start | bytes 786440 | tf_op jit(solution)/shard_map/ppermute | solution.py:362
  60.0 11.4 %collective-permute-start.14 = (bf16[2,640,128]{2,1,0:T(8,128)(2,1)S(1)}, bf16[2,640,128]{2,1,0:T(8,128)(2,1)S(1)}, u32[]{:S(2)}, u32[]{:S(2)}) collective-permute-start(bf16[2,640,128]{2,1,0:T(8,128)(2,1)S(1)} %get-tuple-element.54), channel_id=1, source_target_pairs={{0,2},{1,3},{2,0},{3,1},{4,6},{5,7},{6,4},{7,5},{8,10},{9,11},{10,... | collective-permute-start | bytes 983048 | tf_op jit(solution)/shard_map/ppermute | solution.py:359
  61.5 9.9 %collective-permute-start.15 = (bf16[2,640,128]{2,1,0:T(8,128)(2,1)S(1)}, bf16[2,640,128]{2,1,0:T(8,128)(2,1)S(1)}, u32[]{:S(2)}, u32[]{:S(2)}) collective-permute-start(bf16[2,640,128]{2,1,0:T(8,128)(2,1)S(1)} %get-tuple-element.55), channel_id=1, source_target_pairs={{0,4},{1,5},{2,6},{3,7},{4,0},{5,1},{6,2},{7,3},{8,12},{9,13},{10,... | collective-permute-start | bytes 983048 | tf_op jit(solution)/shard_map/ppermute | solution.py:359
  67.2 4.1 %collective-permute-start.19 = (bf16[4,256,128]{2,1,0:T(8,128)(2,1)S(1)}, bf16[4,256,128]{2,1,0:T(8,128)(2,1)S(1)}, u32[]{:S(2)}, u32[]{:S(2)}) collective-permute-start(bf16[4,256,128]{2,1,0:T(8,128)(2,1)S(1)} %kv_sum.3), channel_id=1, source_target_pairs={{0,1},{1,0},{2,3},{3,2},{4,5},{5,4},{6,7},{7,6},{8,9},{9,8},{10,11... | collective-permute-start | bytes 786440 | tf_op jit(solution)/shard_map/ppermute | solution.py:359
  71.4 3.6 %collective-permute-start.20 = (bf16[4,640,128]{2,1,0:T(8,128)(2,1)S(1)}, bf16[4,640,128]{2,1,0:T(8,128)(2,1)S(1)}, u32[]{:S(2)}, u32[]{:S(2)}) collective-permute-start(bf16[4,640,128]{2,1,0:T(8,128)(2,1)S(1)} %query_relay.1), channel_id=1, source_target_pairs={{0,1},{1,0},{2,3},{3,2},{4,5},{5,4},{6,7},{7,6},{8,9},{9,8},{10,11... | collective-permute-start | bytes 1966088 | tf_op jit(solution)/shard_map/ppermute | solution.py:359
  71.5 5.9 %collective-permute-start.21 = (bf16[2,256,128]{2,1,0:T(8,128)(2,1)S(1)}, bf16[2,256,128]{2,1,0:T(8,128)(2,1)S(1)}, u32[]{:S(2)}, u32[]{:S(2)}) collective-permute-start(bf16[2,256,128]{2,1,0:T(8,128)(2,1)S(1)} %get-tuple-element.63), channel_id=1, source_target_pairs={{0,2},{1,3},{2,0},{3,1},{4,6},{5,7},{6,4},{7,5},{8,10},{9,11},{10,... | collective-permute-start | bytes 393224 | tf_op jit(solution)/shard_map/ppermute | solution.py:359
  72.8 6.3 %collective-permute-start.22 = (bf16[2,256,128]{2,1,0:T(8,128)(2,1)S(1)}, bf16[2,256,128]{2,1,0:T(8,128)(2,1)S(1)}, u32[]{:S(2)}, u32[]{:S(2)}) collective-permute-start(bf16[2,256,128]{2,1,0:T(8,128)(2,1)S(1)} %get-tuple-element.64), channel_id=1, source_target_pairs={{0,4},{1,5},{2,6},{3,7},{4,0},{5,1},{6,2},{7,3},{8,12},{9,13},{10,... | collective-permute-start | bytes 393224 | tf_op jit(solution)/shard_map/ppermute | solution.py:359
  74.3 7.1 %collective-permute-start.23 = (bf16[2,256,128]{2,1,0:T(8,128)(2,1)S(1)}, bf16[2,256,128]{2,1,0:T(8,128)(2,1)S(1)}, u32[]{:S(2)}, u32[]{:S(2)}) collective-permute-start(bf16[2,256,128]{2,1,0:T(8,128)(2,1)S(1)} %get-tuple-element.65), channel_id=1, source_target_pairs={{0,6},{1,7},{2,4},{3,5},{4,2},{5,3},{6,0},{7,1},{8,14},{9,15},{10,... | collective-permute-start | bytes 393224 | tf_op jit(solution)/shard_map/ppermute | solution.py:359
